TPU v7x, 32 devices: a whole 2x2x4 slice. The times are simulated.
32 devices in a mesh: date: 4 (over y, x), space: 8 (over z, core).
Axes of the slice: x: 2, y: 2, z: 4, core: 2. Of those that a mesh axis runs over, the one named last changes fastest.
Arguments:
- acquisitions: bfloat16 [2, 128, 192, 576], P(None, 'date', 'space'), may hold values from -6 to 6
- valid_dates: int32 [128, 192, 576], P('date', 'space'), may hold values 0 or 1
Outputs:
- linked: float32 [2, 128, 32, 192], P(None, 'date', 'space')
All inputs are finite; a program needn't handle non-finite values. No bound on the sum of `valid_dates` on one device may be relied on, other than what follows from the above.
Results may differ from a plain program's by a relative error of at most 0.0028.
Values may be sent and summed in bfloat16 or wider, within the bound.
No kernel may reach another device: no remote copies, remote signals or barrier semaphores. Data moves between devices by JAX's collectives and lax.ppermute only.
A program may use at most 256 MiB of HBM per device.

v0:
```python
import jax
import jax.numpy as jnp
from jax import lax
from jax.sharding import PartitionSpec as P

BOX_ROWS = 15
BOX_COLS = 7
STEP_ROWS = 3
STEP_COLS = 6
ITERS = 4
MARGIN = 6
NBOX = 105


POWER_EPS = 1e-05


def padded(block, sides, width):
    for axis, dim in sides:
        count = lax.axis_size(axis)
        forward = [(i, i + 1) for i in range(count - 1)]
        backward = [(target, source) for source, target in forward]
        low = lax.ppermute(
            lax.slice_in_dim(block, block.shape[dim] - width, None, axis=dim), axis, forward
        )
        high = lax.ppermute(lax.slice_in_dim(block, 0, width, axis=dim), axis, backward)
        block = jnp.concatenate([low, block, high], axis=dim)
    return block


def regroup(outgoing):
    return lax.all_to_all(outgoing, ("date", "space"), split_axis=0, concat_axis=0, tiled=True)


def link_all(framed, all_dates, out_cols, row_groups):
    span = STEP_COLS * (out_cols - 1) + 1

    def link_row(out_row):
        band_rows = lax.dynamic_slice_in_dim(framed, out_row * STEP_ROWS, BOX_ROWS, 2)
        window = jnp.stack(
            [band_rows[..., k : k + span : STEP_COLS] for k in range(BOX_COLS)], axis=3
        )
        real_sum = jnp.einsum(
            "adrkc,aerkc->cde", window, window, preferred_element_type=jnp.float32
        )
        cross_sum = jnp.einsum(
            "drkc,erkc->cde", window[1], window[0], preferred_element_type=jnp.float32
        )
        energy = jnp.diagonal(real_sum, axis1=1, axis2=2) / NBOX + POWER_EPS
        factor = lax.rsqrt(energy)
        weights = factor[:, :, None] * factor[:, None, :] / NBOX
        coh_real = (real_sum * weights).astype(jnp.bfloat16)
        coh_imag = ((cross_sum - jnp.swapaxes(cross_sum, 1, 2)) * weights).astype(jnp.bfloat16)
        vec_real = jnp.ones((out_cols, all_dates), jnp.bfloat16)
        vec_imag = jnp.zeros((out_cols, all_dates), jnp.bfloat16)
        real_out = jnp.zeros((out_cols, all_dates), jnp.float32)
        imag_out = jnp.zeros((out_cols, all_dates), jnp.float32)
        for sweep in range(ITERS):
            real_out = jnp.einsum(
                "cde,ce->cd", coh_real, vec_real, preferred_element_type=jnp.float32
            ) - jnp.einsum("cde,ce->cd", coh_imag, vec_imag, preferred_element_type=jnp.float32)
            imag_out = jnp.einsum(
                "cde,ce->cd", coh_imag, vec_real, preferred_element_type=jnp.float32
            ) + jnp.einsum("cde,ce->cd", coh_real, vec_imag, preferred_element_type=jnp.float32)
            total = (
                jnp.sum(real_out * real_out + imag_out * imag_out, axis=1) / all_dates + POWER_EPS
            )
            norm_factor = lax.rsqrt(total)[:, None]
            real_out = real_out * norm_factor
            imag_out = imag_out * norm_factor
            vec_real = real_out.astype(jnp.bfloat16)
            vec_imag = imag_out.astype(jnp.bfloat16)
        return jnp.stack([real_out, imag_out])

    return lax.map(link_row, jnp.arange(row_groups, dtype=jnp.int32))


def on_device(acquisitions, valid_dates):
    date_count = lax.axis_size("date")
    space_count = lax.axis_size("space")
    tile_count = date_count * space_count
    masked = acquisitions * valid_dates.astype(jnp.bfloat16)[None]
    local_dates = masked.shape[1]
    local_cols = masked.shape[2]
    strip_rows = masked.shape[3]
    all_dates = date_count * local_dates
    left_pad = STEP_COLS // 2
    tile_rows = strip_rows // tile_count
    middle = masked.reshape(2, local_dates, local_cols, tile_count, tile_rows)
    outgoing = jnp.transpose(middle, (3, 0, 1, 4, 2))
    incoming = regroup(outgoing)
    height = incoming.shape[3]
    stacked = incoming.reshape(date_count, space_count, 2, local_dates, height, local_cols)
    stacked = jnp.transpose(stacked, (2, 0, 3, 4, 1, 5)).reshape(
        2, all_dates, height, space_count * local_cols
    )
    extended = padded(stacked, ((("date", "space"), 2),), MARGIN)
    total_cols = space_count * local_cols
    framed = jnp.pad(extended, ((0, 0), (0, 0), (0, 0), (left_pad, BOX_COLS - STEP_COLS)))
    out_cols = total_cols // STEP_COLS
    row_groups = tile_rows // STEP_ROWS
    rows_out = link_all(framed, all_dates, out_cols, row_groups)
    col_share = out_cols // space_count
    sending = rows_out.reshape(row_groups, 2, space_count, col_share, date_count, local_dates)
    sending = jnp.transpose(sending, (4, 2, 1, 5, 0, 3)).reshape(
        tile_count, 2, local_dates, row_groups, col_share
    )
    returned = lax.all_to_all(sending, ("date", "space"), split_axis=0, concat_axis=0, tiled=True)
    linked = jnp.transpose(returned, (1, 2, 4, 0, 3)).reshape(
        2, local_dates, col_share, tile_count * row_groups
    )
    return linked


def solution(mesh):
    in_specs = (P(None, "date", "space", None), P("date", "space", None))
    out_specs = P(None, "date", "space", None)
    return jax.shard_map(
        on_device, mesh=mesh, in_specs=in_specs, out_specs=out_specs, check_vma=False
    )
```

profile of v0, /device:TPU:16, one launch (start us, length us, event | category | flops | bytes accessed | tf_op | source)
XLA Modules:
  0.0 428.9 jit_solution(10081535708639122308)
XLA Ops:
  0.0 8.3 %copy.60 = bf16[2,32,24,576]{1,2,3,0:T(8,128)(2,1)} copy(bf16[2,32,24,576]{3,2,1,0:T(8,128)(2,1)} %param.4) | data formatting | bytes 3538944 | tf_op args[0]
  9.4 4.2 copy.59
  13.6 6.6 %broadcast_multiply_fusion = bf16[2,32,24,576]{1,2,3,0:T(8,128)(2,1)} fusion(bf16[2,32,24,576]{1,2,3,0:T(8,128)(2,1)} %copy.60, bf16[32,24,576]{0,1,2:T(8,128)(2,1)S(1)} %copy.59), kind=kLoop, calls=%fused_computation.93 | loop fusion | flops 884736 | bytes 4423680 | tf_op jit(solution)/shard_map/mul | solution.py:82
  20.2 7.2 %copy.147 = bf16[32,2,32,18,24]{2,4,3,1,0:T(8,128)(2,1)} copy(bf16[32,2,32,18,24]{2,4,3,0,1:T(8,128)(2,1)} %bitcast.265) | data formatting | bytes 3538944 | tf_op jit(solution)/shard_map/transpose | solution.py:90
  27.4 8.0 %reshape.89 = bf16[32,2,13824]{2,1,0:T(2,128)(2,1)S(1)} reshape(bf16[32,2,18,24,32]{4,3,2,1,0:T(8,128)(2,1)} %bitcast.266) | data formatting | bytes 3538944
  35.4 45.3 %all_to_all.10 = bf16[32,2,13824]{2,1,0:T(2,128)(2,1)S(1)} all-to-all(bf16[32,2,13824]{2,1,0:T(2,128)(2,1)S(1)} %reshape.89), channel_id=1, replica_groups=mesh['date'=4,'space'=8] {'date','space'}, dimensions={0} | all-to-all | bytes 3538944 | tf_op jit(solution)/shard_map/all_to_all | solution.py:32
  80.7 6.1 %reshape.90 = bf16[32,2,18,24,32]{4,3,2,1,0:T(8,128)(2,1)} reshape(bf16[32,2,13824]{2,1,0:T(2,128)(2,1)S(1)} %all_to_all.10) | data formatting | bytes 3538944
  86.7 15.1 %copy.62 = bf16[2,4,32,18,8,24]{2,1,5,4,3,0:T(4,128)(2,1)} copy(bf16[2,4,32,18,8,24]{2,5,3,0,4,1:T(8,128)(2,1)} %bitcast.267) | data formatting | bytes 3538944 | tf_op jit(solution)/shard_map/transpose | solution.py:94
  101.8 8.3 %reshape.53 = bf16[2,128,18,192]{1,3,2,0:T(8,128)(2,1)S(1)} reshape(bf16[2,4,32,18,8,24]{2,1,5,4,3,0:T(4,128)(2,1)} %copy.62) | data formatting | bytes 3538944 | tf_op jit(solution)/shard_map/reshape | solution.py:94
  111.0 2.1 collective-permute-start
  113.1 3.7 collective-permute-start.1
  116.8 5.6 %collective-permute-done = bf16[2,128,6,192]{1,3,2,0:T(8,128)(2,1)S(1)} collective-permute-done((bf16[2,128,6,192]{1,3,2,0:T(8,128)(2,1)}, bf16[2,128,6,192]{1,3,2,0:T(8,128)(2,1)S(1)}, u32[]{:S(2)}, u32[]{:S(2)}) %collective-permute-start) | collective-permute-done | bytes 589856 | tf_op jit(solution)/shard_map/ppermute | solution.py:23
  122.4 7.6 %collective-permute-done.1 = bf16[2,128,6,192]{1,3,2,0:T(8,128)(2,1)S(1)} collective-permute-done((bf16[2,128,6,192]{1,3,2,0:T(8,128)(2,1)S(1)}, bf16[2,128,6,192]{1,3,2,0:T(8,128)(2,1)S(1)}, u32[]{:S(2)}, u32[]{:S(2)}) %collective-permute-start.1) | collective-permute-done | bytes 589856 | tf_op jit(solution)/shard_map/ppermute | solution.py:26
  130.0 2.3 fusion.57
  132.3 279.1 %while.10 = (s32[]{:T(128)}, f32[6,2,32,128]{3,2,1,0:T(8,128)S(1)}, s32[6]{0:T(128)S(1)}, bf16[2,128,30,196]{1,3,2,0:T(8,128)(2,1)}, s32[]{:T(128)}, /*index=5*/s32[1]{0:T(128)}, s32[]{:T(128)}, s32[]{:T(128)}) while((s32[]{:T(128)}, f32[6,2,32,128]{3,2,1,0:T(8,128)S(1)}, s32[6]{0:T(128)S(1)}, bf16[2,128,30,196]{1,3,2,0:T(8,128)(2,1)}, ...), condition=%wide.region_5.6_spmd, body=%wide.region_0.5_spmd.sunk | while | flops 350921344 | bytes 52346516 | solution.py:75
  133.5 1.5 constant_dynamic-slice_fusion.2
  146.2 2.1 slice.64
  149.2 2.9 convolution_bitcast_fusion.5
  152.1 4.7 %copy.190 = f32[32,128,128]{0,2,1:T(8,128)} copy(f32[32,128,128]{2,1,0:T(8,128)S(1)} %convolution_bitcast_fusion.5) | data formatting | bytes 4194304 | tf_op jit(solution)/shard_map/while/body/eval_jaxpr/adrkc,aerkc->cde/dot_general | solution.py:43
  156.8 1.8 gather_fusion
  158.6 3.3 convolution_bitcast_fusion.4
  162.0 2.9 copy.189
  164.9 2.6 fusion.180
  180.1 1.5 constant_dynamic-slice_fusion.2
  192.7 2.1 slice.64
  195.7 2.9 convolution_bitcast_fusion.5
  198.6 4.7 %copy.190 = f32[32,128,128]{0,2,1:T(8,128)} copy(f32[32,128,128]{2,1,0:T(8,128)S(1)} %convolution_bitcast_fusion.5) | data formatting | bytes 4194304 | tf_op jit(solution)/shard_map/while/body/eval_jaxpr/adrkc,aerkc->cde/dot_general | solution.py:43
  203.3 1.8 gather_fusion
  205.1 3.3 convolution_bitcast_fusion.4
  208.5 2.9 copy.189
  211.4 2.6 fusion.180
  226.6 1.5 constant_dynamic-slice_fusion.2
  239.2 2.1 slice.64
  242.3 2.9 convolution_bitcast_fusion.5
  245.1 4.7 %copy.190 = f32[32,128,128]{0,2,1:T(8,128)} copy(f32[32,128,128]{2,1,0:T(8,128)S(1)} %convolution_bitcast_fusion.5) | data formatting | bytes 4194304 | tf_op jit(solution)/shard_map/while/body/eval_jaxpr/adrkc,aerkc->cde/dot_general | solution.py:43
  249.8 1.8 gather_fusion
  251.7 3.3 convolution_bitcast_fusion.4
  255.0 2.9 copy.189
  257.9 2.6 fusion.180
  273.1 1.5 constant_dynamic-slice_fusion.2
  285.7 2.1 slice.64
  288.8 2.9 convolution_bitcast_fusion.5
  291.6 4.7 %copy.190 = f32[32,128,128]{0,2,1:T(8,128)} copy(f32[32,128,128]{2,1,0:T(8,128)S(1)} %convolution_bitcast_fusion.5) | data formatting | bytes 4194304 | tf_op jit(solution)/shard_map/while/body/eval_jaxpr/adrkc,aerkc->cde/dot_general | solution.py:43
  296.3 1.8 gather_fusion
  298.2 3.3 convolution_bitcast_fusion.4
  301.5 2.9 copy.189
  304.4 2.6 fusion.180
  319.6 1.5 constant_dynamic-slice_fusion.2
  332.2 2.1 slice.64
  335.3 2.9 convolution_bitcast_fusion.5
  338.2 4.7 %copy.190 = f32[32,128,128]{0,2,1:T(8,128)} copy(f32[32,128,128]{2,1,0:T(8,128)S(1)} %convolution_bitcast_fusion.5) | data formatting | bytes 4194304 | tf_op jit(solution)/shard_map/while/body/eval_jaxpr/adrkc,aerkc->cde/dot_general | solution.py:43
  342.8 1.8 gather_fusion
  344.7 3.3 convolution_bitcast_fusion.4
  348.0 2.9 copy.189
  350.9 2.6 fusion.180
  366.1 1.5 constant_dynamic-slice_fusion.2
  378.8 2.1 slice.64
  381.8 2.9 convolution_bitcast_fusion.5
  384.7 4.7 %copy.190 = f32[32,128,128]{0,2,1:T(8,128)} copy(f32[32,128,128]{2,1,0:T(8,128)S(1)} %convolution_bitcast_fusion.5) | data formatting | bytes 4194304 | tf_op jit(solution)/shard_map/while/body/eval_jaxpr/adrkc,aerkc->cde/dot_general | solution.py:43
  389.4 1.8 gather_fusion
  391.2 3.3 convolution_bitcast_fusion.4
  394.5 2.9 copy.189
  397.4 2.6 fusion.180
  412.5 13.3 %all_to_all.11 = f32[32,1,1536]{2,1,0:T(1,128)S(1)} all-to-all(f32[32,1,1536]{2,1,0:T(1,128)S(1)} %reshape.91), channel_id=1, replica_groups=mesh['date'=4,'space'=8] {'date','space'}, dimensions={0} | all-to-all | bytes 393216 | tf_op jit(solution)/shard_map/all_to_all | solution.py:108
  (293 shorter events, 149.8 us)
Async XLA Ops:
  0.0 8.3 %copy-start = (s32[32,24,576]{2,1,0:T(8,128)S(1)}, s32[32,24,576]{2,1,0:T(8,128)}, u32[]{:S(2)}) copy-start(s32[32,24,576]{2,1,0:T(8,128)} %param.5) | copy-start | bytes 5308420
  111.0 11.4 %collective-permute-start = (bf16[2,128,6,192]{1,3,2,0:T(8,128)(2,1)}, bf16[2,128,6,192]{1,3,2,0:T(8,128)(2,1)S(1)}, u32[]{:S(2)}, u32[]{:S(2)}) collective-permute-start(bf16[2,128,6,192]{1,3,2,0:T(8,128)(2,1)} %get-tuple-element.70), channel_id=1, source_target_pairs={{0,1},{1,2},{2,3},{3,4},{4,5},{5,6},{6,7},{7,8},{8,9},{9,10},{10,1... | collective-permute-start | bytes 1769480 | tf_op jit(solution)/shard_map/ppermute | solution.py:23
  113.1 16.8 %collective-permute-start.1 = (bf16[2,128,6,192]{1,3,2,0:T(8,128)(2,1)S(1)}, bf16[2,128,6,192]{1,3,2,0:T(8,128)(2,1)S(1)}, u32[]{:S(2)}, u32[]{:S(2)}) collective-permute-start(bf16[2,128,6,192]{1,3,2,0:T(8,128)(2,1)S(1)} %get-tuple-element.71), channel_id=1, source_target_pairs={{1,0},{2,1},{3,2},{4,3},{5,4},{6,5},{7,6},{8,7},{9,8},{10,9},{11,1... | collective-permute-start | bytes 1769480 | tf_op jit(solution)/shard_map/ppermute | solution.py:26
  130.0 2.3 copy-start.1
where the time goes:
time: 434 us; the launch traced here: 429 us
  local copies, waits for them, and re-layouts  215 us (50%)
  matrix products  99.8 us (23%)
  blocking collectives  58.6 us (14%)
  other arithmetic  32.1 us (7%)
  waiting for transfers between devices  13.2 us (3%)
  starting transfers between devices  5.77 us (1%)
  loops' own time  4.72 us (1%)
    slice x42, local copies, waits for them, and re-layouts, link_row(): band_rows[..., k:k + span:STEP_COLS]  49.4 us
    all_to_all x1, blocking collectives, regroup(): lax.all_to_all(outgoing, ('date', 'space'), split_axis=0, concat_axis=0,...  45.3 us
    while x36, local copies, waits for them, and re-layouts  30 us
    dot_general x6, local copies, waits for them, and re-layouts, link_row(): jnp.einsum('adrkc,aerkc->cde', window, window, preferred_element_type=jnp...  28.1 us
    unnamed x9, local copies, waits for them, and re-layouts  23.3 us
    dot_general x6, matrix products, link_row(): jnp.einsum('drkc,erkc->cde', window[1], window[0], preferred_element_type...  20 us
    dot_general x6, local copies, waits for them, and re-layouts, link_row(): jnp.einsum('drkc,erkc->cde', window[1], window[0], preferred_element_type...  17.4 us
    dot_general x6, matrix products, link_row(): jnp.einsum('adrkc,aerkc->cde', window, window, preferred_element_type=jnp...  17.2 us
  transfers between devices with their start and end apart: 2, of which 2 were waited for; matrix products, arithmetic and copies ran while one was open for 0% of the time, Pallas kernels for 0%

commit v1 on v0

v1 whole, which is shorter than its diff:
```python
import functools
import math

import jax
import jax.numpy as jnp
from jax import lax
from jax.experimental import pallas as pl
from jax.experimental.pallas import tpu as pltpu
from jax.sharding import PartitionSpec as P

BOX_ROWS = 15
BOX_COLS = 7
STEP_ROWS = 3
STEP_COLS = 6
ITERS = 4
MARGIN = 6
NBOX = 105
POWER_EPS = 1e-05

LANES = 128
TILE_ROWS = 18
SLOTS = TILE_ROWS // STEP_ROWS
LEAD = MARGIN // STEP_ROWS
LEFT = STEP_COLS // 2
BATCH = 24
CONTRACT_LAST = (((1,), (1,)), ((), ()))


def lane_mask(shape, first, count):
    lane = lax.broadcasted_iota(jnp.int32, shape, len(shape) - 1)
    inside = ((lane - first) & (LANES - 1)) < count
    return jnp.where(inside, 1.0, 0.0).astype(jnp.bfloat16)


def pack_kernel(tiles, col_groups, segments, axis, acq_ref, valid_ref, halo_ref, *refs):
    outs, planes = refs[:-1], refs[-1]
    parts, dates, cols, rows = acq_ref.shape
    blocks = planes.shape[1]
    stride = planes.shape[2] // dates
    me = lax.axis_index(axis)
    for part in range(parts):
        for block in range(blocks):
            width = min(LANES, rows - block * LANES)
            span = slice(block * LANES, block * LANES + width)
            if width < LANES:
                planes[part, block] = jnp.zeros(planes.shape[2:], jnp.float32)
            for date in range(dates):
                value = acq_ref[part, date, :, span].astype(jnp.float32) * valid_ref[
                    date, :, span
                ].astype(jnp.float32)
                planes[part, block, date * stride : date * stride + cols, :width] = value
                planes[
                    part, block, date * stride + cols : date * stride + cols + LEFT, :width
                ] = halo_ref[part, date, :, span].astype(jnp.float32)
    for offset, out in enumerate(outs):
        target = me ^ offset
        group = lax.rem(target, col_groups)
        segment = target // col_groups

        def source(part, block, j):
            column = group * STEP_COLS - LEFT + j
            column = jnp.where(column < 0, column + cols + LEFT, column)
            plane = planes[part, block, pl.ds(column, dates, stride=stride), :]
            if j:
                plane = pltpu.roll(plane, TILE_ROWS * j, 1)
            return plane.astype(jnp.bfloat16)

        if segments == 1:
            held = {}
            for part in range(parts):
                for tile in range(tiles):
                    total = None
                    first_row = tile * TILE_ROWS
                    for j in range(BOX_COLS):
                        row = first_row
                        while row < first_row + TILE_ROWS:
                            block = row // LANES
                            stop = min(first_row + TILE_ROWS, (block + 1) * LANES)
                            if (part, block, j) not in held:
                                held[part, block, j] = source(part, block, j)
                            mask = lane_mask((16, LANES), (row + TILE_ROWS * j) % LANES, stop - row)
                            piece = held[part, block, j].reshape(-1, 16, LANES) * mask[None]
                            total = piece if total is None else total + piece
                            row = stop
                    out[tile, part] = total.reshape(dates, LANES)
        else:

            def one(index, carry):
                tile = segment * tiles + index - 1
                first_row = jnp.clip(tile, 0, segments * tiles - 1) * TILE_ROWS
                kept = jnp.where((tile >= 0) & (tile < segments * tiles), 1.0, 0.0)
                low = first_row // LANES
                high = (first_row + TILE_ROWS - 1) // LANES
                split = jnp.minimum(high * LANES - first_row, TILE_ROWS)
                split = jnp.where(high == low, TILE_ROWS, split)
                for part in range(parts):
                    total = jnp.zeros((dates // 16, 16, LANES), jnp.bfloat16)
                    for j in range(BOX_COLS):
                        start = first_row + TILE_ROWS * j
                        for block, first, count in (
                            (low, start, split),
                            (high, start + split, TILE_ROWS - split),
                        ):
                            mask = lane_mask((16, LANES), first & (LANES - 1), count)
                            piece = source(part, block, j).reshape(-1, 16, LANES)
                            total = total + piece * mask[None]
                    total = total * kept.astype(jnp.bfloat16)
                    out[index, part] = total.reshape(dates, LANES)
                return carry

            lax.fori_loop(0, tiles + 2, one, 0)


def pack(acquisitions, valid_dates, halo, axis, peers, tiles, col_groups, segments):
    parts, dates, cols, rows = acquisitions.shape
    sent = tiles if segments == 1 else tiles + 2
    shape = jax.ShapeDtypeStruct((sent, parts, dates, LANES), jnp.bfloat16)
    whole = pl.BlockSpec(memory_space=pltpu.VMEM)
    return pl.pallas_call(
        functools.partial(pack_kernel, tiles, col_groups, segments, axis),
        out_shape=[shape] * peers,
        in_specs=[whole] * 3,
        out_specs=[whole] * peers,
        scratch_shapes=[
            pltpu.VMEM((parts, -(-rows // LANES), dates * 32, LANES), jnp.float32),
        ],
        compiler_params=pltpu.CompilerParams(vmem_limit_bytes=56 << 20),
        name="pack",
    )(acquisitions, valid_dates, halo)


def slot_rows(first):
    lane = lax.broadcasted_iota(jnp.int32, (16, LANES), 1)
    place = (lane - first) & (LANES - 1)
    column = (place * 57) >> 10
    return place - TILE_ROWS * column, column < BOX_COLS


def as_mask(inside):
    return jnp.where(inside, 1.0, 0.0).astype(jnp.bfloat16)[None]


def window_pair(real, imag, k, e, row_now, row_next):
    shape = (-1, 16, LANES)
    if e == 0:
        now = as_mask((row_now >= 0) & (row_now < BOX_ROWS))
    else:
        now = as_mask(row_now >= STEP_ROWS * e)
    a = real[k].reshape(shape) * now
    b = imag[k].reshape(shape) * now
    rest = STEP_ROWS * e + BOX_ROWS - TILE_ROWS
    if rest > 0:
        after = as_mask(row_next < rest)
        a = a + real[k + 1].reshape(shape) * after
        b = b + imag[k + 1].reshape(shape) * after
    return a.reshape(real.shape[1:]), b.reshape(real.shape[1:])


def coherence(a, b, diagonal, held, place):
    count = a.shape[0]
    right = jnp.concatenate([a, b], axis=1)
    left = jnp.concatenate([right, jnp.concatenate([b, -a], axis=1)], axis=0)
    sums = lax.dot_general(left, right, CONTRACT_LAST, preferred_element_type=jnp.float32)
    real, imag = sums[:count], sums[count:]
    energy = jnp.sum(jnp.where(diagonal, real, 0.0), axis=0, keepdims=True) * (1 / NBOX)
    factor = lax.rsqrt(energy + POWER_EPS)
    down = jnp.sum(jnp.where(diagonal, factor, 0.0), axis=1, keepdims=True)
    weights = down * (factor * (1 / NBOX))
    held[place, :count] = (real * weights).astype(jnp.bfloat16)
    held[place, count:] = (imag * weights).astype(jnp.bfloat16)


def iterate(held, pixels, dates):
    row = lax.broadcasted_iota(jnp.int32, (8, dates), 0)
    odd = (row & 1) == 1
    sign = jnp.where((row & 2) == 2, -1.0, 1.0)
    start = jnp.concatenate([jnp.where(odd, 0.0, sign), jnp.where(odd, -sign, 0.0)], axis=1)
    vectors = [start.astype(jnp.bfloat16)] * pixels
    for sweep in range(ITERS):
        scaled = []
        for place in range(pixels):
            product = jnp.dot(vectors[place], held[place], preferred_element_type=jnp.float32)
            square = product * product
            square = square + pltpu.roll(square, 1, 0)
            total = jnp.sum(square, axis=1, keepdims=True) * (1 / dates) + POWER_EPS
            scaled.append(product * lax.rsqrt(total))
        if sweep + 1 < ITERS:
            vectors = [
                jnp.concatenate([v, pltpu.roll(v, 7, 0)], axis=1).astype(jnp.bfloat16)
                for v in scaled
            ]
    return scaled


def link_kernel(peers, padded, *refs):
    sources, outs = refs[:peers], refs[peers : 2 * peers]
    real, imag, held, linked = refs[2 * peers :]
    sent, _, dates, _ = sources[0].shape
    all_dates = peers * dates
    base = 0 if padded else 1
    for peer, source in enumerate(sources):
        span = slice(peer * dates, (peer + 1) * dates)
        real[base : base + sent, span] = source[:, 0]
        imag[base : base + sent, span] = source[:, 1]
    if not padded:
        zero = jnp.zeros((all_dates, LANES), jnp.bfloat16)
        for tiles in (real, imag):
            tiles[0] = zero
            tiles[sent + 1] = zero
    pixels = linked.shape[0] // 8
    batch = math.gcd(BATCH, pixels)
    diagonal = lax.broadcasted_iota(
        jnp.int32, (all_dates, all_dates), 0
    ) == lax.broadcasted_iota(jnp.int32, (all_dates, all_dates), 1)

    def step(index, carry):
        rows_of = {}

        def rows_at(k):
            if k not in rows_of:
                first = (index * (batch // SLOTS) + k - 1) * TILE_ROWS
                if padded:
                    segment = lax.axis_index("date") // padded
                    first = first + segment * (sent - 2) * TILE_ROWS
                row, used = slot_rows(first)
                rows_of[k] = jnp.where(used, row, -1), jnp.where(used, row, LANES)
            return rows_of[k]

        for place in range(batch):
            k, e = divmod(place + SLOTS - LEAD, SLOTS)
            a, b = window_pair(
                real, imag, index * (batch // SLOTS) + k, e, rows_at(k)[0], rows_at(k + 1)[1]
            )
            coherence(a, b, diagonal, held, place)
        for place, tile in enumerate(iterate(held, batch, all_dates)):
            linked[pl.ds((index * batch + place) * 8, 8)] = tile
        return carry

    lax.fori_loop(0, pixels // batch, step, 0)
    for part in range(2):
        vectors = linked[pl.ds(part, pixels, stride=8), :]
        flat = jnp.transpose(vectors)
        for peer, out in enumerate(outs):
            out[part] = flat[peer * dates : (peer + 1) * dates]


def link(sources, pixels, padded):
    peers = len(sources)
    sent, parts, dates, _ = sources[0].shape
    all_dates = peers * dates
    kept = sent if padded else sent + 2
    shape = jax.ShapeDtypeStruct((parts, dates, pixels), jnp.float32)
    whole = pl.BlockSpec(memory_space=pltpu.VMEM)
    return pl.pallas_call(
        functools.partial(link_kernel, peers, padded),
        out_shape=[shape] * peers,
        in_specs=[whole] * peers,
        out_specs=[whole] * peers,
        scratch_shapes=[
            pltpu.VMEM((kept, all_dates, LANES), jnp.bfloat16),
            pltpu.VMEM((kept, all_dates, LANES), jnp.bfloat16),
            pltpu.VMEM((math.gcd(BATCH, pixels), 2 * all_dates, all_dates), jnp.bfloat16),
            pltpu.VMEM((pixels * 8, all_dates), jnp.float32),
        ],
        compiler_params=pltpu.CompilerParams(vmem_limit_bytes=56 << 20),
        name="link",
    )(*sources)


def swap(blocks, axis):
    count = len(blocks)
    return [blocks[0]] + [
        lax.ppermute(blocks[m], axis, [(i, i ^ m) for i in range(count)]) for m in range(1, count)
    ]


def on_device(acquisitions, valid_dates):
    peers = lax.axis_size("date")
    strips = lax.axis_size("space")
    parts, dates, cols, rows = acquisitions.shape
    out_cols = cols // STEP_COLS
    segments = peers // out_cols
    tiles = rows // TILE_ROWS // segments
    pixels = rows // STEP_ROWS // segments
    edge = acquisitions[:, :, cols - LEFT :] * valid_dates[:, cols - LEFT :].astype(jnp.bfloat16)
    halo = lax.ppermute(edge, "space", [(i, i + 1) for i in range(strips - 1)])
    outgoing = pack(acquisitions, valid_dates, halo, "date", peers, tiles, out_cols, segments)
    incoming = swap(outgoing, "date")
    outgoing = link(incoming, pixels, 0 if segments == 1 else out_cols)
    incoming = swap(outgoing, "date")
    me = lax.axis_index("date")
    columns = []
    for target in range(peers):
        block = incoming[target]
        for other in range(1, peers):
            block = jnp.where(me == other, incoming[target ^ other], block)
        columns.append(block)
    strips_out = [
        jnp.concatenate(columns[c::out_cols], axis=2) if segments > 1 else columns[c]
        for c in range(out_cols)
    ]
    return jnp.stack(strips_out, axis=2)


def solution(mesh):
    in_specs = (P(None, "date", "space", None), P("date", "space", None))
    out_specs = P(None, "date", "space", None)
    return jax.shard_map(
        on_device, mesh=mesh, in_specs=in_specs, out_specs=out_specs, check_vma=False
    )
```

time: 434 us -> 74.7 us (0.17); the launches traced: 429 us -> 74.4 us
  local copies, waits for them, and re-layouts: 215 us -> 2.6 us
  matrix products: 99.8 us -> 0 us
  blocking collectives: 58.6 us -> 0 us
  other arithmetic: 32.1 us -> 3.43 us
  Pallas kernels: 0 us -> 27.3 us
  waiting for transfers between devices: 13.2 us -> 32.1 us
  loops' own time: 4.72 us -> 0 us
    dot_general x108 -> x0, matrix products: 99.8 us -> none  [the longest x6 20 us: link_row(): jnp.einsum('drkc,erkc->cde', window[1], window[0], preferred_element_type...]
    all_to_all x2 -> x0, blocking collectives: 58.6 us -> none  [the longest x1 45.3 us: regroup(): lax.all_to_all(outgoing, ('date', 'space'), split_axis=0, concat_axis=0,...]
    slice x43 -> x0, local copies, waits for them, and re-layouts: 50.3 us -> none  [the longest x42 49.4 us: link_row(): band_rows[..., k:k + span:STEP_COLS]]
    dot_general x12 -> x0, local copies, waits for them, and re-layouts: 45.4 us -> none  [the longest x6 28.1 us: link_row(): jnp.einsum('adrkc,aerkc->cde', window, window, preferred_element_type=jnp...]
    while x36 -> x0, local copies, waits for them, and re-layouts: 30 us -> none
    pallas_call x0 -> x2, Pallas kernels: none -> 27.3 us  [the longest x1 18.5 us: link(): pl.pallas_call(functools.partial(link_kernel, peers, padded), out_shape=[...]
    transpose x4 -> x0, local copies, waits for them, and re-layouts: 22.3 us -> none  [the longest x1 15.1 us: on_device(): jnp.transpose(stacked, (2, 0, 3, 4, 1, 5))]
    unnamed x9 -> x8, local copies, waits for them, and re-layouts: 23.3 us -> 1.72 us
  transfers between devices with their start and end apart: 2 -> 7, of which waited for: 2 -> 6; matrix products, arithmetic and copies ran while one was open for 0% -> 0% of each run, Pallas kernels for 0% -> 0%
where the time goes in v1:
time: 74.7 us; the launch traced here: 74.4 us
  waiting for transfers between devices  32.1 us (43%)
  Pallas kernels  27.3 us (37%)
  starting transfers between devices  8.9 us (12%)
  other arithmetic  3.43 us (5%)
  local copies, waits for them, and re-layouts  2.6 us (3%)
    ppermute x6, waiting for transfers between devices, swap(): lax.ppermute(blocks[m], axis, [(i, i ^ m) for i in range(count)])  25.7 us
    pallas_call x1, Pallas kernels, link(): pl.pallas_call(functools.partial(link_kernel, peers, padded), out_shape=[...  18.5 us
    pallas_call x1, Pallas kernels, pack(): pl.pallas_call(functools.partial(pack_kernel, tiles, col_groups, segments...  8.78 us
    ppermute x6, starting transfers between devices, swap(): lax.ppermute(blocks[m], axis, [(i, i ^ m) for i in range(count)])  6.98 us
    ppermute x1, waiting for transfers between devices, on_device(): halo = lax.ppermute(edge, 'space', [(i, i + 1) for i in range(strips - 1)])  6.47 us
    ppermute x1, starting transfers between devices, on_device(): halo = lax.ppermute(edge, 'space', [(i, i + 1) for i in range(strips - 1)])  1.92 us
    unnamed x8, local copies, waits for them, and re-layouts  1.72 us
  transfers between devices with their start and end apart: 7, of which 6 were waited for; matrix products, arithmetic and copies ran while one was open for 0% of the time, Pallas kernels for 0%

profile of v1, /device:TPU:16, one launch (start us, length us, event | category | flops | bytes accessed | tf_op | source)
XLA Modules:
  0.0 74.4 jit_solution(11541499343377534560)
XLA Ops:
  0.0 1.2 %slice_convert_fusion = bf16[32,3,576]{2,1,0:T(4,128)(2,1)S(1)} fusion(s32[32,24,576]{2,1,0:T(8,128)} %valid_ref.1), kind=kLoop, calls=%fused_computation | loop fusion | flops 55296 | bytes 331776 | tf_op jit(solution)/shard_map/convert
  1.2 1.4 %slice_multiply_fusion = bf16[2,32,3,576]{3,2,1,0:T(4,128)(2,1)S(1)} fusion(bf16[2,32,24,576]{3,2,1,0:T(8,128)(2,1)} %acq_ref.1, bf16[32,3,576]{2,1,0:T(4,128)(2,1)S(1)} %slice_convert_fusion), kind=kLoop, calls=%fused_computation.1 | loop fusion | flops 110592 | bytes 552960 | tf_op jit(solution)/shard_map/mul | solution.py:285
  2.5 1.9 %collective-permute-start = (bf16[2,32,3,576]{3,2,1,0:T(4,128)(2,1)S(1)}, bf16[2,32,3,576]{3,2,1,0:T(4,128)(2,1)S(1)}, u32[]{:S(2)}, u32[]{:S(2)}) collective-permute-start(bf16[2,32,3,576]{3,2,1,0:T(4,128)(2,1)S(1)} %slice_multiply_fusion), channel_id=1, source_target_pairs={{0,1},{1,2},{2,3},{3,4},{4,5},{5,6},{6,7},{8,9},{9,10},{10,11},{11... | collective-permute-start | bytes 663560 | tf_op jit(solution)/shard_map/ppermute | solution.py:286
  4.5 6.5 %collective-permute-done.halo_ref = bf16[2,32,3,576]{3,2,1,0:T(4,128)(2,1)S(1)} collective-permute-done((bf16[2,32,3,576]{3,2,1,0:T(4,128)(2,1)S(1)}, bf16[2,32,3,576]{3,2,1,0:T(4,128)(2,1)S(1)}, u32[]{:S(2)}, u32[]{:S(2)}) %collective-permute-start) | collective-permute-done | bytes 221216 | tf_op jit(solution)/shard_map/ppermute | solution.py:286
  10.9 0.0 copy-start.3
  10.9 0.7 copy-done.3
  11.7 8.8 %pack.1 = (bf16[32,2,32,128]{3,2,1,0:T(8,128)(2,1)}, bf16[32,2,32,128]{3,2,1,0:T(8,128)(2,1)}, bf16[32,2,32,128]{3,2,1,0:T(8,128)(2,1)}, bf16[32,2,32,128]{3,2,1,0:T(8,128)(2,1)}) custom-call(bf16[2,32,24,576]{3,2,1,0:T(8,128)(2,1)} %acq_ref.1, s32[32,24,576]{2,1,0:T(8,128)} %valid_ref.1, bf16[2,32,3,576]{3,2,1,0:T(4,128)(2,1)} %copy-done.3), custom_call_target="tpu_custom_call" | custom-call | tf_op jit(solution)/shard_map/pack/pallas_call | solution.py:119
  20.4 1.5 %collective-permute-start.1 = (bf16[32,2,32,128]{3,2,1,0:T(8,128)(2,1)}, bf16[32,2,32,128]{3,2,1,0:T(8,128)(2,1)S(1)}, u32[]{:S(2)}, u32[]{:S(2)}) collective-permute-start(bf16[32,2,32,128]{3,2,1,0:T(8,128)(2,1)} %get-tuple-element.14), channel_id=1, source_target_pairs={{0,8},{8,0},{16,24},{24,16},{1,9},{9,1},{17,25},{25,17},{2,10},{10... | collective-permute-start | bytes 1572872 | tf_op jit(solution)/shard_map/ppermute | solution.py:273
  21.9 1.5 %collective-permute-start.2 = (bf16[32,2,32,128]{3,2,1,0:T(8,128)(2,1)}, bf16[32,2,32,128]{3,2,1,0:T(8,128)(2,1)S(1)}, u32[]{:S(2)}, u32[]{:S(2)}) collective-permute-start(bf16[32,2,32,128]{3,2,1,0:T(8,128)(2,1)} %get-tuple-element.15), channel_id=1, source_target_pairs={{0,16},{8,24},{16,0},{24,8},{1,17},{9,25},{17,1},{25,9},{2,18},{10... | collective-permute-start | bytes 1572872 | tf_op jit(solution)/shard_map/ppermute | solution.py:273
  23.4 0.5 collective-permute-start.3
  23.9 11.6 %collective-permute-done.1.refs_1_ = bf16[32,2,32,128]{3,2,1,0:T(8,128)(2,1)S(1)} collective-permute-done((bf16[32,2,32,128]{3,2,1,0:T(8,128)(2,1)}, bf16[32,2,32,128]{3,2,1,0:T(8,128)(2,1)S(1)}, u32[]{:S(2)}, u32[]{:S(2)}) %collective-permute-start.1) | collective-permute-done | bytes 524320 | tf_op jit(solution)/shard_map/ppermute | solution.py:273
  35.5 0.0 copy-start
  35.5 10.6 %collective-permute-done.2.refs_2_ = bf16[32,2,32,128]{3,2,1,0:T(8,128)(2,1)S(1)} collective-permute-done((bf16[32,2,32,128]{3,2,1,0:T(8,128)(2,1)}, bf16[32,2,32,128]{3,2,1,0:T(8,128)(2,1)S(1)}, u32[]{:S(2)}, u32[]{:S(2)}) %collective-permute-start.2) | collective-permute-done | bytes 524320 | tf_op jit(solution)/shard_map/ppermute | solution.py:273
  46.1 0.0 copy-start.1
  46.2 0.0 collective-permute-done.3.refs_3_
  46.2 0.0 copy-start.2
  46.2 0.0 copy-done
  46.2 0.8 %copy-done.1 = bf16[32,2,32,128]{3,2,1,0:T(8,128)(2,1)} copy-done((bf16[32,2,32,128]{3,2,1,0:T(8,128)(2,1)}, bf16[32,2,32,128]{3,2,1,0:T(8,128)(2,1)S(1)}, u32[]{:S(2)}) %copy-start.1) | copy-done | bytes 524312
  47.0 0.2 copy-done.2
  47.2 18.5 %link.1 = (f32[2,32,192]{2,1,0:T(8,128)}, f32[2,32,192]{2,1,0:T(8,128)}, f32[2,32,192]{2,1,0:T(8,128)}, f32[2,32,192]{2,1,0:T(8,128)}) custom-call(bf16[32,2,32,128]{3,2,1,0:T(8,128)(2,1)} %get-tuple-element.13.refs_0_, bf16[32,2,32,128]{3,2,1,0:T(8,128)(2,1)} %copy-done, bf16[32,2,32,128]{3,2,1,0:T(8,128)(2,1)} %copy-done.1, bf16[32,2,32,128]{3,2,1,0:T(8,128)(2,1)} %copy-done.2), custom_call_target="tpu_custom_call" | custom-call | tf_op jit(solution)/shard_map/link/pallas_call | solution.py:254
  65.7 1.5 %collective-permute-start.4 = (f32[2,32,192]{2,1,0:T(8,128)}, f32[2,32,192]{2,1,0:T(8,128)S(1)}, u32[]{:S(2)}, u32[]{:S(2)}) collective-permute-start(f32[2,32,192]{2,1,0:T(8,128)} %get-tuple-element.17), channel_id=1, source_target_pairs={{0,24},{8,16},{16,8},{24,0},{1,25},{9,17},{17,9},{25,1},{2,26},{10... | collective-permute-start | bytes 147464 | tf_op jit(solution)/shard_map/ppermute | solution.py:273
  67.2 1.0 %collective-permute-start.5 = (f32[2,32,192]{2,1,0:T(8,128)}, f32[2,32,192]{2,1,0:T(8,128)S(1)}, u32[]{:S(2)}, u32[]{:S(2)}) collective-permute-start(f32[2,32,192]{2,1,0:T(8,128)} %get-tuple-element.18), channel_id=1, source_target_pairs={{0,16},{8,24},{16,0},{24,8},{1,17},{9,25},{17,1},{25,9},{2,18},{10... | collective-permute-start | bytes 147464 | tf_op jit(solution)/shard_map/ppermute | solution.py:273
  68.2 1.0 %collective-permute-start.6 = (f32[2,32,192]{2,1,0:T(8,128)}, f32[2,32,192]{2,1,0:T(8,128)S(1)}, u32[]{:S(2)}, u32[]{:S(2)}) collective-permute-start(f32[2,32,192]{2,1,0:T(8,128)} %get-tuple-element.19), channel_id=1, source_target_pairs={{0,8},{8,0},{16,24},{24,16},{1,9},{9,1},{17,25},{25,17},{2,10},{10... | collective-permute-start | bytes 147464 | tf_op jit(solution)/shard_map/ppermute | solution.py:273
  69.2 1.9 %collective-permute-done.4 = f32[2,32,192]{2,1,0:T(8,128)S(1)} collective-permute-done((f32[2,32,192]{2,1,0:T(8,128)}, f32[2,32,192]{2,1,0:T(8,128)S(1)}, u32[]{:S(2)}, u32[]{:S(2)}) %collective-permute-start.4) | collective-permute-done | bytes 49184 | tf_op jit(solution)/shard_map/ppermute | solution.py:273
  71.1 0.7 collective-permute-done.5
  71.8 0.9 %collective-permute-done.6 = f32[2,32,192]{2,1,0:T(8,128)S(1)} collective-permute-done((f32[2,32,192]{2,1,0:T(8,128)}, f32[2,32,192]{2,1,0:T(8,128)S(1)}, u32[]{:S(2)}, u32[]{:S(2)}) %collective-permute-start.6) | collective-permute-done | bytes 49184 | tf_op jit(solution)/shard_map/ppermute | solution.py:273
  72.7 0.9 %select_bitcast_fusion.3 = (f32[2,32,1,192]{3,1,0,2:T(8,128)S(1)}, f32[2,32,1,192]{3,1,0,2:T(8,128)S(1)}, f32[2,32,1,192]{3,1,0,2:T(8,128)S(1)}, f32[2,32,1,192]{3,1,0,2:T(8,128)S(1)}) fusion(f32[2,32,192]{2,1,0:T(8,128)S(1)} %collective-permute-done.4, f32[2,32,192]{2,1,0:T(8,128)S(1)} %collective-permute-done.5, ...), kind=kLoop, calls=%fused_computation.6 | loop fusion | flops 147456 | bytes 393219 | tf_op jit(solution)/shard_map/stack | solution.py:302
  73.6 0.9 %copy.3 = f32[2,32,4,192]{3,2,1,0:T(4,128)} copy(f32[2,32,4,192]{3,1,0,2:T(8,128)S(1)} %pad_maximum_fusion) | data formatting | bytes 393216 | tf_op jit(solution)/shard_map/stack | solution.py:302
  (1 shorter events, 0.0 us)
Async XLA Ops:
  2.5 8.4 %collective-permute-start = (bf16[2,32,3,576]{3,2,1,0:T(4,128)(2,1)S(1)}, bf16[2,32,3,576]{3,2,1,0:T(4,128)(2,1)S(1)}, u32[]{:S(2)}, u32[]{:S(2)}) collective-permute-start(bf16[2,32,3,576]{3,2,1,0:T(4,128)(2,1)S(1)} %slice_multiply_fusion), channel_id=1, source_target_pairs={{0,1},{1,2},{2,3},{3,4},{4,5},{5,6},{6,7},{8,9},{9,10},{10,11},{11... | collective-permute-start | bytes 663560 | tf_op jit(solution)/shard_map/ppermute | solution.py:286
  10.9 0.7 copy-start.3
  20.4 15.1 %collective-permute-start.1 = (bf16[32,2,32,128]{3,2,1,0:T(8,128)(2,1)}, bf16[32,2,32,128]{3,2,1,0:T(8,128)(2,1)S(1)}, u32[]{:S(2)}, u32[]{:S(2)}) collective-permute-start(bf16[32,2,32,128]{3,2,1,0:T(8,128)(2,1)} %get-tuple-element.14), channel_id=1, source_target_pairs={{0,8},{8,0},{16,24},{24,16},{1,9},{9,1},{17,25},{25,17},{2,10},{10... | collective-permute-start | bytes 1572872 | tf_op jit(solution)/shard_map/ppermute | solution.py:273
  21.9 24.2 %collective-permute-start.2 = (bf16[32,2,32,128]{3,2,1,0:T(8,128)(2,1)}, bf16[32,2,32,128]{3,2,1,0:T(8,128)(2,1)S(1)}, u32[]{:S(2)}, u32[]{:S(2)}) collective-permute-start(bf16[32,2,32,128]{3,2,1,0:T(8,128)(2,1)} %get-tuple-element.15), channel_id=1, source_target_pairs={{0,16},{8,24},{16,0},{24,8},{1,17},{9,25},{17,1},{25,9},{2,18},{10... | collective-permute-start | bytes 1572872 | tf_op jit(solution)/shard_map/ppermute | solution.py:273
  23.4 22.7 %collective-permute-start.3 = (bf16[32,2,32,128]{3,2,1,0:T(8,128)(2,1)}, bf16[32,2,32,128]{3,2,1,0:T(8,128)(2,1)S(1)}, u32[]{:S(2)}, u32[]{:S(2)}) collective-permute-start(bf16[32,2,32,128]{3,2,1,0:T(8,128)(2,1)} %get-tuple-element.16), channel_id=1, source_target_pairs={{0,24},{8,16},{16,8},{24,0},{1,25},{9,17},{17,9},{25,1},{2,26},{10... | collective-permute-start | bytes 1572872 | tf_op jit(solution)/shard_map/ppermute | solution.py:273
  35.5 10.6 %copy-start = (bf16[32,2,32,128]{3,2,1,0:T(8,128)(2,1)}, bf16[32,2,32,128]{3,2,1,0:T(8,128)(2,1)S(1)}, u32[]{:S(2)}) copy-start(bf16[32,2,32,128]{3,2,1,0:T(8,128)(2,1)S(1)} %collective-permute-done.1.refs_1_) | copy-start | bytes 1572868
  46.1 0.8 %copy-start.1 = (bf16[32,2,32,128]{3,2,1,0:T(8,128)(2,1)}, bf16[32,2,32,128]{3,2,1,0:T(8,128)(2,1)S(1)}, u32[]{:S(2)}) copy-start(bf16[32,2,32,128]{3,2,1,0:T(8,128)(2,1)S(1)} %collective-permute-done.2.refs_2_) | copy-start | bytes 1572868
  46.2 1.0 %copy-start.2 = (bf16[32,2,32,128]{3,2,1,0:T(8,128)(2,1)}, bf16[32,2,32,128]{3,2,1,0:T(8,128)(2,1)S(1)}, u32[]{:S(2)}) copy-start(bf16[32,2,32,128]{3,2,1,0:T(8,128)(2,1)S(1)} %collective-permute-done.3.refs_3_) | copy-start | bytes 1572868
  65.7 5.4 %collective-permute-start.4 = (f32[2,32,192]{2,1,0:T(8,128)}, f32[2,32,192]{2,1,0:T(8,128)S(1)}, u32[]{:S(2)}, u32[]{:S(2)}) collective-permute-start(f32[2,32,192]{2,1,0:T(8,128)} %get-tuple-element.17), channel_id=1, source_target_pairs={{0,24},{8,16},{16,8},{24,0},{1,25},{9,17},{17,9},{25,1},{2,26},{10... | collective-permute-start | bytes 147464 | tf_op jit(solution)/shard_map/ppermute | solution.py:273
  67.2 4.6 %collective-permute-start.5 = (f32[2,32,192]{2,1,0:T(8,128)}, f32[2,32,192]{2,1,0:T(8,128)S(1)}, u32[]{:S(2)}, u32[]{:S(2)}) collective-permute-start(f32[2,32,192]{2,1,0:T(8,128)} %get-tuple-element.18), channel_id=1, source_target_pairs={{0,16},{8,24},{16,0},{24,8},{1,17},{9,25},{17,1},{25,9},{2,18},{10... | collective-permute-start | bytes 147464 | tf_op jit(solution)/shard_map/ppermute | solution.py:273
  68.2 4.5 %collective-permute-start.6 = (f32[2,32,192]{2,1,0:T(8,128)}, f32[2,32,192]{2,1,0:T(8,128)S(1)}, u32[]{:S(2)}, u32[]{:S(2)}) collective-permute-start(f32[2,32,192]{2,1,0:T(8,128)} %get-tuple-element.19), channel_id=1, source_target_pairs={{0,8},{8,0},{16,24},{24,16},{1,9},{9,1},{17,25},{25,17},{2,10},{10... | collective-permute-start | bytes 147464 | tf_op jit(solution)/shard_map/ppermute | solution.py:273

commit v2 on v1

v2 whole, which is shorter than its diff:
```python
import functools
import math

import jax
import jax.numpy as jnp
from jax import lax
from jax.experimental import pallas as pl
from jax.experimental.pallas import tpu as pltpu
from jax.sharding import PartitionSpec as P

BOX_ROWS = 15
BOX_COLS = 7
STEP_ROWS = 3
STEP_COLS = 6
ITERS = 4
MARGIN = 6
NBOX = 105
POWER_EPS = 1e-05

LANES = 128
TILE_ROWS = 18
SLOTS = TILE_ROWS // STEP_ROWS
LEAD = MARGIN // STEP_ROWS
LEFT = STEP_COLS // 2
BATCH = 48
CHUNKS = (4,)
CONTRACT_LAST = (((1,), (1,)), ((), ()))


def lane_mask(first, count):
    lane = lax.broadcasted_iota(jnp.int32, (16, LANES), 1)
    inside = ((lane - first) & (LANES - 1)) < count
    return (jnp.where(inside, 1.0, 0.0).astype(jnp.bfloat16) > 0)[None]


def choose(mask, yes, no):
    return jnp.where(jnp.broadcast_to(mask, yes.shape), yes, no)


def edge_kernel(first, *refs):
    acq_ref, valid_ref, out, planes = refs
    parts, dates, _, rows = acq_ref.shape
    stride = planes.shape[2] // dates
    span = slice(first // 8 * 8, first // 8 * 8 + 8)
    offset = first % 8

    def one_date(date, carry):
        keep = valid_ref[date, span].astype(jnp.float32)
        for part in range(parts):
            value = acq_ref[part, date, span].astype(jnp.float32) * keep
            for block in range(planes.shape[1]):
                width = min(LANES, rows - block * LANES)
                planes[part, block, pl.ds(date * stride, 8), :width] = value[
                    :, block * LANES : block * LANES + width
                ]
        return carry

    for part in range(parts):
        planes[part, planes.shape[1] - 1] = jnp.zeros(planes.shape[2:], jnp.float32)
    lax.fori_loop(0, dates, one_date, 0, unroll=4)
    for j in range(LEFT):
        for part in range(parts):
            for block in range(planes.shape[1]):
                plane = planes[part, block, pl.ds(offset + j, dates, stride=stride), :]
                out[j, part, :, block * LANES : (block + 1) * LANES] = plane.astype(out.dtype)


def edge(acquisitions, valid_dates):
    parts, dates, cols, rows = acquisitions.shape
    blocks = -(-rows // LANES)
    at = (cols - LEFT) // 16
    shape = jax.ShapeDtypeStruct((LEFT, parts, dates, blocks * LANES), acquisitions.dtype)
    return pl.pallas_call(
        functools.partial(edge_kernel, cols - LEFT - at * 16),
        grid=(1,),
        out_shape=shape,
        in_specs=[
            pl.BlockSpec((parts, dates, 16, rows), lambda i: (0, 0, at, 0)),
            pl.BlockSpec((dates, 16, rows), lambda i: (0, at, 0)),
        ],
        out_specs=pl.BlockSpec(shape.shape, lambda i: (0, 0, 0, 0)),
        scratch_shapes=[pltpu.VMEM((parts, blocks, dates * 9, LANES), jnp.float32)],
        compiler_params=pltpu.CompilerParams(vmem_limit_bytes=56 << 20),
        name="edge",
    )(acquisitions, valid_dates)


def pack_kernel(tiles, first_block, blocks, col_groups, segments, axis, *refs):
    acq_refs, refs = refs[:blocks], refs[blocks:]
    valid_refs, refs = refs[:blocks], refs[blocks:]
    halo_ref, refs = refs[0], refs[1:]
    outs, (planes, shifted, halo, sem) = refs[:-4], refs[-4:]
    parts, dates, cols, _ = acq_refs[0].shape
    stride = cols + LEFT
    me = lax.axis_index(axis)
    fetch = pltpu.make_async_copy(halo_ref, halo, sem)
    fetch.start()

    def one_date(date, carry):
        for block in range(blocks):
            keep = valid_refs[block][date].astype(jnp.float32)
            for part in range(parts):
                value = acq_refs[block][part, date].astype(jnp.float32) * keep
                planes[part, block, pl.ds(date * stride, cols)] = value
        return carry

    lax.fori_loop(0, dates, one_date, 0, unroll=4)

    def place(group, block, j, part, plane):
        if j:
            plane = pltpu.roll(plane, TILE_ROWS * j, 1)
        shifted[group, block, j, part] = plane.astype(jnp.bfloat16)

    def one_block(block, carry):
        for group in range(col_groups):
            for j in range(BOX_COLS):
                column = group * STEP_COLS - LEFT + j
                for part in range(parts):
                    if column >= 0:
                        plane = planes[part, block, pl.ds(column, dates, stride=stride), :]
                        place(group, block, j, part, plane)
        return carry

    lax.fori_loop(0, blocks, one_block, 0)
    fetch.wait()
    for block in range(blocks):
        at = (first_block + block) * LANES
        for j in range(LEFT):
            for part in range(parts):
                place(0, block, j, part, halo[j, part, :, at : at + LANES].astype(jnp.float32))
    masks = {}
    for offset, out in enumerate(outs):
        target = me ^ offset
        group = lax.rem(target, col_groups)
        if segments == 1:
            for index, tile in enumerate(tiles):
                total = jnp.zeros((parts * dates // 16, 16, LANES), jnp.bfloat16)
                for j in range(BOX_COLS):
                    row, end = tile * TILE_ROWS, (tile + 1) * TILE_ROWS
                    while row < end:
                        block = row // LANES
                        stop = min(end, (block + 1) * LANES)
                        key = ((row + TILE_ROWS * j) % LANES, stop - row)
                        if key not in masks:
                            masks[key] = lane_mask(*key)
                        piece = shifted[group, block - first_block, j]
                        total = choose(masks[key], piece.reshape(total.shape), total)
                        row = stop
                out[index] = total.reshape(parts, dates, LANES)
        else:
            segment = target // col_groups
            last = segments * len(tiles) - 1

            def one_tile(index, carry):
                tile = segment * len(tiles) + index - 1
                kept = jnp.where((tile >= 0) & (tile <= last), TILE_ROWS, 0)
                row = jnp.clip(tile, 0, last) * TILE_ROWS
                low, high = row // LANES, (row + TILE_ROWS - 1) // LANES
                split = jnp.where(high == low, TILE_ROWS, high * LANES - row)
                total = jnp.zeros((parts * dates // 16, 16, LANES), jnp.bfloat16)
                for j in range(BOX_COLS):
                    start = row + TILE_ROWS * j
                    for block, first, count in (
                        (low, start, jnp.minimum(split, kept)),
                        (high, start + split, jnp.minimum(TILE_ROWS - split, kept)),
                    ):
                        piece = shifted[group, block, j].reshape(total.shape)
                        total = choose(lane_mask(first, count), piece, total)
                out[index] = total.reshape(parts, dates, LANES)
                return carry

            lax.fori_loop(0, len(tiles) + 2, one_tile, 0)


def pack(acquisitions, valid_dates, halo, peers, tiles, col_groups, segments):
    parts, dates, cols, rows = acquisitions.shape
    if segments == 1:
        sent = len(tiles)
        first = tiles[0] * TILE_ROWS // LANES
        blocks = -(-(tiles[-1] + 1) * TILE_ROWS // LANES) - first
    else:
        sent, first, blocks = len(tiles) + 2, 0, -(-rows // LANES)

    def block_specs(shape):
        return [
            pl.BlockSpec(
                shape + (LANES,), functools.partial(lambda b, i: (0,) * len(shape) + (b,), first + k)
            )
            for k in range(blocks)
        ]

    shape = jax.ShapeDtypeStruct((sent, parts, dates, LANES), jnp.bfloat16)
    kernel = functools.partial(pack_kernel, tiles, first, blocks, col_groups, segments, "date")
    return pl.pallas_call(
        kernel,
        grid=(1,),
        out_shape=[shape] * peers,
        in_specs=block_specs((parts, dates, cols))
        + block_specs((dates, cols))
        + [pl.BlockSpec(memory_space=pl.ANY)],
        out_specs=[pl.BlockSpec(shape.shape, lambda i: (0, 0, 0, 0))] * peers,
        scratch_shapes=[
            pltpu.VMEM((parts, blocks, dates * (cols + LEFT), LANES), jnp.float32),
            pltpu.VMEM((col_groups, blocks, BOX_COLS, parts, dates, LANES), jnp.bfloat16),
            pltpu.VMEM(halo.shape, halo.dtype),
            pltpu.SemaphoreType.DMA,
        ],
        compiler_params=pltpu.CompilerParams(vmem_limit_bytes=56 << 20),
        cost_estimate=pl.CostEstimate(
            flops=10**8, bytes_accessed=blocks * 3 * 10**6, transcendentals=0
        ),
        name="pack",
    )(*[acquisitions] * blocks, *[valid_dates] * blocks, halo)


def slot_rows(first):
    lane = lax.broadcasted_iota(jnp.int32, (16, LANES), 1)
    place = (lane - first) & (LANES - 1)
    column = (place * 57) >> 10
    return place - TILE_ROWS * column, column < BOX_COLS


def as_mask(inside):
    return jnp.where(inside, 1.0, 0.0).astype(jnp.bfloat16)[None]


def window_pair(real, imag, k, e, row_now, row_next):
    shape = (-1, 16, LANES)
    begin, spill = STEP_ROWS * e, STEP_ROWS * e + BOX_ROWS - TILE_ROWS
    now, after = row_now >= begin, row_next < spill + STEP_ROWS
    both, a, b = [], real[k].reshape(shape), imag[k].reshape(shape)
    a, b = a * as_mask(now), b * as_mask(now)
    if spill > 0:
        first = as_mask(now | (row_next < spill))
        second = as_mask((row_now >= begin + STEP_ROWS) | after)
        a = a + real[k + 1].reshape(shape) * as_mask(after)
        b = b + imag[k + 1].reshape(shape) * as_mask(after)
    else:
        first = as_mask(now & (row_now < BOX_ROWS))
        second = as_mask(row_now >= STEP_ROWS)
    for window in (first, second):
        parts = [(part * window).reshape(real.shape[1:]) for part in (a, b)]
        both.append(jnp.concatenate(parts, axis=1))
    return a.reshape(real.shape[1:]), b.reshape(real.shape[1:]), both


def coherence_pair(a, b, both, diagonal, held, place):
    count = a.shape[0]
    left = jnp.concatenate(
        [jnp.concatenate([a, b], axis=1), jnp.concatenate([b, -a], axis=1)], axis=0
    )
    sums = lax.dot_general(
        left, jnp.concatenate(both, axis=0), CONTRACT_LAST, preferred_element_type=jnp.float32
    )
    for index in range(2):
        real = sums[:count, index * count : (index + 1) * count]
        imag = sums[count:, index * count : (index + 1) * count]
        energy = jnp.sum(jnp.where(diagonal, real, 0.0), axis=0, keepdims=True) * (1 / NBOX)
        factor = lax.rsqrt(energy + POWER_EPS)
        down = jnp.sum(jnp.where(diagonal, factor, 0.0), axis=1, keepdims=True)
        weights = down * (factor * (1 / NBOX))
        held[place + index, :count] = (real * weights).astype(jnp.bfloat16)
        held[place + index, count:] = (imag * weights).astype(jnp.bfloat16)


def iterate(held, pixels, dates):
    row = lax.broadcasted_iota(jnp.int32, (8, dates), 0)
    odd = (row & 1) == 1
    sign = jnp.where((row & 2) == 2, -1.0, 1.0)
    start = jnp.concatenate([jnp.where(odd, 0.0, sign), jnp.where(odd, -sign, 0.0)], axis=1)
    vectors = [start.astype(jnp.bfloat16)] * pixels
    for sweep in range(ITERS):
        scaled = []
        for place in range(pixels):
            product = jnp.dot(vectors[place], held[place], preferred_element_type=jnp.float32)
            square = product * product
            square = square + pltpu.roll(square, 1, 0)
            total = jnp.sum(square, axis=1, keepdims=True) * (1 / dates) + POWER_EPS
            scaled.append(product * lax.rsqrt(total))
        if sweep + 1 < ITERS:
            vectors = [
                jnp.concatenate([v, pltpu.roll(v, 7, 0)], axis=1).astype(jnp.bfloat16)
                for v in scaled
            ]
    return scaled


def link_kernel(peers, carried, earlier, start, padded, last, *refs):
    sources, refs = refs[:peers], refs[peers:]
    before, refs = refs[: peers * carried], refs[peers * carried :]
    done, refs = refs[:earlier], refs[earlier:]
    outs, (real, imag, held, linked, sems) = refs[:-5], refs[-5:]
    sent, _, dates, _ = sources[0].shape
    all_dates = peers * dates
    base = 0 if padded else 2 if carried else 1
    copies = []

    def fetch(tiles, part, at, peer):
        room = (real, imag)[part].at[pl.ds(at, tiles.shape[0]), pl.ds(peer * dates, dates)]
        copies.append(pltpu.make_async_copy(tiles.at[:, part], room, sems.at[len(copies)]))
        copies[-1].start()

    for peer, source in enumerate(sources):
        for part in range(2):
            fetch(source, part, base, peer)
            if carried:
                tiles = before[peer]
                fetch(tiles.at[pl.ds(tiles.shape[0] - 2, 2)], part, 0, peer)
    zero = jnp.zeros((all_dates, LANES), jnp.bfloat16)
    for tiles in (real, imag):
        if not carried and not padded:
            tiles[0] = zero
        if last and not padded:
            tiles[base + sent] = zero
    for copy in copies:
        copy.wait()
    pixels = linked.shape[0] // 8
    batch = math.gcd(BATCH, pixels)
    diagonal = lax.broadcasted_iota(
        jnp.int32, (all_dates, all_dates), 0
    ) == lax.broadcasted_iota(jnp.int32, (all_dates, all_dates), 1)

    def step(index, carry):
        rows_of = {}

        def rows_at(k):
            if k not in rows_of:
                tile = start // SLOTS - 1 + index * (batch // SLOTS) + k
                if padded:
                    tile = tile + lax.axis_index("date") // padded * (sent - 2)
                row, used = slot_rows(tile * TILE_ROWS)
                rows_of[k] = jnp.where(used, row, -1), jnp.where(used, row, LANES)
            return rows_of[k]

        for place in range(0, batch, 2):
            k, e = divmod(place + SLOTS - LEAD, SLOTS)
            at = index * (batch // SLOTS) + k
            a, b, both = window_pair(real, imag, at, e, rows_at(k)[0], rows_at(k + 1)[1])
            coherence_pair(a, b, both, diagonal, held, place)
        for place, tile in enumerate(iterate(held, batch, all_dates)):
            linked[pl.ds((index * batch + place) * 8, 8)] = tile
        return carry

    lax.fori_loop(0, pixels // batch, step, 0)
    for part in range(2):
        vectors = linked[pl.ds(part, pixels, stride=8), :]
        if not last:
            outs[0][part] = vectors
            continue
        vectors = jnp.concatenate([ref[part] for ref in done] + [vectors], axis=0)
        flat = jnp.transpose(vectors)
        for peer, out in enumerate(outs):
            out[part] = flat[peer * dates : (peer + 1) * dates]


def link(sources, before, done, start, pixels, padded, last):
    peers = len(sources)
    sent, parts, dates, _ = sources[0].shape
    all_dates = peers * dates
    whole = pl.BlockSpec(memory_space=pltpu.VMEM)
    operands = list(sources) + list(before)
    specs = [pl.BlockSpec(memory_space=pl.ANY)] * len(operands)
    operands += done
    specs += [whole] * len(done)
    if last:
        rows = start + pixels
        outs = [jax.ShapeDtypeStruct((parts, dates, rows), jnp.float32)] * peers
    else:
        outs = [jax.ShapeDtypeStruct((parts, pixels, all_dates), jnp.float32)]
    kept = sent + 3
    kernel = functools.partial(
        link_kernel, peers, len(before) > 0, len(done), start, padded, last
    )
    return pl.pallas_call(
        kernel,
        grid=(1,),
        out_shape=outs,
        in_specs=specs,
        out_specs=[whole] * len(outs),
        scratch_shapes=[
            pltpu.VMEM((kept, all_dates, LANES), jnp.bfloat16),
            pltpu.VMEM((kept, all_dates, LANES), jnp.bfloat16),
            pltpu.VMEM((math.gcd(BATCH, pixels), 2 * all_dates, all_dates), jnp.bfloat16),
            pltpu.VMEM((pixels * 8, all_dates), jnp.float32),
            pltpu.SemaphoreType.DMA((4 * peers,)),
        ],
        compiler_params=pltpu.CompilerParams(vmem_limit_bytes=56 << 20),
        cost_estimate=pl.CostEstimate(
            flops=pixels * 30 * 10**6, bytes_accessed=10**6, transcendentals=0
        ),
        name="link",
    )(*operands)


def swap(blocks, axis):
    count = len(blocks)
    return [blocks[0]] + [
        lax.ppermute(blocks[m], axis, [(i, i ^ m) for i in range(count)]) for m in range(1, count)
    ]


def place_kernel(peers, out_cols, *refs):
    blocks, out = refs[:peers], refs[peers]
    rows = blocks[0].shape[2]
    me = lax.axis_index("date")
    for target in range(peers):
        value = blocks[target][...]
        for other in range(1, peers):
            value = jnp.where(me == other, blocks[target ^ other][...], value)
        segment = target // out_cols * rows
        out[:, :, target % out_cols, segment : segment + rows] = value


def place_blocks(blocks, out_cols, segments):
    parts, dates, rows = blocks[0].shape
    whole = pl.BlockSpec(memory_space=pltpu.VMEM)
    return pl.pallas_call(
        functools.partial(place_kernel, len(blocks), out_cols),
        out_shape=jax.ShapeDtypeStruct((parts, dates, out_cols, rows * segments), jnp.float32),
        in_specs=[whole] * len(blocks),
        out_specs=whole,
        compiler_params=pltpu.CompilerParams(vmem_limit_bytes=56 << 20),
        name="place",
    )(*blocks)


def chunk_ends(tiles, segments):
    step = BATCH // SLOTS
    if segments > 1 or tiles % step:
        return [tiles]
    count = tiles // step
    return [step * (count * share // 8) + 1 for share in CHUNKS] + [tiles]


def on_device(acquisitions, valid_dates):
    peers = lax.axis_size("date")
    strips = lax.axis_size("space")
    parts, dates, cols, rows = acquisitions.shape
    out_cols = cols // STEP_COLS
    segments = peers // out_cols
    tiles = rows // TILE_ROWS // segments
    pixels = rows // STEP_ROWS // segments
    halo = lax.ppermute(
        edge(acquisitions, valid_dates), "space", [(i, i + 1) for i in range(strips - 1)]
    )
    ends = chunk_ends(tiles, segments)
    outgoing = [
        pack(acquisitions, valid_dates, halo, peers, range(low, high), out_cols, segments)
        for low, high in zip([0] + ends[:-1], ends)
    ]
    incoming = [swap(blocks, "date") for blocks in outgoing]
    done, start = [], 0
    for index, blocks in enumerate(incoming):
        last = index == len(ends) - 1
        stop = pixels if last else (ends[index] - 1) * SLOTS
        before = incoming[index - 1] if index else []
        result = link(
            blocks, before, done if last else [], start, stop - start,
            0 if segments == 1 else out_cols, last,
        )
        done, start = done + list(result), stop
    incoming = swap(result, "date")
    return place_blocks(incoming, out_cols, segments)


def solution(mesh):
    in_specs = (P(None, "date", "space", None), P("date", "space", None))
    out_specs = P(None, "date", "space", None)
    return jax.shard_map(
        on_device, mesh=mesh, in_specs=in_specs, out_specs=out_specs, check_vma=False
    )
```

time: 74.7 us -> 62.5 us (0.84)
  waiting for transfers between devices: 32.1 us -> 14.2 us
  starting transfers between devices: 8.9 us -> 13.7 us
  Pallas kernels: 27.3 us -> 31.1 us
  other arithmetic: 3.43 us -> 0 us
    ppermute x6 -> x9, waiting for transfers between devices: 25.7 us -> 8.41 us  [swap(): lax.ppermute(blocks[m], axis, [(i, i ^ m) for i in range(count)])]
    ppermute x6 -> x9, starting transfers between devices: 6.98 us -> 11.8 us  [swap(): lax.ppermute(blocks[m], axis, [(i, i ^ m) for i in range(count)])]
    pallas_call x2 -> x6, Pallas kernels: 27.3 us -> 31.1 us  [the longest x2 19 us: link(): pl.pallas_call(kernel, grid=(1,), out_shape=outs, in_specs=specs, out_spe...]
    another operation x3 -> x0, other arithmetic: 2.07 us -> none
    mul x1 -> x0, other arithmetic: 1.36 us -> none  [on_device(): acquisitions[:, :, cols - LEFT:]]
    unnamed x8 -> x20, local copies, waits for them, and re-layouts: 1.72 us -> 2.85 us
    another operation x1 -> x0, local copies, waits for them, and re-layouts: 0.87 us -> none  [on_device(): return jnp.stack(strips_out, axis=2)]
  transfers between devices with their start and end apart: 7 -> 10, of which waited for: 6 -> 6; matrix products, arithmetic and copies ran while one was open for 0% -> 0% of each run, Pallas kernels for 0% -> 21%
where the time goes in v2:
time: 62.5 us; the launch traced here: 62 us
  Pallas kernels  31.1 us (50%)
  waiting for transfers between devices  14.2 us (23%)
  starting transfers between devices  13.7 us (22%)
  local copies, waits for them, and re-layouts  2.85 us (5%)
    pallas_call x2, Pallas kernels, link(): pl.pallas_call(kernel, grid=(1,), out_shape=outs, in_specs=specs, out_spe...  19 us
    ppermute x9, starting transfers between devices, swap(): lax.ppermute(blocks[m], axis, [(i, i ^ m) for i in range(count)])  11.8 us
    ppermute x9, waiting for transfers between devices, swap(): lax.ppermute(blocks[m], axis, [(i, i ^ m) for i in range(count)])  8.41 us
    pallas_call x2, Pallas kernels, pack(): pl.pallas_call(kernel, grid=(1,), out_shape=[shape] * peers, in_specs=blo...  8.16 us
    ppermute x1, waiting for transfers between devices, on_device(): lax.ppermute(edge(acquisitions, valid_dates), 'space', [(i, i + 1) for i...  5.8 us
    unnamed x20, local copies, waits for them, and re-layouts  2.85 us
    pallas_call x1, Pallas kernels, edge(): pl.pallas_call(functools.partial(edge_kernel, cols - LEFT - at * 16), gri...  2.2 us
    ppermute x1, starting transfers between devices, on_device(): lax.ppermute(edge(acquisitions, valid_dates), 'space', [(i, i + 1) for i...  1.91 us
  transfers between devices with their start and end apart: 10, of which 6 were waited for; matrix products, arithmetic and copies ran while one was open for 0% of the time, Pallas kernels for 21%

profile of v2, /device:TPU:16, one launch (start us, length us, event | category | flops | bytes accessed | tf_op | source)
XLA Modules:
  0.0 62.0 jit_solution(6042009593244140903)
XLA Ops:
  0.0 2.2 %edge.1 = bf16[3,2,32,640]{3,2,1,0:T(8,128)(2,1)} custom-call(bf16[2,32,24,576]{3,2,1,0:T(8,128)(2,1)} %refs_2_.3, s32[32,24,576]{2,1,0:T(8,128)} %refs_5_.3), custom_call_target="tpu_custom_call" | custom-call | tf_op jit(solution)/shard_map/edge/pallas_call | solution.py:73
  2.2 1.9 %collective-permute-start = (bf16[3,2,32,640]{3,2,1,0:T(8,128)(2,1)}, bf16[3,2,32,640]{3,2,1,0:T(8,128)(2,1)S(1)}, u32[]{:S(2)}, u32[]{:S(2)}) collective-permute-start(bf16[3,2,32,640]{3,2,1,0:T(8,128)(2,1)} %edge.1), channel_id=1, source_target_pairs={{0,1},{1,2},{2,3},{3,4},{4,5},{5,6},{6,7},{8,9},{9,10},{10,11},{11... | collective-permute-start | bytes 737288 | tf_op jit(solution)/shard_map/ppermute | solution.py:443
  4.1 5.8 %collective-permute-done.refs_6_ = bf16[3,2,32,640]{3,2,1,0:T(8,128)(2,1)S(1)} collective-permute-done((bf16[3,2,32,640]{3,2,1,0:T(8,128)(2,1)}, bf16[3,2,32,640]{3,2,1,0:T(8,128)(2,1)S(1)}, u32[]{:S(2)}, u32[]{:S(2)}) %collective-permute-start) | collective-permute-done | bytes 245792 | tf_op jit(solution)/shard_map/ppermute | solution.py:443
  9.9 0.0 copy-start
  9.9 0.7 %copy-done = bf16[3,2,32,640]{3,2,1,0:T(8,128)(2,1)} copy-done((bf16[3,2,32,640]{3,2,1,0:T(8,128)(2,1)}, bf16[3,2,32,640]{3,2,1,0:T(8,128)(2,1)S(1)}, u32[]{:S(2)}) %copy-start) | copy-done | bytes 245784
  10.6 4.1 %pack.3 = (bf16[17,2,32,128]{3,2,1,0:T(8,128)(2,1)}, bf16[17,2,32,128]{3,2,1,0:T(8,128)(2,1)}, bf16[17,2,32,128]{3,2,1,0:T(8,128)(2,1)}, bf16[17,2,32,128]{3,2,1,0:T(8,128)(2,1)}) custom-call(bf16[2,32,24,576]{3,2,1,0:T(8,128)(2,1)} %refs_2_.3, bf16[2,32,24,576]{3,2,1,0:T(8,128)(2,1)} %refs_2_.3, bf16[2,32,24,576]{3,2,1,0:T(8,128)(2,1)} %refs_2_.3, ...), custom_call_target="tpu_custom_call" | custom-call | flops 100000000 | bytes 9000000 | tf_op jit(solution)/shard_map/pack/pallas_call | solution.py:194
  14.8 1.6 %collective-permute-start.4 = (bf16[17,2,32,128]{3,2,1,0:T(8,128)(2,1)}, bf16[17,2,32,128]{3,2,1,0:T(8,128)(2,1)S(1)}, u32[]{:S(2)}, u32[]{:S(2)}) collective-permute-start(bf16[17,2,32,128]{3,2,1,0:T(8,128)(2,1)} %get-tuple-element.22), channel_id=1, source_target_pairs={{0,8},{8,0},{16,24},{24,16},{1,9},{9,1},{17,25},{25,17},{2,10},{10... | collective-permute-start | bytes 835592 | tf_op jit(solution)/shard_map/ppermute | solution.py:398
  16.3 1.5 %collective-permute-start.5 = (bf16[17,2,32,128]{3,2,1,0:T(8,128)(2,1)}, bf16[17,2,32,128]{3,2,1,0:T(8,128)(2,1)S(1)}, u32[]{:S(2)}, u32[]{:S(2)}) collective-permute-start(bf16[17,2,32,128]{3,2,1,0:T(8,128)(2,1)} %get-tuple-element.23), channel_id=1, source_target_pairs={{0,16},{8,24},{16,0},{24,8},{1,17},{9,25},{17,1},{25,9},{2,18},{10... | collective-permute-start | bytes 835592 | tf_op jit(solution)/shard_map/ppermute | solution.py:398
  17.8 0.5 collective-permute-start.6
  18.3 4.0 %pack.2 = (bf16[15,2,32,128]{3,2,1,0:T(8,128)(2,1)}, bf16[15,2,32,128]{3,2,1,0:T(8,128)(2,1)}, bf16[15,2,32,128]{3,2,1,0:T(8,128)(2,1)}, bf16[15,2,32,128]{3,2,1,0:T(8,128)(2,1)}) custom-call(bf16[2,32,24,576]{3,2,1,0:T(8,128)(2,1)} %refs_2_.3, bf16[2,32,24,576]{3,2,1,0:T(8,128)(2,1)} %refs_2_.3, bf16[2,32,24,576]{3,2,1,0:T(8,128)(2,1)} %refs_2_.3, ...), custom_call_target="tpu_custom_call" | custom-call | flops 100000000 | bytes 9000000 | tf_op jit(solution)/shard_map/pack/pallas_call | solution.py:194
  22.3 1.6 %collective-permute-start.1 = (bf16[15,2,32,128]{3,2,1,0:T(8,128)(2,1)}, bf16[15,2,32,128]{3,2,1,0:T(8,128)(2,1)S(1)}, u32[]{:S(2)}, u32[]{:S(2)}) collective-permute-start(bf16[15,2,32,128]{3,2,1,0:T(8,128)(2,1)} %get-tuple-element.18), channel_id=1, source_target_pairs={{0,8},{8,0},{16,24},{24,16},{1,9},{9,1},{17,25},{25,17},{2,10},{10... | collective-permute-start | bytes 737288 | tf_op jit(solution)/shard_map/ppermute | solution.py:398
  23.9 1.5 %collective-permute-start.2 = (bf16[15,2,32,128]{3,2,1,0:T(8,128)(2,1)}, bf16[15,2,32,128]{3,2,1,0:T(8,128)(2,1)S(1)}, u32[]{:S(2)}, u32[]{:S(2)}) collective-permute-start(bf16[15,2,32,128]{3,2,1,0:T(8,128)(2,1)} %get-tuple-element.19), channel_id=1, source_target_pairs={{0,16},{8,24},{16,0},{24,8},{1,17},{9,25},{17,1},{25,9},{2,18},{10... | collective-permute-start | bytes 737288 | tf_op jit(solution)/shard_map/ppermute | solution.py:398
  25.4 0.0 collective-permute-done.4.refs_1_.refs_5_
  25.4 0.0 copy-start.4
  25.4 1.6 %collective-permute-start.3 = (bf16[15,2,32,128]{3,2,1,0:T(8,128)(2,1)}, bf16[15,2,32,128]{3,2,1,0:T(8,128)(2,1)S(1)}, u32[]{:S(2)}, u32[]{:S(2)}) collective-permute-start(bf16[15,2,32,128]{3,2,1,0:T(8,128)(2,1)} %get-tuple-element.20), channel_id=1, source_target_pairs={{0,24},{8,16},{16,8},{24,0},{1,25},{9,17},{17,9},{25,1},{2,26},{10... | collective-permute-start | bytes 737288 | tf_op jit(solution)/shard_map/ppermute | solution.py:398
  27.1 3.1 %collective-permute-done.5.refs_2_.refs_6_ = bf16[17,2,32,128]{3,2,1,0:T(8,128)(2,1)S(1)} collective-permute-done((bf16[17,2,32,128]{3,2,1,0:T(8,128)(2,1)}, bf16[17,2,32,128]{3,2,1,0:T(8,128)(2,1)S(1)}, u32[]{:S(2)}, u32[]{:S(2)}) %collective-permute-start.5) | collective-permute-done | bytes 278560 | tf_op jit(solution)/shard_map/ppermute | solution.py:398
  30.2 0.0 copy-start.5
  30.2 1.4 %collective-permute-done.6.refs_3_.refs_7_ = bf16[17,2,32,128]{3,2,1,0:T(8,128)(2,1)S(1)} collective-permute-done((bf16[17,2,32,128]{3,2,1,0:T(8,128)(2,1)}, bf16[17,2,32,128]{3,2,1,0:T(8,128)(2,1)S(1)}, u32[]{:S(2)}, u32[]{:S(2)}) %collective-permute-start.6) | collective-permute-done | bytes 278560 | tf_op jit(solution)/shard_map/ppermute | solution.py:398
  31.6 0.0 copy-start.6
  31.6 0.0 copy-done.4
  31.6 0.0 copy-done.5
  31.6 0.7 %copy-done.6 = bf16[17,2,32,128]{3,2,1,0:T(8,128)(2,1)} copy-done((bf16[17,2,32,128]{3,2,1,0:T(8,128)(2,1)}, bf16[17,2,32,128]{3,2,1,0:T(8,128)(2,1)S(1)}, u32[]{:S(2)}) %copy-start.6) | copy-done | bytes 278552
  32.3 9.0 %link.2.refs_8_ = f32[2,96,128]{2,1,0:T(8,128)} custom-call(bf16[17,2,32,128]{3,2,1,0:T(8,128)(2,1)} %get-tuple-element.21.refs_0_.refs_4_, bf16[17,2,32,128]{3,2,1,0:T(8,128)(2,1)} %copy-done.4, bf16[17,2,32,128]{3,2,1,0:T(8,128)(2,1)} %copy-done.5, bf16[17,2,32,128]{3,2,1,0:T(8,128)(2,1)} %copy-done.6), custom_call_target="tpu_custom_call" | custom-call | flops 2880000000 | bytes 1000000 | tf_op jit(solution)/shard_map/link/pallas_call | solution.py:374
  41.3 0.0 collective-permute-done.1.refs_1_
  41.3 0.0 copy-start.7
  41.3 0.0 collective-permute-done.2.refs_2_
  41.3 0.0 copy-start.8
  41.3 0.0 collective-permute-done.3.refs_3_
  41.3 0.0 copy-start.9
  41.4 0.6 %copy-done.7 = bf16[15,2,32,128]{3,2,1,0:T(8,128)(2,1)} copy-done((bf16[15,2,32,128]{3,2,1,0:T(8,128)(2,1)}, bf16[15,2,32,128]{3,2,1,0:T(8,128)(2,1)S(1)}, u32[]{:S(2)}) %copy-start.7) | copy-done | bytes 245784
  42.0 0.1 copy-done.8
  42.1 0.1 copy-done.9
  42.2 10.1 %link.3 = (f32[2,32,192]{2,1,0:T(8,128)}, f32[2,32,192]{2,1,0:T(8,128)}, f32[2,32,192]{2,1,0:T(8,128)}, f32[2,32,192]{2,1,0:T(8,128)}) custom-call(bf16[15,2,32,128]{3,2,1,0:T(8,128)(2,1)} %get-tuple-element.17.refs_0_, bf16[15,2,32,128]{3,2,1,0:T(8,128)(2,1)} %copy-done.7, bf16[15,2,32,128]{3,2,1,0:T(8,128)(2,1)} %copy-done.8, ...), custom_call_target="tpu_custom_call" | custom-call | flops 2880000000 | bytes 1000000 | tf_op jit(solution)/shard_map/link/pallas_call | solution.py:374
  52.2 1.6 %collective-permute-start.7 = (f32[2,32,192]{2,1,0:T(8,128)}, f32[2,32,192]{2,1,0:T(8,128)S(1)}, u32[]{:S(2)}, u32[]{:S(2)}) collective-permute-start(f32[2,32,192]{2,1,0:T(8,128)} %get-tuple-element.26), channel_id=1, source_target_pairs={{0,8},{8,0},{16,24},{24,16},{1,9},{9,1},{17,25},{25,17},{2,10},{10... | collective-permute-start | bytes 147464 | tf_op jit(solution)/shard_map/ppermute | solution.py:398
  53.8 0.5 collective-permute-start.8
  54.3 1.5 %collective-permute-start.9 = (f32[2,32,192]{2,1,0:T(8,128)}, f32[2,32,192]{2,1,0:T(8,128)S(1)}, u32[]{:S(2)}, u32[]{:S(2)}) collective-permute-start(f32[2,32,192]{2,1,0:T(8,128)} %get-tuple-element.28), channel_id=1, source_target_pairs={{0,24},{8,16},{16,8},{24,0},{1,25},{9,17},{17,9},{25,1},{2,26},{10... | collective-permute-start | bytes 147464 | tf_op jit(solution)/shard_map/ppermute | solution.py:398
  55.8 1.0 %collective-permute-done.7.refs_1_ = f32[2,32,192]{2,1,0:T(8,128)S(1)} collective-permute-done((f32[2,32,192]{2,1,0:T(8,128)}, f32[2,32,192]{2,1,0:T(8,128)S(1)}, u32[]{:S(2)}, u32[]{:S(2)}) %collective-permute-start.7) | collective-permute-done | bytes 49184 | tf_op jit(solution)/shard_map/ppermute | solution.py:398
  56.8 0.0 copy-start.1
  56.8 1.5 %collective-permute-done.8.refs_2_ = f32[2,32,192]{2,1,0:T(8,128)S(1)} collective-permute-done((f32[2,32,192]{2,1,0:T(8,128)}, f32[2,32,192]{2,1,0:T(8,128)S(1)}, u32[]{:S(2)}, u32[]{:S(2)}) %collective-permute-start.8) | collective-permute-done | bytes 49184 | tf_op jit(solution)/shard_map/ppermute | solution.py:398
  58.3 0.0 copy-start.2
  58.3 1.4 %collective-permute-done.9.refs_3_ = f32[2,32,192]{2,1,0:T(8,128)S(1)} collective-permute-done((f32[2,32,192]{2,1,0:T(8,128)}, f32[2,32,192]{2,1,0:T(8,128)S(1)}, u32[]{:S(2)}, u32[]{:S(2)}) %collective-permute-start.9) | collective-permute-done | bytes 49184 | tf_op jit(solution)/shard_map/ppermute | solution.py:398
  59.7 0.0 copy-start.3
  59.7 0.0 copy-done.1
  59.7 0.0 copy-done.2
  59.7 0.6 copy-done.3
  60.3 1.7 %place.1 = f32[2,32,4,192]{3,2,1,0:T(4,128)} custom-call(f32[2,32,192]{2,1,0:T(8,128)} %get-tuple-element.25.refs_0_, f32[2,32,192]{2,1,0:T(8,128)} %copy-done.1, f32[2,32,192]{2,1,0:T(8,128)} %copy-done.2, f32[2,32,192]{2,1,0:T(8,128)} %copy-done.3), custom_call_target="tpu_custom_call" | custom-call | tf_op jit(solution)/shard_map/place/pallas_call | solution.py:417
Async XLA Ops:
  2.2 7.7 %collective-permute-start = (bf16[3,2,32,640]{3,2,1,0:T(8,128)(2,1)}, bf16[3,2,32,640]{3,2,1,0:T(8,128)(2,1)S(1)}, u32[]{:S(2)}, u32[]{:S(2)}) collective-permute-start(bf16[3,2,32,640]{3,2,1,0:T(8,128)(2,1)} %edge.1), channel_id=1, source_target_pairs={{0,1},{1,2},{2,3},{3,4},{4,5},{5,6},{6,7},{8,9},{9,10},{10,11},{11... | collective-permute-start | bytes 737288 | tf_op jit(solution)/shard_map/ppermute | solution.py:443
  9.9 0.7 %copy-start = (bf16[3,2,32,640]{3,2,1,0:T(8,128)(2,1)}, bf16[3,2,32,640]{3,2,1,0:T(8,128)(2,1)S(1)}, u32[]{:S(2)}) copy-start(bf16[3,2,32,640]{3,2,1,0:T(8,128)(2,1)S(1)} %collective-permute-done.refs_6_) | copy-start | bytes 737284
  14.8 10.7 %collective-permute-start.4 = (bf16[17,2,32,128]{3,2,1,0:T(8,128)(2,1)}, bf16[17,2,32,128]{3,2,1,0:T(8,128)(2,1)S(1)}, u32[]{:S(2)}, u32[]{:S(2)}) collective-permute-start(bf16[17,2,32,128]{3,2,1,0:T(8,128)(2,1)} %get-tuple-element.22), channel_id=1, source_target_pairs={{0,8},{8,0},{16,24},{24,16},{1,9},{9,1},{17,25},{25,17},{2,10},{10... | collective-permute-start | bytes 835592 | tf_op jit(solution)/shard_map/ppermute | solution.py:398
  16.3 13.9 %collective-permute-start.5 = (bf16[17,2,32,128]{3,2,1,0:T(8,128)(2,1)}, bf16[17,2,32,128]{3,2,1,0:T(8,128)(2,1)S(1)}, u32[]{:S(2)}, u32[]{:S(2)}) collective-permute-start(bf16[17,2,32,128]{3,2,1,0:T(8,128)(2,1)} %get-tuple-element.23), channel_id=1, source_target_pairs={{0,16},{8,24},{16,0},{24,8},{1,17},{9,25},{17,1},{25,9},{2,18},{10... | collective-permute-start | bytes 835592 | tf_op jit(solution)/shard_map/ppermute | solution.py:398
  17.8 13.8 %collective-permute-start.6 = (bf16[17,2,32,128]{3,2,1,0:T(8,128)(2,1)}, bf16[17,2,32,128]{3,2,1,0:T(8,128)(2,1)S(1)}, u32[]{:S(2)}, u32[]{:S(2)}) collective-permute-start(bf16[17,2,32,128]{3,2,1,0:T(8,128)(2,1)} %get-tuple-element.24), channel_id=1, source_target_pairs={{0,24},{8,16},{16,8},{24,0},{1,25},{9,17},{17,9},{25,1},{2,26},{10... | collective-permute-start | bytes 835592 | tf_op jit(solution)/shard_map/ppermute | solution.py:398
  22.3 19.0 %collective-permute-start.1 = (bf16[15,2,32,128]{3,2,1,0:T(8,128)(2,1)}, bf16[15,2,32,128]{3,2,1,0:T(8,128)(2,1)S(1)}, u32[]{:S(2)}, u32[]{:S(2)}) collective-permute-start(bf16[15,2,32,128]{3,2,1,0:T(8,128)(2,1)} %get-tuple-element.18), channel_id=1, source_target_pairs={{0,8},{8,0},{16,24},{24,16},{1,9},{9,1},{17,25},{25,17},{2,10},{10... | collective-permute-start | bytes 737288 | tf_op jit(solution)/shard_map/ppermute | solution.py:398
  23.9 17.4 %collective-permute-start.2 = (bf16[15,2,32,128]{3,2,1,0:T(8,128)(2,1)}, bf16[15,2,32,128]{3,2,1,0:T(8,128)(2,1)S(1)}, u32[]{:S(2)}, u32[]{:S(2)}) collective-permute-start(bf16[15,2,32,128]{3,2,1,0:T(8,128)(2,1)} %get-tuple-element.19), channel_id=1, source_target_pairs={{0,16},{8,24},{16,0},{24,8},{1,17},{9,25},{17,1},{25,9},{2,18},{10... | collective-permute-start | bytes 737288 | tf_op jit(solution)/shard_map/ppermute | solution.py:398
  25.4 6.2 %copy-start.4 = (bf16[17,2,32,128]{3,2,1,0:T(8,128)(2,1)}, bf16[17,2,32,128]{3,2,1,0:T(8,128)(2,1)S(1)}, u32[]{:S(2)}) copy-start(bf16[17,2,32,128]{3,2,1,0:T(8,128)(2,1)S(1)} %collective-permute-done.4.refs_1_.refs_5_) | copy-start | bytes 835588
  25.4 15.9 %collective-permute-start.3 = (bf16[15,2,32,128]{3,2,1,0:T(8,128)(2,1)}, bf16[15,2,32,128]{3,2,1,0:T(8,128)(2,1)S(1)}, u32[]{:S(2)}, u32[]{:S(2)}) collective-permute-start(bf16[15,2,32,128]{3,2,1,0:T(8,128)(2,1)} %get-tuple-element.20), channel_id=1, source_target_pairs={{0,24},{8,16},{16,8},{24,0},{1,25},{9,17},{17,9},{25,1},{2,26},{10... | collective-permute-start | bytes 737288 | tf_op jit(solution)/shard_map/ppermute | solution.py:398
  30.2 1.4 %copy-start.5 = (bf16[17,2,32,128]{3,2,1,0:T(8,128)(2,1)}, bf16[17,2,32,128]{3,2,1,0:T(8,128)(2,1)S(1)}, u32[]{:S(2)}) copy-start(bf16[17,2,32,128]{3,2,1,0:T(8,128)(2,1)S(1)} %collective-permute-done.5.refs_2_.refs_6_) | copy-start | bytes 835588
  31.6 0.7 %copy-start.6 = (bf16[17,2,32,128]{3,2,1,0:T(8,128)(2,1)}, bf16[17,2,32,128]{3,2,1,0:T(8,128)(2,1)S(1)}, u32[]{:S(2)}) copy-start(bf16[17,2,32,128]{3,2,1,0:T(8,128)(2,1)S(1)} %collective-permute-done.6.refs_3_.refs_7_) | copy-start | bytes 835588
  41.3 0.7 %copy-start.7 = (bf16[15,2,32,128]{3,2,1,0:T(8,128)(2,1)}, bf16[15,2,32,128]{3,2,1,0:T(8,128)(2,1)S(1)}, u32[]{:S(2)}) copy-start(bf16[15,2,32,128]{3,2,1,0:T(8,128)(2,1)S(1)} %collective-permute-done.1.refs_1_) | copy-start | bytes 737284
  41.3 0.7 %copy-start.8 = (bf16[15,2,32,128]{3,2,1,0:T(8,128)(2,1)}, bf16[15,2,32,128]{3,2,1,0:T(8,128)(2,1)S(1)}, u32[]{:S(2)}) copy-start(bf16[15,2,32,128]{3,2,1,0:T(8,128)(2,1)S(1)} %collective-permute-done.2.refs_2_) | copy-start | bytes 737284
  41.3 0.8 %copy-start.9 = (bf16[15,2,32,128]{3,2,1,0:T(8,128)(2,1)}, bf16[15,2,32,128]{3,2,1,0:T(8,128)(2,1)S(1)}, u32[]{:S(2)}) copy-start(bf16[15,2,32,128]{3,2,1,0:T(8,128)(2,1)S(1)} %collective-permute-done.3.refs_3_) | copy-start | bytes 737284
  52.2 4.5 %collective-permute-start.7 = (f32[2,32,192]{2,1,0:T(8,128)}, f32[2,32,192]{2,1,0:T(8,128)S(1)}, u32[]{:S(2)}, u32[]{:S(2)}) collective-permute-start(f32[2,32,192]{2,1,0:T(8,128)} %get-tuple-element.26), channel_id=1, source_target_pairs={{0,8},{8,0},{16,24},{24,16},{1,9},{9,1},{17,25},{25,17},{2,10},{10... | collective-permute-start | bytes 147464 | tf_op jit(solution)/shard_map/ppermute | solution.py:398
  53.8 4.5 %collective-permute-start.8 = (f32[2,32,192]{2,1,0:T(8,128)}, f32[2,32,192]{2,1,0:T(8,128)S(1)}, u32[]{:S(2)}, u32[]{:S(2)}) collective-permute-start(f32[2,32,192]{2,1,0:T(8,128)} %get-tuple-element.27), channel_id=1, source_target_pairs={{0,16},{8,24},{16,0},{24,8},{1,17},{9,25},{17,1},{25,9},{2,18},{10... | collective-permute-start | bytes 147464 | tf_op jit(solution)/shard_map/ppermute | solution.py:398
  54.3 5.4 %collective-permute-start.9 = (f32[2,32,192]{2,1,0:T(8,128)}, f32[2,32,192]{2,1,0:T(8,128)S(1)}, u32[]{:S(2)}, u32[]{:S(2)}) collective-permute-start(f32[2,32,192]{2,1,0:T(8,128)} %get-tuple-element.28), channel_id=1, source_target_pairs={{0,24},{8,16},{16,8},{24,0},{1,25},{9,17},{17,9},{25,1},{2,26},{10... | collective-permute-start | bytes 147464 | tf_op jit(solution)/shard_map/ppermute | solution.py:398
  56.8 2.9 %copy-start.1 = (f32[2,32,192]{2,1,0:T(8,128)}, f32[2,32,192]{2,1,0:T(8,128)S(1)}, u32[]{:S(2)}) copy-start(f32[2,32,192]{2,1,0:T(8,128)S(1)} %collective-permute-done.7.refs_1_) | copy-start | bytes 147460
  58.3 1.4 %copy-start.2 = (f32[2,32,192]{2,1,0:T(8,128)}, f32[2,32,192]{2,1,0:T(8,128)S(1)}, u32[]{:S(2)}) copy-start(f32[2,32,192]{2,1,0:T(8,128)S(1)} %collective-permute-done.8.refs_2_) | copy-start | bytes 147460
  59.7 0.6 %copy-start.3 = (f32[2,32,192]{2,1,0:T(8,128)}, f32[2,32,192]{2,1,0:T(8,128)S(1)}, u32[]{:S(2)}) copy-start(f32[2,32,192]{2,1,0:T(8,128)S(1)} %collective-permute-done.9.refs_3_) | copy-start | bytes 147460

commit v3 on v2

--- a/solution.py
+++ b/solution.py
@@ -80,21 +80,65 @@
         ],
         out_specs=pl.BlockSpec(shape.shape, lambda i: (0, 0, 0, 0)),
         scratch_shapes=[pltpu.VMEM((parts, blocks, dates * 9, LANES), jnp.float32)],
-        compiler_params=pltpu.CompilerParams(vmem_limit_bytes=56 << 20),
+        compiler_params=pltpu.CompilerParams(vmem_limit_bytes=16 << 20),
         name="edge",
     )(acquisitions, valid_dates)
 
 
-def pack_kernel(tiles, first_block, blocks, col_groups, segments, axis, *refs):
+def turn(plane, j):
+    return pltpu.roll(plane, TILE_ROWS * j, 1) if j else plane
+
+
+def edge_planes(halo, first_block, blocks, keep):
+    for block in range(blocks):
+        at = (first_block + block) * LANES
+        for j in range(LEFT):
+            for part in range(halo.shape[1]):
+                plane = halo[j, part, :, at : at + LANES].astype(jnp.float32)
+                keep(block, j, part, turn(plane, j).astype(jnp.bfloat16))
+
+
+def compose(total, tile, columns, piece, masks):
+    for j in columns:
+        row, end = tile * TILE_ROWS, (tile + 1) * TILE_ROWS
+        while row < end:
+            block = row // LANES
+            stop = min(end, (block + 1) * LANES)
+            key = ((row + TILE_ROWS * j) % LANES, stop - row)
+            if key not in masks:
+                masks[key] = lane_mask(*key)
+            total = choose(masks[key], piece(block, j).reshape(total.shape), total)
+            row = stop
+    return total
+
+
+def compose_at(total, tile, last, columns, piece):
+    kept = jnp.where((tile >= 0) & (tile <= last), TILE_ROWS, 0)
+    row = jnp.clip(tile, 0, last) * TILE_ROWS
+    low, high = row // LANES, (row + TILE_ROWS - 1) // LANES
+    split = jnp.where(high == low, TILE_ROWS, high * LANES - row)
+    for j in columns:
+        start = row + TILE_ROWS * j
+        for block, first, count in (
+            (low, start, jnp.minimum(split, kept)),
+            (high, start + split, jnp.minimum(TILE_ROWS - split, kept)),
+        ):
+            total = choose(lane_mask(first, count), piece(block, j).reshape(total.shape), total)
+    return total
+
+
+def pack_kernel(ends, first_block, blocks, col_groups, segments, with_halo, *refs):
     acq_refs, refs = refs[:blocks], refs[blocks:]
     valid_refs, refs = refs[:blocks], refs[blocks:]
-    halo_ref, refs = refs[0], refs[1:]
-    outs, (planes, shifted, halo, sem) = refs[:-4], refs[-4:]
+    if with_halo:
+        halo_ref, refs = refs[0], refs[1:]
+        refs, (halo, sem) = refs[:-2], refs[-2:]
+        fetch = pltpu.make_async_copy(halo_ref, halo, sem)
+        fetch.start()
+    outs, (planes, shifted) = refs[:-2], refs[-2:]
     parts, dates, cols, _ = acq_refs[0].shape
-    stride = cols + LEFT
-    me = lax.axis_index(axis)
-    fetch = pltpu.make_async_copy(halo_ref, halo, sem)
-    fetch.start()
+    stride = planes.shape[2] // dates
+    me = lax.axis_index("date")
 
     def one_date(date, carry):
         for block in range(blocks):
@@ -106,11 +150,6 @@
 
     lax.fori_loop(0, dates, one_date, 0, unroll=4)
 
-    def place(group, block, j, part, plane):
-        if j:
-            plane = pltpu.roll(plane, TILE_ROWS * j, 1)
-        shifted[group, block, j, part] = plane.astype(jnp.bfloat16)
-
     def one_block(block, carry):
         for group in range(col_groups):
             for j in range(BOX_COLS):
@@ -118,68 +157,59 @@
                 for part in range(parts):
                     if column >= 0:
                         plane = planes[part, block, pl.ds(column, dates, stride=stride), :]
-                        place(group, block, j, part, plane)
+                        shifted[group, block, j, part] = turn(plane, j).astype(jnp.bfloat16)
         return carry
 
     lax.fori_loop(0, blocks, one_block, 0)
-    fetch.wait()
-    for block in range(blocks):
-        at = (first_block + block) * LANES
-        for j in range(LEFT):
-            for part in range(parts):
-                place(0, block, j, part, halo[j, part, :, at : at + LANES].astype(jnp.float32))
+
+    def keep_edge(block, j, part, plane):
+        shifted[0, block, j, part] = plane
+
+    if with_halo:
+        fetch.wait()
+        edge_planes(halo, first_block, blocks, keep_edge)
+    else:
+        zero = jnp.zeros((dates, LANES), jnp.bfloat16)
+        for block in range(blocks):
+            for j in range(LEFT):
+                for part in range(parts):
+                    keep_edge(block, j, part, zero)
     masks = {}
-    for offset, out in enumerate(outs):
+    chunks = len(ends) - 1
+    empty = jnp.zeros((parts * dates // 16, 16, LANES), jnp.bfloat16)
+    for offset in range(len(outs) // chunks):
+        mine = outs[offset * chunks : (offset + 1) * chunks]
         target = me ^ offset
         group = lax.rem(target, col_groups)
+
+        def piece(block, j):
+            return shifted[group, block - first_block, j]
+
         if segments == 1:
-            for index, tile in enumerate(tiles):
-                total = jnp.zeros((parts * dates // 16, 16, LANES), jnp.bfloat16)
-                for j in range(BOX_COLS):
-                    row, end = tile * TILE_ROWS, (tile + 1) * TILE_ROWS
-                    while row < end:
-                        block = row // LANES
-                        stop = min(end, (block + 1) * LANES)
-                        key = ((row + TILE_ROWS * j) % LANES, stop - row)
-                        if key not in masks:
-                            masks[key] = lane_mask(*key)
-                        piece = shifted[group, block - first_block, j]
-                        total = choose(masks[key], piece.reshape(total.shape), total)
-                        row = stop
-                out[index] = total.reshape(parts, dates, LANES)
+            for tile in range(ends[0], ends[-1]):
+                chunk = sum(tile >= end for end in ends[1:])
+                total = compose(empty, tile, range(BOX_COLS), piece, masks)
+                mine[chunk][tile - ends[chunk]] = total.reshape(parts, dates, LANES)
         else:
-            segment = target // col_groups
-            last = segments * len(tiles) - 1
+            tiles, segment = ends[-1], target // col_groups
 
             def one_tile(index, carry):
-                tile = segment * len(tiles) + index - 1
-                kept = jnp.where((tile >= 0) & (tile <= last), TILE_ROWS, 0)
-                row = jnp.clip(tile, 0, last) * TILE_ROWS
-                low, high = row // LANES, (row + TILE_ROWS - 1) // LANES
-                split = jnp.where(high == low, TILE_ROWS, high * LANES - row)
-                total = jnp.zeros((parts * dates // 16, 16, LANES), jnp.bfloat16)
-                for j in range(BOX_COLS):
-                    start = row + TILE_ROWS * j
-                    for block, first, count in (
-                        (low, start, jnp.minimum(split, kept)),
-                        (high, start + split, jnp.minimum(TILE_ROWS - split, kept)),
-                    ):
-                        piece = shifted[group, block, j].reshape(total.shape)
-                        total = choose(lane_mask(first, count), piece, total)
-                out[index] = total.reshape(parts, dates, LANES)
+                tile, last = segment * tiles + index - 1, segments * tiles - 1
+                total = compose_at(empty, tile, last, range(BOX_COLS), piece)
+                mine[0][index] = total.reshape(parts, dates, LANES)
                 return carry
 
-            lax.fori_loop(0, len(tiles) + 2, one_tile, 0)
-
-
-def pack(acquisitions, valid_dates, halo, peers, tiles, col_groups, segments):
+            lax.fori_loop(0, tiles + 2, one_tile, 0)
+
+
+def pack(acquisitions, valid_dates, halo, peers, ends, col_groups, segments):
     parts, dates, cols, rows = acquisitions.shape
     if segments == 1:
-        sent = len(tiles)
-        first = tiles[0] * TILE_ROWS // LANES
-        blocks = -(-(tiles[-1] + 1) * TILE_ROWS // LANES) - first
+        sent = [high - low for low, high in zip(ends, ends[1:])]
+        first = ends[0] * TILE_ROWS // LANES
+        blocks = -(-ends[-1] * TILE_ROWS // LANES) - first
     else:
-        sent, first, blocks = len(tiles) + 2, 0, -(-rows // LANES)
+        sent, first, blocks = [ends[-1] + 2], 0, -(-rows // LANES)
 
     def block_specs(shape):
         return [
@@ -189,28 +219,109 @@
             for k in range(blocks)
         ]
 
-    shape = jax.ShapeDtypeStruct((sent, parts, dates, LANES), jnp.bfloat16)
-    kernel = functools.partial(pack_kernel, tiles, first, blocks, col_groups, segments, "date")
-    return pl.pallas_call(
-        kernel,
+    chunks = len(sent)
+    shapes = [jax.ShapeDtypeStruct((n, parts, dates, LANES), jnp.bfloat16) for n in sent]
+    operands = [acquisitions] * blocks + [valid_dates] * blocks
+    specs = block_specs((parts, dates, cols)) + block_specs((dates, cols))
+    scratch = [
+        pltpu.VMEM((parts, blocks, dates * (cols + 1), LANES), jnp.float32),
+        pltpu.VMEM((col_groups, blocks, BOX_COLS, parts, dates, LANES), jnp.bfloat16),
+    ]
+    if halo is not None:
+        operands.append(halo)
+        specs.append(pl.BlockSpec(memory_space=pl.ANY))
+        scratch += [pltpu.VMEM(halo.shape, halo.dtype), pltpu.SemaphoreType.DMA]
+    outs = pl.pallas_call(
+        functools.partial(
+            pack_kernel, ends, first, blocks, col_groups, segments, halo is not None
+        ),
         grid=(1,),
-        out_shape=[shape] * peers,
-        in_specs=block_specs((parts, dates, cols))
-        + block_specs((dates, cols))
-        + [pl.BlockSpec(memory_space=pl.ANY)],
-        out_specs=[pl.BlockSpec(shape.shape, lambda i: (0, 0, 0, 0))] * peers,
-        scratch_shapes=[
-            pltpu.VMEM((parts, blocks, dates * (cols + LEFT), LANES), jnp.float32),
-            pltpu.VMEM((col_groups, blocks, BOX_COLS, parts, dates, LANES), jnp.bfloat16),
-            pltpu.VMEM(halo.shape, halo.dtype),
-            pltpu.SemaphoreType.DMA,
-        ],
-        compiler_params=pltpu.CompilerParams(vmem_limit_bytes=56 << 20),
+        out_shape=shapes * peers,
+        in_specs=specs,
+        out_specs=[pl.BlockSpec(memory_space=pltpu.VMEM)] * (peers * chunks),
+        scratch_shapes=scratch,
+        compiler_params=pltpu.CompilerParams(vmem_limit_bytes=36 << 20),
         cost_estimate=pl.CostEstimate(
             flops=10**8, bytes_accessed=blocks * 3 * 10**6, transcendentals=0
         ),
         name="pack",
-    )(*[acquisitions] * blocks, *[valid_dates] * blocks, halo)
+    )(*operands)
+    return [list(outs[chunk::chunks]) for chunk in range(chunks)]
+
+
+def patch_kernel(tiles, col_groups, segments, *refs):
+    halo_ref, refs = refs[0], refs[1:]
+    peers = (len(refs) - 4) // 2
+    outs, (halo, planes, held, sems) = refs[peers:-4], refs[-4:]
+    sent, parts, dates, _ = held.shape
+    blocks = planes.shape[0]
+    me = lax.axis_index("date")
+    fetch = pltpu.make_async_copy(halo_ref, halo, sems.at[0])
+    fetch.start()
+    shape = (parts * dates // 16, 16, LANES)
+
+    def keep_edge(block, j, part, plane):
+        planes[block, j, part] = plane
+
+    def piece(block, j):
+        return planes[block, j]
+
+    for offset, out in enumerate(outs):
+        target = me ^ offset
+
+        @pl.when(lax.rem(target, col_groups) == 0)
+        def _(out=out, target=target):
+            read = pltpu.make_async_copy(out, held, sems.at[1])
+            read.start()
+            if offset < col_groups:
+                fetch.wait()
+                edge_planes(halo, 0, blocks, keep_edge)
+            read.wait()
+            masks = {}
+            if segments == 1:
+                for tile in range(tiles):
+                    total = held[tile].reshape(shape)
+                    total = compose(total, tile, range(LEFT), piece, masks)
+                    held[tile] = total.reshape(held.shape[1:])
+            else:
+                segment = target // col_groups
+
+                def one_tile(index, carry):
+                    tile, last = segment * tiles + index - 1, segments * tiles - 1
+                    total = held[index].reshape(shape)
+                    total = compose_at(total, tile, last, range(LEFT), piece)
+                    held[index] = total.reshape(held.shape[1:])
+                    return carry
+
+                lax.fori_loop(0, sent, one_tile, 0)
+            write = pltpu.make_async_copy(held, out, sems.at[2])
+            write.start()
+            write.wait()
+
+
+def patch(blocks, halo, tiles, col_groups, segments):
+    peers = len(blocks)
+    _, parts, dates, _ = blocks[0].shape
+    if segments == 1:
+        lanes = -(-tiles * TILE_ROWS // LANES)
+    else:
+        lanes = halo.shape[3] // LANES
+    anywhere = pl.BlockSpec(memory_space=pl.ANY)
+    return pl.pallas_call(
+        functools.partial(patch_kernel, tiles, col_groups, segments),
+        out_shape=[jax.ShapeDtypeStruct(block.shape, block.dtype) for block in blocks],
+        in_specs=[anywhere] * (1 + peers),
+        out_specs=[anywhere] * peers,
+        scratch_shapes=[
+            pltpu.VMEM(halo.shape, halo.dtype),
+            pltpu.VMEM((lanes, LEFT, parts, dates, LANES), jnp.bfloat16),
+            pltpu.VMEM(blocks[0].shape, jnp.bfloat16),
+            pltpu.SemaphoreType.DMA((3,)),
+        ],
+        input_output_aliases={1 + m: m for m in range(peers)},
+        compiler_params=pltpu.CompilerParams(vmem_limit_bytes=16 << 20),
+        name="patch",
+    )(halo, *blocks)
 
 
 def slot_rows(first):
@@ -314,7 +425,7 @@
             tiles[base + sent] = zero
     for copy in copies:
         copy.wait()
-    pixels = linked.shape[0] // 8
+    pixels = linked.shape[1]
     batch = math.gcd(BATCH, pixels)
     diagonal = lax.broadcasted_iota(
         jnp.int32, (all_dates, all_dates), 0
@@ -338,12 +449,13 @@
             a, b, both = window_pair(real, imag, at, e, rows_at(k)[0], rows_at(k + 1)[1])
             coherence_pair(a, b, both, diagonal, held, place)
         for place, tile in enumerate(iterate(held, batch, all_dates)):
-            linked[pl.ds((index * batch + place) * 8, 8)] = tile
+            for part in range(2):
+                linked[part, pl.ds(index * batch + place, 1)] = tile[part : part + 1]
         return carry
 
     lax.fori_loop(0, pixels // batch, step, 0)
     for part in range(2):
-        vectors = linked[pl.ds(part, pixels, stride=8), :]
+        vectors = linked[part]
         if not last:
             outs[0][part] = vectors
             continue
@@ -381,10 +493,10 @@
             pltpu.VMEM((kept, all_dates, LANES), jnp.bfloat16),
             pltpu.VMEM((kept, all_dates, LANES), jnp.bfloat16),
             pltpu.VMEM((math.gcd(BATCH, pixels), 2 * all_dates, all_dates), jnp.bfloat16),
-            pltpu.VMEM((pixels * 8, all_dates), jnp.float32),
+            pltpu.VMEM((2, pixels, all_dates), jnp.float32),
             pltpu.SemaphoreType.DMA((4 * peers,)),
         ],
-        compiler_params=pltpu.CompilerParams(vmem_limit_bytes=56 << 20),
+        compiler_params=pltpu.CompilerParams(vmem_limit_bytes=20 << 20),
         cost_estimate=pl.CostEstimate(
             flops=pixels * 30 * 10**6, bytes_accessed=10**6, transcendentals=0
         ),
@@ -419,7 +531,7 @@
         out_shape=jax.ShapeDtypeStruct((parts, dates, out_cols, rows * segments), jnp.float32),
         in_specs=[whole] * len(blocks),
         out_specs=whole,
-        compiler_params=pltpu.CompilerParams(vmem_limit_bytes=56 << 20),
+        compiler_params=pltpu.CompilerParams(vmem_limit_bytes=8 << 20),
         name="place",
     )(*blocks)
 
@@ -444,10 +556,11 @@
         edge(acquisitions, valid_dates), "space", [(i, i + 1) for i in range(strips - 1)]
     )
     ends = chunk_ends(tiles, segments)
-    outgoing = [
-        pack(acquisitions, valid_dates, halo, peers, range(low, high), out_cols, segments)
-        for low, high in zip([0] + ends[:-1], ends)
-    ]
+    first, *rest = ends
+    (blocks,) = pack(acquisitions, valid_dates, None, peers, [0, first], out_cols, segments)
+    outgoing = [patch(blocks, halo, first, out_cols, segments)]
+    if rest:
+        outgoing += pack(acquisitions, valid_dates, halo, peers, ends, out_cols, segments)
     incoming = [swap(blocks, "date") for blocks in outgoing]
     done, start = [], 0
     for index, blocks in enumerate(incoming):

time: 62.5 us -> 53.3 us (0.85)
  Pallas kernels: 31.1 us -> 20.4 us
  starting transfers between devices: 13.7 us -> 14.8 us
    pallas_call x2, Pallas kernels: 19 us -> 14.6 us  [link(): pl.pallas_call(kernel, grid=(1,), out_shape=outs, in_specs=specs, out_spe...]
    pallas_call x2 -> x3, Pallas kernels: 8.16 us -> 4.68 us  [the longest x2 3.86 us: pack(): pl.pallas_call(functools.partial(pack_kernel, ends, first, blocks, col_gr...]
    ppermute x9, waiting for transfers between devices: 8.41 us -> 10.9 us  [swap(): lax.ppermute(blocks[m], axis, [(i, i ^ m) for i in range(count)])]
    ppermute x1, waiting for transfers between devices: 5.8 us -> 3.78 us  [on_device(): lax.ppermute(edge(acquisitions, valid_dates), 'space', [(i, i + 1) for i...]
    pallas_call x1, Pallas kernels: 2.2 us -> 0.3 us  [edge(): pl.pallas_call(functools.partial(edge_kernel, cols - LEFT - at * 16), gri...]
    pallas_call x1, Pallas kernels: 1.75 us -> 0.81 us  [place_blocks(): pl.pallas_call(functools.partial(place_kernel, len(blocks), out_cols), ou...]
    ppermute x9, starting transfers between devices: 11.8 us -> 12.6 us  [swap(): lax.ppermute(blocks[m], axis, [(i, i ^ m) for i in range(count)])]
    unnamed x20 -> x8, local copies, waits for them, and re-layouts: 2.85 us -> 3.1 us
  transfers between devices with their start and end apart: 10 -> 10, of which waited for: 6 -> 8; matrix products, arithmetic and copies ran while one was open for 0% -> 0% of each run, Pallas kernels for 21% -> 21%
where the time goes in v3:
time: 53.3 us; the launch traced here: 53.1 us
  Pallas kernels  20.4 us (38%)
  starting transfers between devices  14.8 us (28%)
  waiting for transfers between devices  14.7 us (28%)
  local copies, waits for them, and re-layouts  3.1 us (6%)
    pallas_call x2, Pallas kernels, link(): pl.pallas_call(kernel, grid=(1,), out_shape=outs, in_specs=specs, out_spe...  14.6 us
    ppermute x9, starting transfers between devices, swap(): lax.ppermute(blocks[m], axis, [(i, i ^ m) for i in range(count)])  12.6 us
    ppermute x9, waiting for transfers between devices, swap(): lax.ppermute(blocks[m], axis, [(i, i ^ m) for i in range(count)])  10.9 us
    pallas_call x2, Pallas kernels, pack(): pl.pallas_call(functools.partial(pack_kernel, ends, first, blocks, col_gr...  3.86 us
    ppermute x1, waiting for transfers between devices, on_device(): lax.ppermute(edge(acquisitions, valid_dates), 'space', [(i, i + 1) for i...  3.78 us
    unnamed x8, local copies, waits for them, and re-layouts  3.1 us
    ppermute x1, starting transfers between devices, on_device(): lax.ppermute(edge(acquisitions, valid_dates), 'space', [(i, i + 1) for i...  2.18 us
  transfers between devices with their start and end apart: 10, of which 8 were waited for; matrix products, arithmetic and copies ran while one was open for 0% of the time, Pallas kernels for 21%

profile of v3, /device:TPU:16, one launch (start us, length us, event | category | flops | bytes accessed | tf_op | source)
XLA Modules:
  0.0 53.1 jit_solution(5100525116454250933)
XLA Ops:
  0.0 0.0 copy-start
  0.0 1.5 %copy-done = bf16[2,32,24,576]{3,2,1,0:T(8,128)(2,1)S(1)} copy-done((bf16[2,32,24,576]{3,2,1,0:T(8,128)(2,1)S(1)}, bf16[2,32,24,576]{3,2,1,0:T(8,128)(2,1)}, u32[]{:S(2)}) %copy-start) | copy-done | bytes 1769496
  1.5 0.0 copy-start.2
  1.5 1.5 %copy-done.2 = s32[32,24,576]{2,1,0:T(8,128)S(1)} copy-done((s32[32,24,576]{2,1,0:T(8,128)S(1)}, s32[32,24,576]{2,1,0:T(8,128)}, u32[]{:S(2)}) %copy-start.2) | copy-done | bytes 1769496
  3.1 0.0 copy-start.1
  3.1 0.0 copy-start.3
  3.1 0.3 edge.1
  3.4 2.2 %collective-permute-start = (bf16[3,2,32,640]{3,2,1,0:T(8,128)(2,1)S(1)}, bf16[3,2,32,640]{3,2,1,0:T(8,128)(2,1)S(1)}, u32[]{:S(2)}, u32[]{:S(2)}) collective-permute-start(bf16[3,2,32,640]{3,2,1,0:T(8,128)(2,1)S(1)} %edge.1), channel_id=1, source_target_pairs={{0,1},{1,2},{2,3},{3,4},{4,5},{5,6},{6,7},{8,9},{9,10},{10,11},{11... | collective-permute-start | bytes 737288 | tf_op jit(solution)/shard_map/ppermute | solution.py:555
  5.6 0.0 copy-done.1
  5.6 0.0 copy-done.3
  5.6 1.8 %pack.3 = (bf16[17,2,32,128]{3,2,1,0:T(8,128)(2,1)S(1)}, bf16[17,2,32,128]{3,2,1,0:T(8,128)(2,1)S(1)}, bf16[17,2,32,128]{3,2,1,0:T(8,128)(2,1)S(1)}, bf16[17,2,32,128]{3,2,1,0:T(8,128)(2,1)S(1)}) custom-call(bf16[2,32,24,576]{3,2,1,0:T(8,128)(2,1)S(1)} %copy-done.1, bf16[2,32,24,576]{3,2,1,0:T(8,128)(2,1)S(1)} %copy-done.1, ...), custom_call_target="tpu_custom_call" | custom-call | flops 100000000 | bytes 9000000 | tf_op jit(solution)/shard_map/pack/pallas_call | solution.py:234
  7.4 3.8 %collective-permute-done.refs_6_.refs_0_ = bf16[3,2,32,640]{3,2,1,0:T(8,128)(2,1)S(1)} collective-permute-done((bf16[3,2,32,640]{3,2,1,0:T(8,128)(2,1)S(1)}, bf16[3,2,32,640]{3,2,1,0:T(8,128)(2,1)S(1)}, u32[]{:S(2)}, u32[]{:S(2)}) %collective-permute-start) | collective-permute-done | bytes 245792 | tf_op jit(solution)/shard_map/ppermute | solution.py:555
  11.2 0.8 %patch.1 = (bf16[17,2,32,128]{3,2,1,0:T(8,128)(2,1)S(1)}, bf16[17,2,32,128]{3,2,1,0:T(8,128)(2,1)S(1)}, bf16[17,2,32,128]{3,2,1,0:T(8,128)(2,1)S(1)}, bf16[17,2,32,128]{3,2,1,0:T(8,128)(2,1)S(1)}) custom-call(bf16[3,2,32,640]{3,2,1,0:T(8,128)(2,1)S(1)} %collective-permute-done.refs_6_.refs_0_, ...), custom_call_target="tpu_custom_call", output_to_operand_aliasing={{0}: (1, {}), {1}: (2, {}), {2}: (3, {}), {3}: (4, {})} | custom-call | tf_op jit(solution)/shard_map/patch/pallas_call | solution.py:310
  12.0 1.6 %collective-permute-start.4 = (bf16[17,2,32,128]{3,2,1,0:T(8,128)(2,1)S(1)}, bf16[17,2,32,128]{3,2,1,0:T(8,128)(2,1)S(1)}, u32[]{:S(2)}, u32[]{:S(2)}) collective-permute-start(bf16[17,2,32,128]{3,2,1,0:T(8,128)(2,1)S(1)} %get-tuple-element.30), channel_id=1, source_target_pairs={{0,8},{8,0},{16,24},{24,16},{1,9},{9,1},{17,25},{25,17},{2,10},{10... | collective-permute-start | bytes 835592 | tf_op jit(solution)/shard_map/ppermute | solution.py:510
  13.6 1.5 %collective-permute-start.5 = (bf16[17,2,32,128]{3,2,1,0:T(8,128)(2,1)S(1)}, bf16[17,2,32,128]{3,2,1,0:T(8,128)(2,1)S(1)}, u32[]{:S(2)}, u32[]{:S(2)}) collective-permute-start(bf16[17,2,32,128]{3,2,1,0:T(8,128)(2,1)S(1)} %get-tuple-element.31), channel_id=1, source_target_pairs={{0,16},{8,24},{16,0},{24,8},{1,17},{9,25},{17,1},{25,9},{2,18},{10... | collective-permute-start | bytes 835592 | tf_op jit(solution)/shard_map/ppermute | solution.py:510
  15.1 0.5 collective-permute-start.6
  15.6 2.1 %pack.2 = (bf16[15,2,32,128]{3,2,1,0:T(8,128)(2,1)S(1)}, bf16[15,2,32,128]{3,2,1,0:T(8,128)(2,1)S(1)}, bf16[15,2,32,128]{3,2,1,0:T(8,128)(2,1)S(1)}, bf16[15,2,32,128]{3,2,1,0:T(8,128)(2,1)S(1)}) custom-call(bf16[2,32,24,576]{3,2,1,0:T(8,128)(2,1)S(1)} %copy-done.1, bf16[2,32,24,576]{3,2,1,0:T(8,128)(2,1)S(1)} %copy-done.1, ...), custom_call_target="tpu_custom_call" | custom-call | flops 100000000 | bytes 9000000 | tf_op jit(solution)/shard_map/pack/pallas_call | solution.py:234
  17.7 1.6 %collective-permute-start.1 = (bf16[15,2,32,128]{3,2,1,0:T(8,128)(2,1)S(1)}, bf16[15,2,32,128]{3,2,1,0:T(8,128)(2,1)S(1)}, u32[]{:S(2)}, u32[]{:S(2)}) collective-permute-start(bf16[15,2,32,128]{3,2,1,0:T(8,128)(2,1)S(1)} %get-tuple-element.22), channel_id=1, source_target_pairs={{0,8},{8,0},{16,24},{24,16},{1,9},{9,1},{17,25},{25,17},{2,10},{10... | collective-permute-start | bytes 737288 | tf_op jit(solution)/shard_map/ppermute | solution.py:510
  19.2 1.5 %collective-permute-start.2 = (bf16[15,2,32,128]{3,2,1,0:T(8,128)(2,1)S(1)}, bf16[15,2,32,128]{3,2,1,0:T(8,128)(2,1)S(1)}, u32[]{:S(2)}, u32[]{:S(2)}) collective-permute-start(bf16[15,2,32,128]{3,2,1,0:T(8,128)(2,1)S(1)} %get-tuple-element.23), channel_id=1, source_target_pairs={{0,16},{8,24},{16,0},{24,8},{1,17},{9,25},{17,1},{25,9},{2,18},{10... | collective-permute-start | bytes 737288 | tf_op jit(solution)/shard_map/ppermute | solution.py:510
  20.7 0.9 %collective-permute-done.4.refs_1_.refs_5_ = bf16[17,2,32,128]{3,2,1,0:T(8,128)(2,1)S(1)} collective-permute-done((bf16[17,2,32,128]{3,2,1,0:T(8,128)(2,1)S(1)}, bf16[17,2,32,128]{3,2,1,0:T(8,128)(2,1)S(1)}, u32[]{:S(2)}, u32[]{:S(2)}) %collective-permute-start.4) | collective-permute-done | bytes 278560 | tf_op jit(solution)/shard_map/ppermute | solution.py:510
  21.7 2.4 %collective-permute-start.3 = (bf16[15,2,32,128]{3,2,1,0:T(8,128)(2,1)S(1)}, bf16[15,2,32,128]{3,2,1,0:T(8,128)(2,1)S(1)}, u32[]{:S(2)}, u32[]{:S(2)}) collective-permute-start(bf16[15,2,32,128]{3,2,1,0:T(8,128)(2,1)S(1)} %get-tuple-element.24), channel_id=1, source_target_pairs={{0,24},{8,16},{16,8},{24,0},{1,25},{9,17},{17,9},{25,1},{2,26},{10... | collective-permute-start | bytes 737288 | tf_op jit(solution)/shard_map/ppermute | solution.py:510
  24.1 4.4 %collective-permute-done.5.refs_2_.refs_6_ = bf16[17,2,32,128]{3,2,1,0:T(8,128)(2,1)S(1)} collective-permute-done((bf16[17,2,32,128]{3,2,1,0:T(8,128)(2,1)S(1)}, bf16[17,2,32,128]{3,2,1,0:T(8,128)(2,1)S(1)}, u32[]{:S(2)}, u32[]{:S(2)}) %collective-permute-start.5) | collective-permute-done | bytes 278560 | tf_op jit(solution)/shard_map/ppermute | solution.py:510
  28.5 0.1 collective-permute-done.6.refs_3_.refs_7_
  28.6 7.2 %link.2.refs_8_ = f32[2,96,128]{2,1,0:T(8,128)S(1)} custom-call(bf16[17,2,32,128]{3,2,1,0:T(8,128)(2,1)S(1)} %get-tuple-element.29.refs_0_.refs_4_, bf16[17,2,32,128]{3,2,1,0:T(8,128)(2,1)S(1)} %collective-permute-done.4.refs_1_.refs_5_, bf16[17,2,32,128]{3,2,1,0:T(8,128)(2,1)S(1)} %collective-permute-done.5.refs_2_.refs_6_, ...), custom_call_target="tpu_custom_call" | custom-call | flops 2880000000 | bytes 1000000 | tf_op jit(solution)/shard_map/link/pallas_call | solution.py:486
  35.9 0.0 collective-permute-done.1.refs_1_
  35.9 1.7 %collective-permute-done.2.refs_2_ = bf16[15,2,32,128]{3,2,1,0:T(8,128)(2,1)S(1)} collective-permute-done((bf16[15,2,32,128]{3,2,1,0:T(8,128)(2,1)S(1)}, bf16[15,2,32,128]{3,2,1,0:T(8,128)(2,1)S(1)}, u32[]{:S(2)}, u32[]{:S(2)}) %collective-permute-start.2) | collective-permute-done | bytes 245792 | tf_op jit(solution)/shard_map/ppermute | solution.py:510
  37.6 0.0 collective-permute-done.3.refs_3_
  37.6 7.4 %link.3 = (f32[2,32,192]{2,1,0:T(8,128)S(1)}, f32[2,32,192]{2,1,0:T(8,128)S(1)}, f32[2,32,192]{2,1,0:T(8,128)S(1)}, f32[2,32,192]{2,1,0:T(8,128)S(1)}) custom-call(bf16[15,2,32,128]{3,2,1,0:T(8,128)(2,1)S(1)} %get-tuple-element.21.refs_0_, bf16[15,2,32,128]{3,2,1,0:T(8,128)(2,1)S(1)} %collective-permute-done.1.refs_1_, ...), custom_call_target="tpu_custom_call" | custom-call | flops 2880000000 | bytes 1000000 | tf_op jit(solution)/shard_map/link/pallas_call | solution.py:486
  45.0 1.3 %collective-permute-start.7 = (f32[2,32,192]{2,1,0:T(8,128)S(1)}, f32[2,32,192]{2,1,0:T(8,128)S(1)}, u32[]{:S(2)}, u32[]{:S(2)}) collective-permute-start(f32[2,32,192]{2,1,0:T(8,128)S(1)} %get-tuple-element.34), channel_id=1, source_target_pairs={{0,8},{8,0},{16,24},{24,16},{1,9},{9,1},{17,25},{25,17},{2,10},{10... | collective-permute-start | bytes 147464 | tf_op jit(solution)/shard_map/ppermute | solution.py:510
  46.3 0.8 %collective-permute-start.8 = (f32[2,32,192]{2,1,0:T(8,128)S(1)}, f32[2,32,192]{2,1,0:T(8,128)S(1)}, u32[]{:S(2)}, u32[]{:S(2)}) collective-permute-start(f32[2,32,192]{2,1,0:T(8,128)S(1)} %get-tuple-element.35), channel_id=1, source_target_pairs={{0,16},{8,24},{16,0},{24,8},{1,17},{9,25},{17,1},{25,9},{2,18},{10... | collective-permute-start | bytes 147464 | tf_op jit(solution)/shard_map/ppermute | solution.py:510
  47.1 1.4 %collective-permute-start.9 = (f32[2,32,192]{2,1,0:T(8,128)S(1)}, f32[2,32,192]{2,1,0:T(8,128)S(1)}, u32[]{:S(2)}, u32[]{:S(2)}) collective-permute-start(f32[2,32,192]{2,1,0:T(8,128)S(1)} %get-tuple-element.36), channel_id=1, source_target_pairs={{0,24},{8,16},{16,8},{24,0},{1,25},{9,17},{17,9},{25,1},{2,26},{10... | collective-permute-start | bytes 147464 | tf_op jit(solution)/shard_map/ppermute | solution.py:510
  48.5 1.0 %collective-permute-done.7.refs_1_ = f32[2,32,192]{2,1,0:T(8,128)S(1)} collective-permute-done((f32[2,32,192]{2,1,0:T(8,128)S(1)}, f32[2,32,192]{2,1,0:T(8,128)S(1)}, u32[]{:S(2)}, u32[]{:S(2)}) %collective-permute-start.7) | collective-permute-done | bytes 49184 | tf_op jit(solution)/shard_map/ppermute | solution.py:510
  49.5 1.1 %collective-permute-done.8.refs_2_ = f32[2,32,192]{2,1,0:T(8,128)S(1)} collective-permute-done((f32[2,32,192]{2,1,0:T(8,128)S(1)}, f32[2,32,192]{2,1,0:T(8,128)S(1)}, u32[]{:S(2)}, u32[]{:S(2)}) %collective-permute-start.8) | collective-permute-done | bytes 49184 | tf_op jit(solution)/shard_map/ppermute | solution.py:510
  50.6 1.7 %collective-permute-done.9.refs_3_ = f32[2,32,192]{2,1,0:T(8,128)S(1)} collective-permute-done((f32[2,32,192]{2,1,0:T(8,128)S(1)}, f32[2,32,192]{2,1,0:T(8,128)S(1)}, u32[]{:S(2)}, u32[]{:S(2)}) %collective-permute-start.9) | collective-permute-done | bytes 49184 | tf_op jit(solution)/shard_map/ppermute | solution.py:510
  52.3 0.8 %place.1 = f32[2,32,4,192]{3,2,1,0:T(4,128)} custom-call(f32[2,32,192]{2,1,0:T(8,128)S(1)} %get-tuple-element.33.refs_0_, f32[2,32,192]{2,1,0:T(8,128)S(1)} %collective-permute-done.7.refs_1_, f32[2,32,192]{2,1,0:T(8,128)S(1)} %collective-permute-done.8.refs_2_, f32[2,32,192]{2,1,0:T(8,128)S(1)} %collective-permute-done.9.refs_3_), custom_call_target="tpu_custom_call" | custom-call | tf_op jit(solution)/shard_map/place/pallas_call | solution.py:529
Async XLA Ops:
  0.0 1.5 %copy-start = (bf16[2,32,24,576]{3,2,1,0:T(8,128)(2,1)S(1)}, bf16[2,32,24,576]{3,2,1,0:T(8,128)(2,1)}, u32[]{:S(2)}) copy-start(bf16[2,32,24,576]{3,2,1,0:T(8,128)(2,1)} %refs_2_.3) | copy-start | bytes 5308420
  1.5 1.5 %copy-start.2 = (s32[32,24,576]{2,1,0:T(8,128)S(1)}, s32[32,24,576]{2,1,0:T(8,128)}, u32[]{:S(2)}) copy-start(s32[32,24,576]{2,1,0:T(8,128)} %refs_5_.3) | copy-start | bytes 5308420
  3.1 2.5 %copy-start.1 = (bf16[2,32,24,576]{3,2,1,0:T(8,128)(2,1)S(1)}, bf16[2,32,24,576]{3,2,1,0:T(8,128)(2,1)}, u32[]{:S(2)}) copy-start(bf16[2,32,24,576]{3,2,1,0:T(8,128)(2,1)} %refs_2_.3) | copy-start | bytes 5308420
  3.1 2.5 %copy-start.3 = (s32[32,24,576]{2,1,0:T(8,128)S(1)}, s32[32,24,576]{2,1,0:T(8,128)}, u32[]{:S(2)}) copy-start(s32[32,24,576]{2,1,0:T(8,128)} %refs_5_.3) | copy-start | bytes 5308420
  3.4 7.8 %collective-permute-start = (bf16[3,2,32,640]{3,2,1,0:T(8,128)(2,1)S(1)}, bf16[3,2,32,640]{3,2,1,0:T(8,128)(2,1)S(1)}, u32[]{:S(2)}, u32[]{:S(2)}) collective-permute-start(bf16[3,2,32,640]{3,2,1,0:T(8,128)(2,1)S(1)} %edge.1), channel_id=1, source_target_pairs={{0,1},{1,2},{2,3},{3,4},{4,5},{5,6},{6,7},{8,9},{9,10},{10,11},{11... | collective-permute-start | bytes 737288 | tf_op jit(solution)/shard_map/ppermute | solution.py:555
  12.0 9.7 %collective-permute-start.4 = (bf16[17,2,32,128]{3,2,1,0:T(8,128)(2,1)S(1)}, bf16[17,2,32,128]{3,2,1,0:T(8,128)(2,1)S(1)}, u32[]{:S(2)}, u32[]{:S(2)}) collective-permute-start(bf16[17,2,32,128]{3,2,1,0:T(8,128)(2,1)S(1)} %get-tuple-element.30), channel_id=1, source_target_pairs={{0,8},{8,0},{16,24},{24,16},{1,9},{9,1},{17,25},{25,17},{2,10},{10... | collective-permute-start | bytes 835592 | tf_op jit(solution)/shard_map/ppermute | solution.py:510
  13.6 15.0 %collective-permute-start.5 = (bf16[17,2,32,128]{3,2,1,0:T(8,128)(2,1)S(1)}, bf16[17,2,32,128]{3,2,1,0:T(8,128)(2,1)S(1)}, u32[]{:S(2)}, u32[]{:S(2)}) collective-permute-start(bf16[17,2,32,128]{3,2,1,0:T(8,128)(2,1)S(1)} %get-tuple-element.31), channel_id=1, source_target_pairs={{0,16},{8,24},{16,0},{24,8},{1,17},{9,25},{17,1},{25,9},{2,18},{10... | collective-permute-start | bytes 835592 | tf_op jit(solution)/shard_map/ppermute | solution.py:510
  15.1 13.6 %collective-permute-start.6 = (bf16[17,2,32,128]{3,2,1,0:T(8,128)(2,1)S(1)}, bf16[17,2,32,128]{3,2,1,0:T(8,128)(2,1)S(1)}, u32[]{:S(2)}, u32[]{:S(2)}) collective-permute-start(bf16[17,2,32,128]{3,2,1,0:T(8,128)(2,1)S(1)} %get-tuple-element.32), channel_id=1, source_target_pairs={{0,24},{8,16},{16,8},{24,0},{1,25},{9,17},{17,9},{25,1},{2,26},{10... | collective-permute-start | bytes 835592 | tf_op jit(solution)/shard_map/ppermute | solution.py:510
  17.7 18.2 %collective-permute-start.1 = (bf16[15,2,32,128]{3,2,1,0:T(8,128)(2,1)S(1)}, bf16[15,2,32,128]{3,2,1,0:T(8,128)(2,1)S(1)}, u32[]{:S(2)}, u32[]{:S(2)}) collective-permute-start(bf16[15,2,32,128]{3,2,1,0:T(8,128)(2,1)S(1)} %get-tuple-element.22), channel_id=1, source_target_pairs={{0,8},{8,0},{16,24},{24,16},{1,9},{9,1},{17,25},{25,17},{2,10},{10... | collective-permute-start | bytes 737288 | tf_op jit(solution)/shard_map/ppermute | solution.py:510
  19.2 18.3 %collective-permute-start.2 = (bf16[15,2,32,128]{3,2,1,0:T(8,128)(2,1)S(1)}, bf16[15,2,32,128]{3,2,1,0:T(8,128)(2,1)S(1)}, u32[]{:S(2)}, u32[]{:S(2)}) collective-permute-start(bf16[15,2,32,128]{3,2,1,0:T(8,128)(2,1)S(1)} %get-tuple-element.23), channel_id=1, source_target_pairs={{0,16},{8,24},{16,0},{24,8},{1,17},{9,25},{17,1},{25,9},{2,18},{10... | collective-permute-start | bytes 737288 | tf_op jit(solution)/shard_map/ppermute | solution.py:510
  21.7 15.9 %collective-permute-start.3 = (bf16[15,2,32,128]{3,2,1,0:T(8,128)(2,1)S(1)}, bf16[15,2,32,128]{3,2,1,0:T(8,128)(2,1)S(1)}, u32[]{:S(2)}, u32[]{:S(2)}) collective-permute-start(bf16[15,2,32,128]{3,2,1,0:T(8,128)(2,1)S(1)} %get-tuple-element.24), channel_id=1, source_target_pairs={{0,24},{8,16},{16,8},{24,0},{1,25},{9,17},{17,9},{25,1},{2,26},{10... | collective-permute-start | bytes 737288 | tf_op jit(solution)/shard_map/ppermute | solution.py:510
  45.0 4.5 %collective-permute-start.7 = (f32[2,32,192]{2,1,0:T(8,128)S(1)}, f32[2,32,192]{2,1,0:T(8,128)S(1)}, u32[]{:S(2)}, u32[]{:S(2)}) collective-permute-start(f32[2,32,192]{2,1,0:T(8,128)S(1)} %get-tuple-element.34), channel_id=1, source_target_pairs={{0,8},{8,0},{16,24},{24,16},{1,9},{9,1},{17,25},{25,17},{2,10},{10... | collective-permute-start | bytes 147464 | tf_op jit(solution)/shard_map/ppermute | solution.py:510
  46.3 4.3 %collective-permute-start.8 = (f32[2,32,192]{2,1,0:T(8,128)S(1)}, f32[2,32,192]{2,1,0:T(8,128)S(1)}, u32[]{:S(2)}, u32[]{:S(2)}) collective-permute-start(f32[2,32,192]{2,1,0:T(8,128)S(1)} %get-tuple-element.35), channel_id=1, source_target_pairs={{0,16},{8,24},{16,0},{24,8},{1,17},{9,25},{17,1},{25,9},{2,18},{10... | collective-permute-start | bytes 147464 | tf_op jit(solution)/shard_map/ppermute | solution.py:510
  47.1 5.2 %collective-permute-start.9 = (f32[2,32,192]{2,1,0:T(8,128)S(1)}, f32[2,32,192]{2,1,0:T(8,128)S(1)}, u32[]{:S(2)}, u32[]{:S(2)}) collective-permute-start(f32[2,32,192]{2,1,0:T(8,128)S(1)} %get-tuple-element.36), channel_id=1, source_target_pairs={{0,24},{8,16},{16,8},{24,0},{1,25},{9,17},{17,9},{25,1},{2,26},{10... | collective-permute-start | bytes 147464 | tf_op jit(solution)/shard_map/ppermute | solution.py:510

commit v4 on v3

--- a/solution.py
+++ b/solution.py
@@ -1,5 +1,4 @@
 import functools
-import math
 
 import jax
 import jax.numpy as jnp
@@ -22,8 +21,8 @@
 SLOTS = TILE_ROWS // STEP_ROWS
 LEAD = MARGIN // STEP_ROWS
 LEFT = STEP_COLS // 2
-BATCH = 48
-CHUNKS = (4,)
+BATCH = 60
+FIRST = 19
 CONTRACT_LAST = (((1,), (1,)), ((), ()))
 
 
@@ -37,8 +36,8 @@
     return jnp.where(jnp.broadcast_to(mask, yes.shape), yes, no)
 
 
-def edge_kernel(first, *refs):
-    acq_ref, valid_ref, out, planes = refs
+def edge_kernel(first, ranges, *refs):
+    acq_ref, valid_ref, *outs, planes = refs
     parts, dates, _, rows = acq_ref.shape
     stride = planes.shape[2] // dates
     span = slice(first // 8 * 8, first // 8 * 8 + 8)
@@ -60,27 +59,32 @@
     lax.fori_loop(0, dates, one_date, 0, unroll=4)
     for j in range(LEFT):
         for part in range(parts):
-            for block in range(planes.shape[1]):
-                plane = planes[part, block, pl.ds(offset + j, dates, stride=stride), :]
-                out[j, part, :, block * LANES : (block + 1) * LANES] = plane.astype(out.dtype)
-
-
-def edge(acquisitions, valid_dates):
+            for out, span in zip(outs, ranges):
+                for index, block in enumerate(span):
+                    plane = planes[part, block, pl.ds(offset + j, dates, stride=stride), :]
+                    lanes = slice(index * LANES, (index + 1) * LANES)
+                    out[j, part, :, lanes] = plane.astype(out.dtype)
+
+
+def edge(acquisitions, valid_dates, ranges):
     parts, dates, cols, rows = acquisitions.shape
     blocks = -(-rows // LANES)
     at = (cols - LEFT) // 16
-    shape = jax.ShapeDtypeStruct((LEFT, parts, dates, blocks * LANES), acquisitions.dtype)
+    shapes = [
+        jax.ShapeDtypeStruct((LEFT, parts, dates, len(span) * LANES), acquisitions.dtype)
+        for span in ranges
+    ]
     return pl.pallas_call(
-        functools.partial(edge_kernel, cols - LEFT - at * 16),
+        functools.partial(edge_kernel, cols - LEFT - at * 16, ranges),
         grid=(1,),
-        out_shape=shape,
+        out_shape=shapes,
         in_specs=[
             pl.BlockSpec((parts, dates, 16, rows), lambda i: (0, 0, at, 0)),
             pl.BlockSpec((dates, 16, rows), lambda i: (0, at, 0)),
         ],
-        out_specs=pl.BlockSpec(shape.shape, lambda i: (0, 0, 0, 0)),
+        out_specs=[pl.BlockSpec(shape.shape, lambda i: (0, 0, 0, 0)) for shape in shapes],
         scratch_shapes=[pltpu.VMEM((parts, blocks, dates * 9, LANES), jnp.float32)],
-        compiler_params=pltpu.CompilerParams(vmem_limit_bytes=16 << 20),
+        compiler_params=pltpu.CompilerParams(vmem_limit_bytes=60 << 20),
         name="edge",
     )(acquisitions, valid_dates)
 
@@ -89,9 +93,9 @@
     return pltpu.roll(plane, TILE_ROWS * j, 1) if j else plane
 
 
-def edge_planes(halo, first_block, blocks, keep):
-    for block in range(blocks):
-        at = (first_block + block) * LANES
+def edge_planes(halo, keep):
+    for block in range(halo.shape[3] // LANES):
+        at = block * LANES
         for j in range(LEFT):
             for part in range(halo.shape[1]):
                 plane = halo[j, part, :, at : at + LANES].astype(jnp.float32)
@@ -167,7 +171,7 @@
 
     if with_halo:
         fetch.wait()
-        edge_planes(halo, first_block, blocks, keep_edge)
+        edge_planes(halo, keep_edge)
     else:
         zero = jnp.zeros((dates, LANES), jnp.bfloat16)
         for block in range(blocks):
@@ -202,14 +206,17 @@
             lax.fori_loop(0, tiles + 2, one_tile, 0)
 
 
+def blocks_of(low, high, rows, segments):
+    if segments > 1:
+        return range(-(-rows // LANES))
+    return range(low * TILE_ROWS // LANES, -(-high * TILE_ROWS // LANES))
+
+
 def pack(acquisitions, valid_dates, halo, peers, ends, col_groups, segments):
     parts, dates, cols, rows = acquisitions.shape
-    if segments == 1:
-        sent = [high - low for low, high in zip(ends, ends[1:])]
-        first = ends[0] * TILE_ROWS // LANES
-        blocks = -(-ends[-1] * TILE_ROWS // LANES) - first
-    else:
-        sent, first, blocks = [ends[-1] + 2], 0, -(-rows // LANES)
+    span = blocks_of(ends[0], ends[-1], rows, segments)
+    first, blocks = span[0], len(span)
+    sent = [high - low + (2 if segments > 1 else 0) for low, high in zip(ends, ends[1:])]
 
     def block_specs(shape):
         return [
@@ -254,7 +261,6 @@
     peers = (len(refs) - 4) // 2
     outs, (halo, planes, held, sems) = refs[peers:-4], refs[-4:]
     sent, parts, dates, _ = held.shape
-    blocks = planes.shape[0]
     me = lax.axis_index("date")
     fetch = pltpu.make_async_copy(halo_ref, halo, sems.at[0])
     fetch.start()
@@ -275,7 +281,7 @@
             read.start()
             if offset < col_groups:
                 fetch.wait()
-                edge_planes(halo, 0, blocks, keep_edge)
+                edge_planes(halo, keep_edge)
             read.wait()
             masks = {}
             if segments == 1:
@@ -302,10 +308,6 @@
 def patch(blocks, halo, tiles, col_groups, segments):
     peers = len(blocks)
     _, parts, dates, _ = blocks[0].shape
-    if segments == 1:
-        lanes = -(-tiles * TILE_ROWS // LANES)
-    else:
-        lanes = halo.shape[3] // LANES
     anywhere = pl.BlockSpec(memory_space=pl.ANY)
     return pl.pallas_call(
         functools.partial(patch_kernel, tiles, col_groups, segments),
@@ -314,7 +316,7 @@
         out_specs=[anywhere] * peers,
         scratch_shapes=[
             pltpu.VMEM(halo.shape, halo.dtype),
-            pltpu.VMEM((lanes, LEFT, parts, dates, LANES), jnp.bfloat16),
+            pltpu.VMEM((halo.shape[3] // LANES, LEFT, parts, dates, LANES), jnp.bfloat16),
             pltpu.VMEM(blocks[0].shape, jnp.bfloat16),
             pltpu.SemaphoreType.DMA((3,)),
         ],
@@ -396,6 +398,10 @@
     return scaled
 
 
+def batch_of(pixels):
+    return max(size for size in range(SLOTS, BATCH + 1, SLOTS) if pixels % size == 0)
+
+
 def link_kernel(peers, carried, earlier, start, padded, last, *refs):
     sources, refs = refs[:peers], refs[peers:]
     before, refs = refs[: peers * carried], refs[peers * carried :]
@@ -426,7 +432,7 @@
     for copy in copies:
         copy.wait()
     pixels = linked.shape[1]
-    batch = math.gcd(BATCH, pixels)
+    batch = batch_of(pixels)
     diagonal = lax.broadcasted_iota(
         jnp.int32, (all_dates, all_dates), 0
     ) == lax.broadcasted_iota(jnp.int32, (all_dates, all_dates), 1)
@@ -492,7 +498,7 @@
         scratch_shapes=[
             pltpu.VMEM((kept, all_dates, LANES), jnp.bfloat16),
             pltpu.VMEM((kept, all_dates, LANES), jnp.bfloat16),
-            pltpu.VMEM((math.gcd(BATCH, pixels), 2 * all_dates, all_dates), jnp.bfloat16),
+            pltpu.VMEM((batch_of(pixels), 2 * all_dates, all_dates), jnp.bfloat16),
             pltpu.VMEM((2, pixels, all_dates), jnp.float32),
             pltpu.SemaphoreType.DMA((4 * peers,)),
         ],
@@ -537,11 +543,9 @@
 
 
 def chunk_ends(tiles, segments):
-    step = BATCH // SLOTS
-    if segments > 1 or tiles % step:
+    if segments > 1 or tiles < 8:
         return [tiles]
-    count = tiles // step
-    return [step * (count * share // 8) + 1 for share in CHUNKS] + [tiles]
+    return [tiles * FIRST // 32, tiles]
 
 
 def on_device(acquisitions, valid_dates):
@@ -552,15 +556,19 @@
     segments = peers // out_cols
     tiles = rows // TILE_ROWS // segments
     pixels = rows // STEP_ROWS // segments
-    halo = lax.ppermute(
-        edge(acquisitions, valid_dates), "space", [(i, i + 1) for i in range(strips - 1)]
-    )
     ends = chunk_ends(tiles, segments)
     first, *rest = ends
+    ranges = [blocks_of(0, first, rows, segments)]
+    if rest:
+        ranges.append(blocks_of(first, tiles, rows, segments))
+    halos = [
+        lax.ppermute(edges, "space", [(i, i + 1) for i in range(strips - 1)])
+        for edges in edge(acquisitions, valid_dates, ranges)
+    ]
     (blocks,) = pack(acquisitions, valid_dates, None, peers, [0, first], out_cols, segments)
-    outgoing = [patch(blocks, halo, first, out_cols, segments)]
+    outgoing = [patch(blocks, halos[0], first, out_cols, segments)]
     if rest:
-        outgoing += pack(acquisitions, valid_dates, halo, peers, ends, out_cols, segments)
+        outgoing += pack(acquisitions, valid_dates, halos[1], peers, ends, out_cols, segments)
     incoming = [swap(blocks, "date") for blocks in outgoing]
     done, start = [], 0
     for index, blocks in enumerate(incoming):

time: 53.3 us -> 50.4 us (0.946)
  local copies, waits for them, and re-layouts: 3.1 us -> 0.01 us
  Pallas kernels: 20.4 us -> 22.2 us
  waiting for transfers between devices: 14.7 us -> 13.1 us
    ppermute x9, waiting for transfers between devices: 10.9 us -> 5.89 us  [swap(): lax.ppermute(blocks[m], axis, [(i, i ^ m) for i in range(count)])]
    ppermute x1 -> x2, waiting for transfers between devices: 3.78 us -> 7.21 us  [on_device(): lax.ppermute(edges, 'space', [(i, i + 1) for i in range(strips - 1)])]
    unnamed x8 -> x6, local copies, waits for them, and re-layouts: 3.1 us -> 0.01 us
    pallas_call x1, Pallas kernels: 0.3 us -> 2.38 us  [edge(): pl.pallas_call(functools.partial(edge_kernel, cols - LEFT - at * 16, rang...]
    ppermute x9, starting transfers between devices: 12.6 us -> 10.7 us  [swap(): lax.ppermute(blocks[m], axis, [(i, i ^ m) for i in range(count)])]
    ppermute x1 -> x2, starting transfers between devices: 2.18 us -> 4.13 us  [on_device(): lax.ppermute(edges, 'space', [(i, i + 1) for i in range(strips - 1)])]
  transfers between devices with their start and end apart: 10 -> 11, of which waited for: 8 -> 7; matrix products, arithmetic and copies ran while one was open for 0% -> 0% of each run, Pallas kernels for 21% -> 23%
where the time goes in v4:
time: 50.4 us; the launch traced here: 50.2 us
  Pallas kernels  22.2 us (44%)
  starting transfers between devices  14.8 us (29%)
  waiting for transfers between devices  13.1 us (26%)
    pallas_call x2, Pallas kernels, link(): pl.pallas_call(kernel, grid=(1,), out_shape=outs, in_specs=specs, out_spe...  14.6 us
    ppermute x9, starting transfers between devices, swap(): lax.ppermute(blocks[m], axis, [(i, i ^ m) for i in range(count)])  10.7 us
    ppermute x2, waiting for transfers between devices, on_device(): lax.ppermute(edges, 'space', [(i, i + 1) for i in range(strips - 1)])  7.21 us
    ppermute x9, waiting for transfers between devices, swap(): lax.ppermute(blocks[m], axis, [(i, i ^ m) for i in range(count)])  5.89 us
    ppermute x2, starting transfers between devices, on_device(): lax.ppermute(edges, 'space', [(i, i + 1) for i in range(strips - 1)])  4.13 us
    pallas_call x2, Pallas kernels, pack(): pl.pallas_call(functools.partial(pack_kernel, ends, first, blocks, col_gr...  3.75 us
    pallas_call x1, Pallas kernels, edge(): pl.pallas_call(functools.partial(edge_kernel, cols - LEFT - at * 16, rang...  2.38 us
  transfers between devices with their start and end apart: 11, of which 7 were waited for; matrix products, arithmetic and copies ran while one was open for 0% of the time, Pallas kernels for 23%

profile of v4, /device:TPU:16, one launch (start us, length us, event | category | flops | bytes accessed | tf_op | source)
XLA Modules:
  0.0 50.2 jit_solution(12137265847806765349)
XLA Ops:
  0.0 0.0 copy-start
  0.0 0.0 copy-start.1
  0.0 2.4 %edge.1 = (bf16[3,2,32,384]{3,2,1,0:T(8,128)(2,1)}, bf16[3,2,32,384]{3,2,1,0:T(8,128)(2,1)}) custom-call(bf16[2,32,24,576]{3,2,1,0:T(8,128)(2,1)} %refs_2_.3, s32[32,24,576]{2,1,0:T(8,128)} %refs_5_.3), custom_call_target="tpu_custom_call" | custom-call | tf_op jit(solution)/shard_map/edge/pallas_call | solution.py:77
  2.4 0.0 copy-start.2
  2.4 2.0 %collective-permute-start.4 = (bf16[3,2,32,384]{3,2,1,0:T(8,128)(2,1)}, bf16[3,2,32,384]{3,2,1,0:T(8,128)(2,1)S(1)}, u32[]{:S(2)}, u32[]{:S(2)}) collective-permute-start(bf16[3,2,32,384]{3,2,1,0:T(8,128)(2,1)} %get-tuple-element.28), channel_id=1, source_target_pairs={{0,1},{1,2},{2,3},{3,4},{4,5},{5,6},{6,7},{8,9},{9,10},{10,11},{11... | collective-permute-start | bytes 442376 | tf_op jit(solution)/shard_map/ppermute | solution.py:565
  4.4 0.0 copy-done
  4.4 0.0 copy-done.1
  4.5 1.9 %pack.3 = (bf16[19,2,32,128]{3,2,1,0:T(8,128)(2,1)S(1)}, bf16[19,2,32,128]{3,2,1,0:T(8,128)(2,1)S(1)}, bf16[19,2,32,128]{3,2,1,0:T(8,128)(2,1)S(1)}, bf16[19,2,32,128]{3,2,1,0:T(8,128)(2,1)S(1)}) custom-call(bf16[2,32,24,576]{3,2,1,0:T(8,128)(2,1)S(1)} %copy-done, bf16[2,32,24,576]{3,2,1,0:T(8,128)(2,1)S(1)} %copy-done, ...), custom_call_target="tpu_custom_call" | custom-call | flops 100000000 | bytes 9000000 | tf_op jit(solution)/shard_map/pack/pallas_call | solution.py:241
  6.3 2.9 %collective-permute-done.4.refs_0_ = bf16[3,2,32,384]{3,2,1,0:T(8,128)(2,1)S(1)} collective-permute-done((bf16[3,2,32,384]{3,2,1,0:T(8,128)(2,1)}, bf16[3,2,32,384]{3,2,1,0:T(8,128)(2,1)S(1)}, u32[]{:S(2)}, u32[]{:S(2)}) %collective-permute-start.4) | collective-permute-done | bytes 147488 | tf_op jit(solution)/shard_map/ppermute | solution.py:565
  9.2 0.6 %patch.1 = (bf16[19,2,32,128]{3,2,1,0:T(8,128)(2,1)S(1)}, bf16[19,2,32,128]{3,2,1,0:T(8,128)(2,1)S(1)}, bf16[19,2,32,128]{3,2,1,0:T(8,128)(2,1)S(1)}, bf16[19,2,32,128]{3,2,1,0:T(8,128)(2,1)S(1)}) custom-call(bf16[3,2,32,384]{3,2,1,0:T(8,128)(2,1)S(1)} %collective-permute-done.4.refs_0_, ...), custom_call_target="tpu_custom_call", output_to_operand_aliasing={{0}: (1, {}), {1}: (2, {}), {2}: (3, {}), {3}: (4, {})} | custom-call | tf_op jit(solution)/shard_map/patch/pallas_call | solution.py:312
  9.8 1.6 %collective-permute-start.5 = (bf16[19,2,32,128]{3,2,1,0:T(8,128)(2,1)S(1)}, bf16[19,2,32,128]{3,2,1,0:T(8,128)(2,1)S(1)}, u32[]{:S(2)}, u32[]{:S(2)}) collective-permute-start(bf16[19,2,32,128]{3,2,1,0:T(8,128)(2,1)S(1)} %get-tuple-element.34), channel_id=1, source_target_pairs={{0,8},{8,0},{16,24},{24,16},{1,9},{9,1},{17,25},{25,17},{2,10},{10... | collective-permute-start | bytes 933896 | tf_op jit(solution)/shard_map/ppermute | solution.py:516
  11.4 1.5 %collective-permute-start.6 = (bf16[19,2,32,128]{3,2,1,0:T(8,128)(2,1)S(1)}, bf16[19,2,32,128]{3,2,1,0:T(8,128)(2,1)S(1)}, u32[]{:S(2)}, u32[]{:S(2)}) collective-permute-start(bf16[19,2,32,128]{3,2,1,0:T(8,128)(2,1)S(1)} %get-tuple-element.35), channel_id=1, source_target_pairs={{0,16},{8,24},{16,0},{24,8},{1,17},{9,25},{17,1},{25,9},{2,18},{10... | collective-permute-start | bytes 933896 | tf_op jit(solution)/shard_map/ppermute | solution.py:516
  12.9 0.5 collective-permute-start.7
  13.4 0.0 copy-done.2
  13.4 2.1 %collective-permute-start = (bf16[3,2,32,384]{3,2,1,0:T(8,128)(2,1)S(1)}, bf16[3,2,32,384]{3,2,1,0:T(8,128)(2,1)S(1)}, u32[]{:S(2)}, u32[]{:S(2)}) collective-permute-start(bf16[3,2,32,384]{3,2,1,0:T(8,128)(2,1)S(1)} %copy-done.2), channel_id=1, source_target_pairs={{0,1},{1,2},{2,3},{3,4},{4,5},{5,6},{6,7},{8,9},{9,10},{10,11},{11... | collective-permute-start | bytes 442376 | tf_op jit(solution)/shard_map/ppermute | solution.py:565
  15.5 4.4 %collective-permute-done.refs_6_ = bf16[3,2,32,384]{3,2,1,0:T(8,128)(2,1)S(1)} collective-permute-done((bf16[3,2,32,384]{3,2,1,0:T(8,128)(2,1)S(1)}, bf16[3,2,32,384]{3,2,1,0:T(8,128)(2,1)S(1)}, u32[]{:S(2)}, u32[]{:S(2)}) %collective-permute-start) | collective-permute-done | bytes 147488 | tf_op jit(solution)/shard_map/ppermute | solution.py:565
  19.8 1.9 %pack.2 = (bf16[13,2,32,128]{3,2,1,0:T(8,128)(2,1)S(1)}, bf16[13,2,32,128]{3,2,1,0:T(8,128)(2,1)S(1)}, bf16[13,2,32,128]{3,2,1,0:T(8,128)(2,1)S(1)}, bf16[13,2,32,128]{3,2,1,0:T(8,128)(2,1)S(1)}) custom-call(bf16[2,32,24,576]{3,2,1,0:T(8,128)(2,1)S(1)} %copy-done, bf16[2,32,24,576]{3,2,1,0:T(8,128)(2,1)S(1)} %copy-done, ...), custom_call_target="tpu_custom_call" | custom-call | flops 100000000 | bytes 9000000 | tf_op jit(solution)/shard_map/pack/pallas_call | solution.py:241
  21.7 1.6 %collective-permute-start.1 = (bf16[13,2,32,128]{3,2,1,0:T(8,128)(2,1)S(1)}, bf16[13,2,32,128]{3,2,1,0:T(8,128)(2,1)S(1)}, u32[]{:S(2)}, u32[]{:S(2)}) collective-permute-start(bf16[13,2,32,128]{3,2,1,0:T(8,128)(2,1)S(1)} %get-tuple-element.25), channel_id=1, source_target_pairs={{0,8},{8,0},{16,24},{24,16},{1,9},{9,1},{17,25},{25,17},{2,10},{10... | collective-permute-start | bytes 638984 | tf_op jit(solution)/shard_map/ppermute | solution.py:516
  23.3 1.5 %collective-permute-start.2 = (bf16[13,2,32,128]{3,2,1,0:T(8,128)(2,1)S(1)}, bf16[13,2,32,128]{3,2,1,0:T(8,128)(2,1)S(1)}, u32[]{:S(2)}, u32[]{:S(2)}) collective-permute-start(bf16[13,2,32,128]{3,2,1,0:T(8,128)(2,1)S(1)} %get-tuple-element.26), channel_id=1, source_target_pairs={{0,16},{8,24},{16,0},{24,8},{1,17},{9,25},{17,1},{25,9},{2,18},{10... | collective-permute-start | bytes 638984 | tf_op jit(solution)/shard_map/ppermute | solution.py:516
  24.8 0.0 collective-permute-done.5.refs_1_.refs_5_
  24.8 0.5 collective-permute-start.3
  25.3 0.4 collective-permute-done.6.refs_2_.refs_6_
  25.7 2.0 %collective-permute-done.7.refs_3_.refs_7_ = bf16[19,2,32,128]{3,2,1,0:T(8,128)(2,1)S(1)} collective-permute-done((bf16[19,2,32,128]{3,2,1,0:T(8,128)(2,1)S(1)}, bf16[19,2,32,128]{3,2,1,0:T(8,128)(2,1)S(1)}, u32[]{:S(2)}, u32[]{:S(2)}) %collective-permute-start.7) | collective-permute-done | bytes 311328 | tf_op jit(solution)/shard_map/ppermute | solution.py:516
  27.6 8.0 %link.2.refs_8_ = f32[2,108,128]{2,1,0:T(8,128)S(1)} custom-call(bf16[19,2,32,128]{3,2,1,0:T(8,128)(2,1)S(1)} %get-tuple-element.33.refs_0_.refs_4_, bf16[19,2,32,128]{3,2,1,0:T(8,128)(2,1)S(1)} %collective-permute-done.5.refs_1_.refs_5_, bf16[19,2,32,128]{3,2,1,0:T(8,128)(2,1)S(1)} %collective-permute-done.6.refs_2_.refs_6_, ...), custom_call_target="tpu_custom_call" | custom-call | flops 3240000000 | bytes 1000000 | tf_op jit(solution)/shard_map/link/pallas_call | solution.py:492
  35.7 0.0 collective-permute-done.1.refs_1_
  35.7 0.0 collective-permute-done.2.refs_2_
  35.7 0.0 collective-permute-done.3.refs_3_
  35.7 6.6 %link.3 = (f32[2,32,192]{2,1,0:T(8,128)S(1)}, f32[2,32,192]{2,1,0:T(8,128)S(1)}, f32[2,32,192]{2,1,0:T(8,128)S(1)}, f32[2,32,192]{2,1,0:T(8,128)S(1)}) custom-call(bf16[13,2,32,128]{3,2,1,0:T(8,128)(2,1)S(1)} %get-tuple-element.24.refs_0_, bf16[13,2,32,128]{3,2,1,0:T(8,128)(2,1)S(1)} %collective-permute-done.1.refs_1_, ...), custom_call_target="tpu_custom_call" | custom-call | flops 2520000000 | bytes 1000000 | tf_op jit(solution)/shard_map/link/pallas_call | solution.py:492
  42.3 1.5 %collective-permute-start.10 = (f32[2,32,192]{2,1,0:T(8,128)S(1)}, f32[2,32,192]{2,1,0:T(8,128)S(1)}, u32[]{:S(2)}, u32[]{:S(2)}) collective-permute-start(f32[2,32,192]{2,1,0:T(8,128)S(1)} %get-tuple-element.40), channel_id=1, source_target_pairs={{0,24},{8,16},{16,8},{24,0},{1,25},{9,17},{17,9},{25,1},{2,26},{10... | collective-permute-start | bytes 147464 | tf_op jit(solution)/shard_map/ppermute | solution.py:516
  43.8 1.3 %collective-permute-start.8 = (f32[2,32,192]{2,1,0:T(8,128)S(1)}, f32[2,32,192]{2,1,0:T(8,128)S(1)}, u32[]{:S(2)}, u32[]{:S(2)}) collective-permute-start(f32[2,32,192]{2,1,0:T(8,128)S(1)} %get-tuple-element.38), channel_id=1, source_target_pairs={{0,8},{8,0},{16,24},{24,16},{1,9},{9,1},{17,25},{25,17},{2,10},{10... | collective-permute-start | bytes 147464 | tf_op jit(solution)/shard_map/ppermute | solution.py:516
  45.1 0.8 %collective-permute-start.9 = (f32[2,32,192]{2,1,0:T(8,128)S(1)}, f32[2,32,192]{2,1,0:T(8,128)S(1)}, u32[]{:S(2)}, u32[]{:S(2)}) collective-permute-start(f32[2,32,192]{2,1,0:T(8,128)S(1)} %get-tuple-element.39), channel_id=1, source_target_pairs={{0,16},{8,24},{16,0},{24,8},{1,17},{9,25},{17,1},{25,9},{2,18},{10... | collective-permute-start | bytes 147464 | tf_op jit(solution)/shard_map/ppermute | solution.py:516
  45.9 1.8 %collective-permute-done.10.refs_3_ = f32[2,32,192]{2,1,0:T(8,128)S(1)} collective-permute-done((f32[2,32,192]{2,1,0:T(8,128)S(1)}, f32[2,32,192]{2,1,0:T(8,128)S(1)}, u32[]{:S(2)}, u32[]{:S(2)}) %collective-permute-start.10) | collective-permute-done | bytes 49184 | tf_op jit(solution)/shard_map/ppermute | solution.py:516
  47.7 0.4 collective-permute-done.8.refs_1_
  48.1 1.3 %collective-permute-done.9.refs_2_ = f32[2,32,192]{2,1,0:T(8,128)S(1)} collective-permute-done((f32[2,32,192]{2,1,0:T(8,128)S(1)}, f32[2,32,192]{2,1,0:T(8,128)S(1)}, u32[]{:S(2)}, u32[]{:S(2)}) %collective-permute-start.9) | collective-permute-done | bytes 49184 | tf_op jit(solution)/shard_map/ppermute | solution.py:516
  49.4 0.8 %place.1 = f32[2,32,4,192]{3,2,1,0:T(4,128)} custom-call(f32[2,32,192]{2,1,0:T(8,128)S(1)} %get-tuple-element.37.refs_0_, f32[2,32,192]{2,1,0:T(8,128)S(1)} %collective-permute-done.8.refs_1_, f32[2,32,192]{2,1,0:T(8,128)S(1)} %collective-permute-done.9.refs_2_, f32[2,32,192]{2,1,0:T(8,128)S(1)} %collective-permute-done.10.refs_3_), custom_call_target="tpu_custom_call" | custom-call | tf_op jit(solution)/shard_map/place/pallas_call | solution.py:535
Async XLA Ops:
  0.0 4.4 %copy-start = (bf16[2,32,24,576]{3,2,1,0:T(8,128)(2,1)S(1)}, bf16[2,32,24,576]{3,2,1,0:T(8,128)(2,1)}, u32[]{:S(2)}) copy-start(bf16[2,32,24,576]{3,2,1,0:T(8,128)(2,1)} %refs_2_.3) | copy-start | bytes 5308420
  0.0 4.4 %copy-start.1 = (s32[32,24,576]{2,1,0:T(8,128)S(1)}, s32[32,24,576]{2,1,0:T(8,128)}, u32[]{:S(2)}) copy-start(s32[32,24,576]{2,1,0:T(8,128)} %refs_5_.3) | copy-start | bytes 5308420
  2.4 11.0 %copy-start.2 = (bf16[3,2,32,384]{3,2,1,0:T(8,128)(2,1)S(1)}, bf16[3,2,32,384]{3,2,1,0:T(8,128)(2,1)}, u32[]{:S(2)}) copy-start(bf16[3,2,32,384]{3,2,1,0:T(8,128)(2,1)} %get-tuple-element.23) | copy-start | bytes 442372
  2.4 6.8 %collective-permute-start.4 = (bf16[3,2,32,384]{3,2,1,0:T(8,128)(2,1)}, bf16[3,2,32,384]{3,2,1,0:T(8,128)(2,1)S(1)}, u32[]{:S(2)}, u32[]{:S(2)}) collective-permute-start(bf16[3,2,32,384]{3,2,1,0:T(8,128)(2,1)} %get-tuple-element.28), channel_id=1, source_target_pairs={{0,1},{1,2},{2,3},{3,4},{4,5},{5,6},{6,7},{8,9},{9,10},{10,11},{11... | collective-permute-start | bytes 442376 | tf_op jit(solution)/shard_map/ppermute | solution.py:565
  9.8 15.0 %collective-permute-start.5 = (bf16[19,2,32,128]{3,2,1,0:T(8,128)(2,1)S(1)}, bf16[19,2,32,128]{3,2,1,0:T(8,128)(2,1)S(1)}, u32[]{:S(2)}, u32[]{:S(2)}) collective-permute-start(bf16[19,2,32,128]{3,2,1,0:T(8,128)(2,1)S(1)} %get-tuple-element.34), channel_id=1, source_target_pairs={{0,8},{8,0},{16,24},{24,16},{1,9},{9,1},{17,25},{25,17},{2,10},{10... | collective-permute-start | bytes 933896 | tf_op jit(solution)/shard_map/ppermute | solution.py:516
  11.4 14.3 %collective-permute-start.6 = (bf16[19,2,32,128]{3,2,1,0:T(8,128)(2,1)S(1)}, bf16[19,2,32,128]{3,2,1,0:T(8,128)(2,1)S(1)}, u32[]{:S(2)}, u32[]{:S(2)}) collective-permute-start(bf16[19,2,32,128]{3,2,1,0:T(8,128)(2,1)S(1)} %get-tuple-element.35), channel_id=1, source_target_pairs={{0,16},{8,24},{16,0},{24,8},{1,17},{9,25},{17,1},{25,9},{2,18},{10... | collective-permute-start | bytes 933896 | tf_op jit(solution)/shard_map/ppermute | solution.py:516
  12.9 14.8 %collective-permute-start.7 = (bf16[19,2,32,128]{3,2,1,0:T(8,128)(2,1)S(1)}, bf16[19,2,32,128]{3,2,1,0:T(8,128)(2,1)S(1)}, u32[]{:S(2)}, u32[]{:S(2)}) collective-permute-start(bf16[19,2,32,128]{3,2,1,0:T(8,128)(2,1)S(1)} %get-tuple-element.36), channel_id=1, source_target_pairs={{0,24},{8,16},{16,8},{24,0},{1,25},{9,17},{17,9},{25,1},{2,26},{10... | collective-permute-start | bytes 933896 | tf_op jit(solution)/shard_map/ppermute | solution.py:516
  13.4 6.5 %collective-permute-start = (bf16[3,2,32,384]{3,2,1,0:T(8,128)(2,1)S(1)}, bf16[3,2,32,384]{3,2,1,0:T(8,128)(2,1)S(1)}, u32[]{:S(2)}, u32[]{:S(2)}) collective-permute-start(bf16[3,2,32,384]{3,2,1,0:T(8,128)(2,1)S(1)} %copy-done.2), channel_id=1, source_target_pairs={{0,1},{1,2},{2,3},{3,4},{4,5},{5,6},{6,7},{8,9},{9,10},{10,11},{11... | collective-permute-start | bytes 442376 | tf_op jit(solution)/shard_map/ppermute | solution.py:565
  21.7 14.0 %collective-permute-start.1 = (bf16[13,2,32,128]{3,2,1,0:T(8,128)(2,1)S(1)}, bf16[13,2,32,128]{3,2,1,0:T(8,128)(2,1)S(1)}, u32[]{:S(2)}, u32[]{:S(2)}) collective-permute-start(bf16[13,2,32,128]{3,2,1,0:T(8,128)(2,1)S(1)} %get-tuple-element.25), channel_id=1, source_target_pairs={{0,8},{8,0},{16,24},{24,16},{1,9},{9,1},{17,25},{25,17},{2,10},{10... | collective-permute-start | bytes 638984 | tf_op jit(solution)/shard_map/ppermute | solution.py:516
  23.3 12.5 %collective-permute-start.2 = (bf16[13,2,32,128]{3,2,1,0:T(8,128)(2,1)S(1)}, bf16[13,2,32,128]{3,2,1,0:T(8,128)(2,1)S(1)}, u32[]{:S(2)}, u32[]{:S(2)}) collective-permute-start(bf16[13,2,32,128]{3,2,1,0:T(8,128)(2,1)S(1)} %get-tuple-element.26), channel_id=1, source_target_pairs={{0,16},{8,24},{16,0},{24,8},{1,17},{9,25},{17,1},{25,9},{2,18},{10... | collective-permute-start | bytes 638984 | tf_op jit(solution)/shard_map/ppermute | solution.py:516
  24.8 10.9 %collective-permute-start.3 = (bf16[13,2,32,128]{3,2,1,0:T(8,128)(2,1)S(1)}, bf16[13,2,32,128]{3,2,1,0:T(8,128)(2,1)S(1)}, u32[]{:S(2)}, u32[]{:S(2)}) collective-permute-start(bf16[13,2,32,128]{3,2,1,0:T(8,128)(2,1)S(1)} %get-tuple-element.27), channel_id=1, source_target_pairs={{0,24},{8,16},{16,8},{24,0},{1,25},{9,17},{17,9},{25,1},{2,26},{10... | collective-permute-start | bytes 638984 | tf_op jit(solution)/shard_map/ppermute | solution.py:516
  42.3 5.3 %collective-permute-start.10 = (f32[2,32,192]{2,1,0:T(8,128)S(1)}, f32[2,32,192]{2,1,0:T(8,128)S(1)}, u32[]{:S(2)}, u32[]{:S(2)}) collective-permute-start(f32[2,32,192]{2,1,0:T(8,128)S(1)} %get-tuple-element.40), channel_id=1, source_target_pairs={{0,24},{8,16},{16,8},{24,0},{1,25},{9,17},{17,9},{25,1},{2,26},{10... | collective-permute-start | bytes 147464 | tf_op jit(solution)/shard_map/ppermute | solution.py:516
  43.8 4.3 %collective-permute-start.8 = (f32[2,32,192]{2,1,0:T(8,128)S(1)}, f32[2,32,192]{2,1,0:T(8,128)S(1)}, u32[]{:S(2)}, u32[]{:S(2)}) collective-permute-start(f32[2,32,192]{2,1,0:T(8,128)S(1)} %get-tuple-element.38), channel_id=1, source_target_pairs={{0,8},{8,0},{16,24},{24,16},{1,9},{9,1},{17,25},{25,17},{2,10},{10... | collective-permute-start | bytes 147464 | tf_op jit(solution)/shard_map/ppermute | solution.py:516
  45.1 4.3 %collective-permute-start.9 = (f32[2,32,192]{2,1,0:T(8,128)S(1)}, f32[2,32,192]{2,1,0:T(8,128)S(1)}, u32[]{:S(2)}, u32[]{:S(2)}) collective-permute-start(f32[2,32,192]{2,1,0:T(8,128)S(1)} %get-tuple-element.39), channel_id=1, source_target_pairs={{0,16},{8,24},{16,0},{24,8},{1,17},{9,25},{17,1},{25,9},{2,18},{10... | collective-permute-start | bytes 147464 | tf_op jit(solution)/shard_map/ppermute | solution.py:516

commit v5 on v4

--- a/solution.py
+++ b/solution.py
@@ -131,14 +131,9 @@
     return total
 
 
-def pack_kernel(ends, first_block, blocks, col_groups, segments, with_halo, *refs):
+def pack_kernel(ends, first_block, blocks, col_groups, segments, *refs):
     acq_refs, refs = refs[:blocks], refs[blocks:]
     valid_refs, refs = refs[:blocks], refs[blocks:]
-    if with_halo:
-        halo_ref, refs = refs[0], refs[1:]
-        refs, (halo, sem) = refs[:-2], refs[-2:]
-        fetch = pltpu.make_async_copy(halo_ref, halo, sem)
-        fetch.start()
     outs, (planes, shifted) = refs[:-2], refs[-2:]
     parts, dates, cols, _ = acq_refs[0].shape
     stride = planes.shape[2] // dates
@@ -166,18 +161,10 @@
 
     lax.fori_loop(0, blocks, one_block, 0)
 
-    def keep_edge(block, j, part, plane):
-        shifted[0, block, j, part] = plane
-
-    if with_halo:
-        fetch.wait()
-        edge_planes(halo, keep_edge)
-    else:
-        zero = jnp.zeros((dates, LANES), jnp.bfloat16)
-        for block in range(blocks):
-            for j in range(LEFT):
-                for part in range(parts):
-                    keep_edge(block, j, part, zero)
+    zero = jnp.zeros((parts, dates, LANES), jnp.bfloat16)
+    for block in range(blocks):
+        for j in range(LEFT):
+            shifted[0, block, j] = zero
     masks = {}
     chunks = len(ends) - 1
     empty = jnp.zeros((parts * dates // 16, 16, LANES), jnp.bfloat16)
@@ -212,7 +199,7 @@
     return range(low * TILE_ROWS // LANES, -(-high * TILE_ROWS // LANES))
 
 
-def pack(acquisitions, valid_dates, halo, peers, ends, col_groups, segments):
+def pack(acquisitions, valid_dates, peers, ends, col_groups, segments):
     parts, dates, cols, rows = acquisitions.shape
     span = blocks_of(ends[0], ends[-1], rows, segments)
     first, blocks = span[0], len(span)
@@ -234,14 +221,8 @@
         pltpu.VMEM((parts, blocks, dates * (cols + 1), LANES), jnp.float32),
         pltpu.VMEM((col_groups, blocks, BOX_COLS, parts, dates, LANES), jnp.bfloat16),
     ]
-    if halo is not None:
-        operands.append(halo)
-        specs.append(pl.BlockSpec(memory_space=pl.ANY))
-        scratch += [pltpu.VMEM(halo.shape, halo.dtype), pltpu.SemaphoreType.DMA]
     outs = pl.pallas_call(
-        functools.partial(
-            pack_kernel, ends, first, blocks, col_groups, segments, halo is not None
-        ),
+        functools.partial(pack_kernel, ends, first, blocks, col_groups, segments),
         grid=(1,),
         out_shape=shapes * peers,
         in_specs=specs,
@@ -256,7 +237,7 @@
     return [list(outs[chunk::chunks]) for chunk in range(chunks)]
 
 
-def patch_kernel(tiles, col_groups, segments, *refs):
+def patch_kernel(low, high, first_block, col_groups, segments, *refs):
     halo_ref, refs = refs[0], refs[1:]
     peers = (len(refs) - 4) // 2
     outs, (halo, planes, held, sems) = refs[peers:-4], refs[-4:]
@@ -270,7 +251,7 @@
         planes[block, j, part] = plane
 
     def piece(block, j):
-        return planes[block, j]
+        return planes[block - first_block, j]
 
     for offset, out in enumerate(outs):
         target = me ^ offset
@@ -285,12 +266,12 @@
             read.wait()
             masks = {}
             if segments == 1:
-                for tile in range(tiles):
-                    total = held[tile].reshape(shape)
+                for tile in range(low, high):
+                    total = held[tile - low].reshape(shape)
                     total = compose(total, tile, range(LEFT), piece, masks)
-                    held[tile] = total.reshape(held.shape[1:])
+                    held[tile - low] = total.reshape(held.shape[1:])
             else:
-                segment = target // col_groups
+                tiles, segment = high, target // col_groups
 
                 def one_tile(index, carry):
                     tile, last = segment * tiles + index - 1, segments * tiles - 1
@@ -305,12 +286,12 @@
             write.wait()
 
 
-def patch(blocks, halo, tiles, col_groups, segments):
+def patch(blocks, halo, low, high, first_block, col_groups, segments):
     peers = len(blocks)
     _, parts, dates, _ = blocks[0].shape
     anywhere = pl.BlockSpec(memory_space=pl.ANY)
     return pl.pallas_call(
-        functools.partial(patch_kernel, tiles, col_groups, segments),
+        functools.partial(patch_kernel, low, high, first_block, col_groups, segments),
         out_shape=[jax.ShapeDtypeStruct(block.shape, block.dtype) for block in blocks],
         in_specs=[anywhere] * (1 + peers),
         out_specs=[anywhere] * peers,
@@ -357,7 +338,21 @@
     return a.reshape(real.shape[1:]), b.reshape(real.shape[1:]), both
 
 
+def stack_parts(real, imag):
+    row = lax.broadcasted_iota(jnp.int32, real.shape, 0)
+    both = jnp.where((row & 1) == 1, imag, real)
+    return jnp.where((row & 2) == 2, -both, both)
+
+
+def column_sums(matrix):
+    total = jnp.sum(matrix.astype(jnp.float32).reshape(-1, 8, matrix.shape[1]), axis=0)
+    for distance in (4, 2, 1):
+        total = total + pltpu.roll(total, distance, 0)
+    return total
+
+
 def coherence_pair(a, b, both, diagonal, held, place):
+    matrices, begun = held
     count = a.shape[0]
     left = jnp.concatenate(
         [jnp.concatenate([a, b], axis=1), jnp.concatenate([b, -a], axis=1)], axis=0
@@ -372,29 +367,30 @@
         factor = lax.rsqrt(energy + POWER_EPS)
         down = jnp.sum(jnp.where(diagonal, factor, 0.0), axis=1, keepdims=True)
         weights = down * (factor * (1 / NBOX))
-        held[place + index, :count] = (real * weights).astype(jnp.bfloat16)
-        held[place + index, count:] = (imag * weights).astype(jnp.bfloat16)
+        real, imag = (real * weights).astype(jnp.bfloat16), (imag * weights).astype(jnp.bfloat16)
+        matrices[place + index, :count] = real
+        matrices[place + index, count:] = imag
+        begun[place + index] = stack_parts(column_sums(real), -column_sums(imag))
 
 
 def iterate(held, pixels, dates):
-    row = lax.broadcasted_iota(jnp.int32, (8, dates), 0)
-    odd = (row & 1) == 1
-    sign = jnp.where((row & 2) == 2, -1.0, 1.0)
-    start = jnp.concatenate([jnp.where(odd, 0.0, sign), jnp.where(odd, -sign, 0.0)], axis=1)
-    vectors = [start.astype(jnp.bfloat16)] * pixels
+    matrices, begun = held
+    products = [begun[place] for place in range(pixels)]
     for sweep in range(ITERS):
+        if sweep:
+            products = [
+                jnp.dot(vectors[place], matrices[place], preferred_element_type=jnp.float32)
+                for place in range(pixels)
+            ]
         scaled = []
-        for place in range(pixels):
-            product = jnp.dot(vectors[place], held[place], preferred_element_type=jnp.float32)
+        for product in products:
             square = product * product
             square = square + pltpu.roll(square, 1, 0)
             total = jnp.sum(square, axis=1, keepdims=True) * (1 / dates) + POWER_EPS
             scaled.append(product * lax.rsqrt(total))
-        if sweep + 1 < ITERS:
-            vectors = [
-                jnp.concatenate([v, pltpu.roll(v, 7, 0)], axis=1).astype(jnp.bfloat16)
-                for v in scaled
-            ]
+        vectors = [
+            jnp.concatenate([v, pltpu.roll(v, 7, 0)], axis=1).astype(jnp.bfloat16) for v in scaled
+        ]
     return scaled
 
 
@@ -406,7 +402,7 @@
     sources, refs = refs[:peers], refs[peers:]
     before, refs = refs[: peers * carried], refs[peers * carried :]
     done, refs = refs[:earlier], refs[earlier:]
-    outs, (real, imag, held, linked, sems) = refs[:-5], refs[-5:]
+    outs, (real, imag, *held, linked, sems) = refs[:-8], refs[-8:]
     sent, _, dates, _ = sources[0].shape
     all_dates = peers * dates
     base = 0 if padded else 2 if carried else 1
@@ -437,7 +433,7 @@
         jnp.int32, (all_dates, all_dates), 0
     ) == lax.broadcasted_iota(jnp.int32, (all_dates, all_dates), 1)
 
-    def step(index, carry):
+    def gram(index, held):
         rows_of = {}
 
         def rows_at(k):
@@ -454,12 +450,28 @@
             at = index * (batch // SLOTS) + k
             a, b, both = window_pair(real, imag, at, e, rows_at(k)[0], rows_at(k + 1)[1])
             coherence_pair(a, b, both, diagonal, held, place)
+
+    def power(index, held):
         for place, tile in enumerate(iterate(held, batch, all_dates)):
             for part in range(2):
                 linked[part, pl.ds(index * batch + place, 1)] = tile[part : part + 1]
+
+    batches = pixels // batch
+    slots = held[:2], held[2:]
+    gram(0, slots[0])
+
+    def step(index, carry):
+        gram(2 * index + 1, slots[1])
+        power(2 * index, slots[0])
+        gram(2 * index + 2, slots[0])
+        power(2 * index + 1, slots[1])
         return carry
 
-    lax.fori_loop(0, pixels // batch, step, 0)
+    lax.fori_loop(0, (batches - 1) // 2, step, 0)
+    if batches % 2 == 0:
+        gram(batches - 1, slots[1])
+        power(batches - 2, slots[0])
+    power(batches - 1, slots[(batches - 1) % 2])
     for part in range(2):
         vectors = linked[part]
         if not last:
@@ -498,11 +510,15 @@
         scratch_shapes=[
             pltpu.VMEM((kept, all_dates, LANES), jnp.bfloat16),
             pltpu.VMEM((kept, all_dates, LANES), jnp.bfloat16),
-            pltpu.VMEM((batch_of(pixels), 2 * all_dates, all_dates), jnp.bfloat16),
+            *[
+                pltpu.VMEM((batch_of(pixels), 2 * all_dates, all_dates), jnp.bfloat16),
+                pltpu.VMEM((batch_of(pixels), 8, all_dates), jnp.float32),
+            ]
+            * 2,
             pltpu.VMEM((2, pixels, all_dates), jnp.float32),
             pltpu.SemaphoreType.DMA((4 * peers,)),
         ],
-        compiler_params=pltpu.CompilerParams(vmem_limit_bytes=20 << 20),
+        compiler_params=pltpu.CompilerParams(vmem_limit_bytes=(17 << 20) + kept * (128 << 10)),
         cost_estimate=pl.CostEstimate(
             flops=pixels * 30 * 10**6, bytes_accessed=10**6, transcendentals=0
         ),
@@ -565,10 +581,10 @@
         lax.ppermute(edges, "space", [(i, i + 1) for i in range(strips - 1)])
         for edges in edge(acquisitions, valid_dates, ranges)
     ]
-    (blocks,) = pack(acquisitions, valid_dates, None, peers, [0, first], out_cols, segments)
-    outgoing = [patch(blocks, halos[0], first, out_cols, segments)]
-    if rest:
-        outgoing += pack(acquisitions, valid_dates, halos[1], peers, ends, out_cols, segments)
+    outgoing = []
+    for low, high, span, halo in zip([0] + ends, ends, ranges, halos):
+        (blocks,) = pack(acquisitions, valid_dates, peers, [low, high], out_cols, segments)
+        outgoing.append(patch(blocks, halo, low, high, span[0], out_cols, segments))
     incoming = [swap(blocks, "date") for blocks in outgoing]
     done, start = [], 0
     for index, blocks in enumerate(incoming):

time: 50.4 us -> 50 us (level)
    ppermute x2, waiting for transfers between devices: 7.21 us -> 5.75 us  [on_device(): lax.ppermute(edges, 'space', [(i, i + 1) for i in range(strips - 1)])]
    ppermute x9, waiting for transfers between devices: 5.89 us -> 7.31 us  [swap(): lax.ppermute(blocks[m], axis, [(i, i ^ m) for i in range(count)])]
    pallas_call x1 -> x2, Pallas kernels: 0.61 us -> 1.75 us  [patch(): pl.pallas_call(functools.partial(patch_kernel, low, high, first_block, co...]
    pallas_call x2, Pallas kernels: 14.6 us -> 13.6 us  [link(): pl.pallas_call(kernel, grid=(1,), out_shape=outs, in_specs=specs, out_spe...]
  transfers between devices with their start and end apart: 11 -> 11, of which waited for: 7 -> 8; matrix products, arithmetic and copies ran while one was open for 0% -> 0% of each run, Pallas kernels for 23% -> 24%
where the time goes in v5:
time: 50 us; the launch traced here: 49.8 us
  Pallas kernels  22.1 us (44%)
  starting transfers between devices  14.6 us (29%)
  waiting for transfers between devices  13.1 us (26%)
    pallas_call x2, Pallas kernels, link(): pl.pallas_call(kernel, grid=(1,), out_shape=outs, in_specs=specs, out_spe...  13.6 us
    ppermute x9, starting transfers between devices, swap(): lax.ppermute(blocks[m], axis, [(i, i ^ m) for i in range(count)])  10.7 us
    ppermute x9, waiting for transfers between devices, swap(): lax.ppermute(blocks[m], axis, [(i, i ^ m) for i in range(count)])  7.31 us
    ppermute x2, waiting for transfers between devices, on_device(): lax.ppermute(edges, 'space', [(i, i + 1) for i in range(strips - 1)])  5.75 us
    ppermute x2, starting transfers between devices, on_device(): lax.ppermute(edges, 'space', [(i, i + 1) for i in range(strips - 1)])  3.95 us
    pallas_call x2, Pallas kernels, pack(): pl.pallas_call(functools.partial(pack_kernel, ends, first, blocks, col_gr...  3.49 us
    pallas_call x1, Pallas kernels, edge(): pl.pallas_call(functools.partial(edge_kernel, cols - LEFT - at * 16, rang...  2.36 us
    pallas_call x2, Pallas kernels, patch(): pl.pallas_call(functools.partial(patch_kernel, low, high, first_block, co...  1.75 us
  transfers between devices with their start and end apart: 11, of which 8 were waited for; matrix products, arithmetic and copies ran while one was open for 0% of the time, Pallas kernels for 24%

profile of v5, /device:TPU:16, one launch (start us, length us, event | category | flops | bytes accessed | tf_op | source)
XLA Modules:
  0.0 49.8 jit_solution(17209441632045725462)
XLA Ops:
  0.0 0.0 copy-start
  0.0 0.0 copy-start.1
  0.0 2.4 %edge.1 = (bf16[3,2,32,384]{3,2,1,0:T(8,128)(2,1)}, bf16[3,2,32,384]{3,2,1,0:T(8,128)(2,1)}) custom-call(bf16[2,32,24,576]{3,2,1,0:T(8,128)(2,1)} %refs_2_.3, s32[32,24,576]{2,1,0:T(8,128)} %refs_5_.3), custom_call_target="tpu_custom_call" | custom-call | tf_op jit(solution)/shard_map/edge/pallas_call | solution.py:77
  2.4 0.0 copy-start.2
  2.4 2.0 %collective-permute-start.4 = (bf16[3,2,32,384]{3,2,1,0:T(8,128)(2,1)}, bf16[3,2,32,384]{3,2,1,0:T(8,128)(2,1)S(1)}, u32[]{:S(2)}, u32[]{:S(2)}) collective-permute-start(bf16[3,2,32,384]{3,2,1,0:T(8,128)(2,1)} %get-tuple-element.36), channel_id=1, source_target_pairs={{0,1},{1,2},{2,3},{3,4},{4,5},{5,6},{6,7},{8,9},{9,10},{10,11},{11... | collective-permute-start | bytes 442376 | tf_op jit(solution)/shard_map/ppermute | solution.py:581
  4.4 0.0 copy-done
  4.4 0.0 copy-done.1
  4.4 1.9 %pack.3 = (bf16[19,2,32,128]{3,2,1,0:T(8,128)(2,1)S(1)}, bf16[19,2,32,128]{3,2,1,0:T(8,128)(2,1)S(1)}, bf16[19,2,32,128]{3,2,1,0:T(8,128)(2,1)S(1)}, bf16[19,2,32,128]{3,2,1,0:T(8,128)(2,1)S(1)}) custom-call(bf16[2,32,24,576]{3,2,1,0:T(8,128)(2,1)S(1)} %copy-done, bf16[2,32,24,576]{3,2,1,0:T(8,128)(2,1)S(1)} %copy-done, ...), custom_call_target="tpu_custom_call" | custom-call | flops 100000000 | bytes 9000000 | tf_op jit(solution)/shard_map/pack/pallas_call | solution.py:224
  6.3 2.9 %collective-permute-done.4.refs_0_ = bf16[3,2,32,384]{3,2,1,0:T(8,128)(2,1)S(1)} collective-permute-done((bf16[3,2,32,384]{3,2,1,0:T(8,128)(2,1)}, bf16[3,2,32,384]{3,2,1,0:T(8,128)(2,1)S(1)}, u32[]{:S(2)}, u32[]{:S(2)}) %collective-permute-start.4) | collective-permute-done | bytes 147488 | tf_op jit(solution)/shard_map/ppermute | solution.py:581
  9.2 0.6 %patch.3 = (bf16[19,2,32,128]{3,2,1,0:T(8,128)(2,1)S(1)}, bf16[19,2,32,128]{3,2,1,0:T(8,128)(2,1)S(1)}, bf16[19,2,32,128]{3,2,1,0:T(8,128)(2,1)S(1)}, bf16[19,2,32,128]{3,2,1,0:T(8,128)(2,1)S(1)}) custom-call(bf16[3,2,32,384]{3,2,1,0:T(8,128)(2,1)S(1)} %collective-permute-done.4.refs_0_, ...), custom_call_target="tpu_custom_call", output_to_operand_aliasing={{0}: (1, {}), {1}: (2, {}), {2}: (3, {}), {3}: (4, {})} | custom-call | tf_op jit(solution)/shard_map/patch/pallas_call | solution.py:293
  9.8 1.6 %collective-permute-start.5 = (bf16[19,2,32,128]{3,2,1,0:T(8,128)(2,1)S(1)}, bf16[19,2,32,128]{3,2,1,0:T(8,128)(2,1)S(1)}, u32[]{:S(2)}, u32[]{:S(2)}) collective-permute-start(bf16[19,2,32,128]{3,2,1,0:T(8,128)(2,1)S(1)} %get-tuple-element.42), channel_id=1, source_target_pairs={{0,8},{8,0},{16,24},{24,16},{1,9},{9,1},{17,25},{25,17},{2,10},{10... | collective-permute-start | bytes 933896 | tf_op jit(solution)/shard_map/ppermute | solution.py:532
  11.3 1.5 %collective-permute-start.6 = (bf16[19,2,32,128]{3,2,1,0:T(8,128)(2,1)S(1)}, bf16[19,2,32,128]{3,2,1,0:T(8,128)(2,1)S(1)}, u32[]{:S(2)}, u32[]{:S(2)}) collective-permute-start(bf16[19,2,32,128]{3,2,1,0:T(8,128)(2,1)S(1)} %get-tuple-element.43), channel_id=1, source_target_pairs={{0,16},{8,24},{16,0},{24,8},{1,17},{9,25},{17,1},{25,9},{2,18},{10... | collective-permute-start | bytes 933896 | tf_op jit(solution)/shard_map/ppermute | solution.py:532
  12.9 0.5 collective-permute-start.7
  13.3 0.0 copy-done.2
  13.3 1.9 %collective-permute-start = (bf16[3,2,32,384]{3,2,1,0:T(8,128)(2,1)S(1)}, bf16[3,2,32,384]{3,2,1,0:T(8,128)(2,1)S(1)}, u32[]{:S(2)}, u32[]{:S(2)}) collective-permute-start(bf16[3,2,32,384]{3,2,1,0:T(8,128)(2,1)S(1)} %copy-done.2), channel_id=1, source_target_pairs={{0,1},{1,2},{2,3},{3,4},{4,5},{5,6},{6,7},{8,9},{9,10},{10,11},{11... | collective-permute-start | bytes 442376 | tf_op jit(solution)/shard_map/ppermute | solution.py:581
  15.3 1.6 %pack.2 = (bf16[13,2,32,128]{3,2,1,0:T(8,128)(2,1)S(1)}, bf16[13,2,32,128]{3,2,1,0:T(8,128)(2,1)S(1)}, bf16[13,2,32,128]{3,2,1,0:T(8,128)(2,1)S(1)}, bf16[13,2,32,128]{3,2,1,0:T(8,128)(2,1)S(1)}) custom-call(bf16[2,32,24,576]{3,2,1,0:T(8,128)(2,1)S(1)} %copy-done, bf16[2,32,24,576]{3,2,1,0:T(8,128)(2,1)S(1)} %copy-done, ...), custom_call_target="tpu_custom_call" | custom-call | flops 100000000 | bytes 9000000 | tf_op jit(solution)/shard_map/pack/pallas_call | solution.py:224
  16.9 2.9 %collective-permute-done.refs_0_ = bf16[3,2,32,384]{3,2,1,0:T(8,128)(2,1)S(1)} collective-permute-done((bf16[3,2,32,384]{3,2,1,0:T(8,128)(2,1)S(1)}, bf16[3,2,32,384]{3,2,1,0:T(8,128)(2,1)S(1)}, u32[]{:S(2)}, u32[]{:S(2)}) %collective-permute-start) | collective-permute-done | bytes 147488 | tf_op jit(solution)/shard_map/ppermute | solution.py:581
  19.8 1.1 %patch.2 = (bf16[13,2,32,128]{3,2,1,0:T(8,128)(2,1)S(1)}, bf16[13,2,32,128]{3,2,1,0:T(8,128)(2,1)S(1)}, bf16[13,2,32,128]{3,2,1,0:T(8,128)(2,1)S(1)}, bf16[13,2,32,128]{3,2,1,0:T(8,128)(2,1)S(1)}) custom-call(bf16[3,2,32,384]{3,2,1,0:T(8,128)(2,1)S(1)} %collective-permute-done.refs_0_, ...), custom_call_target="tpu_custom_call", output_to_operand_aliasing={{0}: (1, {}), {1}: (2, {}), {2}: (3, {}), {3}: (4, {})} | custom-call | tf_op jit(solution)/shard_map/patch/pallas_call | solution.py:293
  20.9 1.6 %collective-permute-start.1 = (bf16[13,2,32,128]{3,2,1,0:T(8,128)(2,1)S(1)}, bf16[13,2,32,128]{3,2,1,0:T(8,128)(2,1)S(1)}, u32[]{:S(2)}, u32[]{:S(2)}) collective-permute-start(bf16[13,2,32,128]{3,2,1,0:T(8,128)(2,1)S(1)} %get-tuple-element.33), channel_id=1, source_target_pairs={{0,8},{8,0},{16,24},{24,16},{1,9},{9,1},{17,25},{25,17},{2,10},{10... | collective-permute-start | bytes 638984 | tf_op jit(solution)/shard_map/ppermute | solution.py:532
  22.5 1.5 %collective-permute-start.2 = (bf16[13,2,32,128]{3,2,1,0:T(8,128)(2,1)S(1)}, bf16[13,2,32,128]{3,2,1,0:T(8,128)(2,1)S(1)}, u32[]{:S(2)}, u32[]{:S(2)}) collective-permute-start(bf16[13,2,32,128]{3,2,1,0:T(8,128)(2,1)S(1)} %get-tuple-element.34), channel_id=1, source_target_pairs={{0,16},{8,24},{16,0},{24,8},{1,17},{9,25},{17,1},{25,9},{2,18},{10... | collective-permute-start | bytes 638984 | tf_op jit(solution)/shard_map/ppermute | solution.py:532
  24.0 0.0 collective-permute-done.5.refs_1_.refs_5_
  24.0 0.5 collective-permute-start.3
  24.5 1.5 %collective-permute-done.6.refs_2_.refs_6_ = bf16[19,2,32,128]{3,2,1,0:T(8,128)(2,1)S(1)} collective-permute-done((bf16[19,2,32,128]{3,2,1,0:T(8,128)(2,1)S(1)}, bf16[19,2,32,128]{3,2,1,0:T(8,128)(2,1)S(1)}, u32[]{:S(2)}, u32[]{:S(2)}) %collective-permute-start.6) | collective-permute-done | bytes 311328 | tf_op jit(solution)/shard_map/ppermute | solution.py:532
  26.0 1.8 %collective-permute-done.7.refs_3_.refs_7_ = bf16[19,2,32,128]{3,2,1,0:T(8,128)(2,1)S(1)} collective-permute-done((bf16[19,2,32,128]{3,2,1,0:T(8,128)(2,1)S(1)}, bf16[19,2,32,128]{3,2,1,0:T(8,128)(2,1)S(1)}, u32[]{:S(2)}, u32[]{:S(2)}) %collective-permute-start.7) | collective-permute-done | bytes 311328 | tf_op jit(solution)/shard_map/ppermute | solution.py:532
  27.8 7.4 %link.2.refs_8_ = f32[2,108,128]{2,1,0:T(8,128)S(1)} custom-call(bf16[19,2,32,128]{3,2,1,0:T(8,128)(2,1)S(1)} %get-tuple-element.41.refs_0_.refs_4_, bf16[19,2,32,128]{3,2,1,0:T(8,128)(2,1)S(1)} %collective-permute-done.5.refs_1_.refs_5_, bf16[19,2,32,128]{3,2,1,0:T(8,128)(2,1)S(1)} %collective-permute-done.6.refs_2_.refs_6_, ...), custom_call_target="tpu_custom_call" | custom-call | flops 3240000000 | bytes 1000000 | tf_op jit(solution)/shard_map/link/pallas_call | solution.py:504
  35.2 0.0 collective-permute-done.1.refs_1_
  35.2 0.2 collective-permute-done.2.refs_2_
  35.4 0.0 collective-permute-done.3.refs_3_
  35.5 6.3 %link.3 = (f32[2,32,192]{2,1,0:T(8,128)S(1)}, f32[2,32,192]{2,1,0:T(8,128)S(1)}, f32[2,32,192]{2,1,0:T(8,128)S(1)}, f32[2,32,192]{2,1,0:T(8,128)S(1)}) custom-call(bf16[13,2,32,128]{3,2,1,0:T(8,128)(2,1)S(1)} %get-tuple-element.32.refs_0_, bf16[13,2,32,128]{3,2,1,0:T(8,128)(2,1)S(1)} %collective-permute-done.1.refs_1_, ...), custom_call_target="tpu_custom_call" | custom-call | flops 2520000000 | bytes 1000000 | tf_op jit(solution)/shard_map/link/pallas_call | solution.py:504
  41.7 1.6 %collective-permute-start.10 = (f32[2,32,192]{2,1,0:T(8,128)S(1)}, f32[2,32,192]{2,1,0:T(8,128)S(1)}, u32[]{:S(2)}, u32[]{:S(2)}) collective-permute-start(f32[2,32,192]{2,1,0:T(8,128)S(1)} %get-tuple-element.48), channel_id=1, source_target_pairs={{0,24},{8,16},{16,8},{24,0},{1,25},{9,17},{17,9},{25,1},{2,26},{10... | collective-permute-start | bytes 147464 | tf_op jit(solution)/shard_map/ppermute | solution.py:532
  43.3 1.5 %collective-permute-start.8 = (f32[2,32,192]{2,1,0:T(8,128)S(1)}, f32[2,32,192]{2,1,0:T(8,128)S(1)}, u32[]{:S(2)}, u32[]{:S(2)}) collective-permute-start(f32[2,32,192]{2,1,0:T(8,128)S(1)} %get-tuple-element.46), channel_id=1, source_target_pairs={{0,8},{8,0},{16,24},{24,16},{1,9},{9,1},{17,25},{25,17},{2,10},{10... | collective-permute-start | bytes 147464 | tf_op jit(solution)/shard_map/ppermute | solution.py:532
  44.8 0.5 %collective-permute-start.9 = (f32[2,32,192]{2,1,0:T(8,128)S(1)}, f32[2,32,192]{2,1,0:T(8,128)S(1)}, u32[]{:S(2)}, u32[]{:S(2)}) collective-permute-start(f32[2,32,192]{2,1,0:T(8,128)S(1)} %get-tuple-element.47), channel_id=1, source_target_pairs={{0,16},{8,24},{16,0},{24,8},{1,17},{9,25},{17,1},{25,9},{2,18},{10... | collective-permute-start | bytes 147464 | tf_op jit(solution)/shard_map/ppermute | solution.py:532
  45.3 1.8 %collective-permute-done.10.refs_3_ = f32[2,32,192]{2,1,0:T(8,128)S(1)} collective-permute-done((f32[2,32,192]{2,1,0:T(8,128)S(1)}, f32[2,32,192]{2,1,0:T(8,128)S(1)}, u32[]{:S(2)}, u32[]{:S(2)}) %collective-permute-start.10) | collective-permute-done | bytes 49184 | tf_op jit(solution)/shard_map/ppermute | solution.py:532
  47.1 0.6 %collective-permute-done.8.refs_1_ = f32[2,32,192]{2,1,0:T(8,128)S(1)} collective-permute-done((f32[2,32,192]{2,1,0:T(8,128)S(1)}, f32[2,32,192]{2,1,0:T(8,128)S(1)}, u32[]{:S(2)}, u32[]{:S(2)}) %collective-permute-start.8) | collective-permute-done | bytes 49184 | tf_op jit(solution)/shard_map/ppermute | solution.py:532
  47.7 1.3 %collective-permute-done.9.refs_2_ = f32[2,32,192]{2,1,0:T(8,128)S(1)} collective-permute-done((f32[2,32,192]{2,1,0:T(8,128)S(1)}, f32[2,32,192]{2,1,0:T(8,128)S(1)}, u32[]{:S(2)}, u32[]{:S(2)}) %collective-permute-start.9) | collective-permute-done | bytes 49184 | tf_op jit(solution)/shard_map/ppermute | solution.py:532
  49.0 0.8 %place.1 = f32[2,32,4,192]{3,2,1,0:T(4,128)} custom-call(f32[2,32,192]{2,1,0:T(8,128)S(1)} %get-tuple-element.45.refs_0_, f32[2,32,192]{2,1,0:T(8,128)S(1)} %collective-permute-done.8.refs_1_, f32[2,32,192]{2,1,0:T(8,128)S(1)} %collective-permute-done.9.refs_2_, f32[2,32,192]{2,1,0:T(8,128)S(1)} %collective-permute-done.10.refs_3_), custom_call_target="tpu_custom_call" | custom-call | tf_op jit(solution)/shard_map/place/pallas_call | solution.py:551
Async XLA Ops:
  0.0 4.4 %copy-start = (bf16[2,32,24,576]{3,2,1,0:T(8,128)(2,1)S(1)}, bf16[2,32,24,576]{3,2,1,0:T(8,128)(2,1)}, u32[]{:S(2)}) copy-start(bf16[2,32,24,576]{3,2,1,0:T(8,128)(2,1)} %refs_2_.3) | copy-start | bytes 5308420
  0.0 4.4 %copy-start.1 = (s32[32,24,576]{2,1,0:T(8,128)S(1)}, s32[32,24,576]{2,1,0:T(8,128)}, u32[]{:S(2)}) copy-start(s32[32,24,576]{2,1,0:T(8,128)} %refs_5_.3) | copy-start | bytes 5308420
  2.4 11.0 %copy-start.2 = (bf16[3,2,32,384]{3,2,1,0:T(8,128)(2,1)S(1)}, bf16[3,2,32,384]{3,2,1,0:T(8,128)(2,1)}, u32[]{:S(2)}) copy-start(bf16[3,2,32,384]{3,2,1,0:T(8,128)(2,1)} %get-tuple-element.27) | copy-start | bytes 442372
  2.4 6.8 %collective-permute-start.4 = (bf16[3,2,32,384]{3,2,1,0:T(8,128)(2,1)}, bf16[3,2,32,384]{3,2,1,0:T(8,128)(2,1)S(1)}, u32[]{:S(2)}, u32[]{:S(2)}) collective-permute-start(bf16[3,2,32,384]{3,2,1,0:T(8,128)(2,1)} %get-tuple-element.36), channel_id=1, source_target_pairs={{0,1},{1,2},{2,3},{3,4},{4,5},{5,6},{6,7},{8,9},{9,10},{10,11},{11... | collective-permute-start | bytes 442376 | tf_op jit(solution)/shard_map/ppermute | solution.py:581
  9.8 14.2 %collective-permute-start.5 = (bf16[19,2,32,128]{3,2,1,0:T(8,128)(2,1)S(1)}, bf16[19,2,32,128]{3,2,1,0:T(8,128)(2,1)S(1)}, u32[]{:S(2)}, u32[]{:S(2)}) collective-permute-start(bf16[19,2,32,128]{3,2,1,0:T(8,128)(2,1)S(1)} %get-tuple-element.42), channel_id=1, source_target_pairs={{0,8},{8,0},{16,24},{24,16},{1,9},{9,1},{17,25},{25,17},{2,10},{10... | collective-permute-start | bytes 933896 | tf_op jit(solution)/shard_map/ppermute | solution.py:532
  11.3 14.7 %collective-permute-start.6 = (bf16[19,2,32,128]{3,2,1,0:T(8,128)(2,1)S(1)}, bf16[19,2,32,128]{3,2,1,0:T(8,128)(2,1)S(1)}, u32[]{:S(2)}, u32[]{:S(2)}) collective-permute-start(bf16[19,2,32,128]{3,2,1,0:T(8,128)(2,1)S(1)} %get-tuple-element.43), channel_id=1, source_target_pairs={{0,16},{8,24},{16,0},{24,8},{1,17},{9,25},{17,1},{25,9},{2,18},{10... | collective-permute-start | bytes 933896 | tf_op jit(solution)/shard_map/ppermute | solution.py:532
  12.9 15.0 %collective-permute-start.7 = (bf16[19,2,32,128]{3,2,1,0:T(8,128)(2,1)S(1)}, bf16[19,2,32,128]{3,2,1,0:T(8,128)(2,1)S(1)}, u32[]{:S(2)}, u32[]{:S(2)}) collective-permute-start(bf16[19,2,32,128]{3,2,1,0:T(8,128)(2,1)S(1)} %get-tuple-element.44), channel_id=1, source_target_pairs={{0,24},{8,16},{16,8},{24,0},{1,25},{9,17},{17,9},{25,1},{2,26},{10... | collective-permute-start | bytes 933896 | tf_op jit(solution)/shard_map/ppermute | solution.py:532
  13.3 6.5 %collective-permute-start = (bf16[3,2,32,384]{3,2,1,0:T(8,128)(2,1)S(1)}, bf16[3,2,32,384]{3,2,1,0:T(8,128)(2,1)S(1)}, u32[]{:S(2)}, u32[]{:S(2)}) collective-permute-start(bf16[3,2,32,384]{3,2,1,0:T(8,128)(2,1)S(1)} %copy-done.2), channel_id=1, source_target_pairs={{0,1},{1,2},{2,3},{3,4},{4,5},{5,6},{6,7},{8,9},{9,10},{10,11},{11... | collective-permute-start | bytes 442376 | tf_op jit(solution)/shard_map/ppermute | solution.py:581
  20.9 14.3 %collective-permute-start.1 = (bf16[13,2,32,128]{3,2,1,0:T(8,128)(2,1)S(1)}, bf16[13,2,32,128]{3,2,1,0:T(8,128)(2,1)S(1)}, u32[]{:S(2)}, u32[]{:S(2)}) collective-permute-start(bf16[13,2,32,128]{3,2,1,0:T(8,128)(2,1)S(1)} %get-tuple-element.33), channel_id=1, source_target_pairs={{0,8},{8,0},{16,24},{24,16},{1,9},{9,1},{17,25},{25,17},{2,10},{10... | collective-permute-start | bytes 638984 | tf_op jit(solution)/shard_map/ppermute | solution.py:532
  22.5 13.0 %collective-permute-start.2 = (bf16[13,2,32,128]{3,2,1,0:T(8,128)(2,1)S(1)}, bf16[13,2,32,128]{3,2,1,0:T(8,128)(2,1)S(1)}, u32[]{:S(2)}, u32[]{:S(2)}) collective-permute-start(bf16[13,2,32,128]{3,2,1,0:T(8,128)(2,1)S(1)} %get-tuple-element.34), channel_id=1, source_target_pairs={{0,16},{8,24},{16,0},{24,8},{1,17},{9,25},{17,1},{25,9},{2,18},{10... | collective-permute-start | bytes 638984 | tf_op jit(solution)/shard_map/ppermute | solution.py:532
  24.0 11.4 %collective-permute-start.3 = (bf16[13,2,32,128]{3,2,1,0:T(8,128)(2,1)S(1)}, bf16[13,2,32,128]{3,2,1,0:T(8,128)(2,1)S(1)}, u32[]{:S(2)}, u32[]{:S(2)}) collective-permute-start(bf16[13,2,32,128]{3,2,1,0:T(8,128)(2,1)S(1)} %get-tuple-element.35), channel_id=1, source_target_pairs={{0,24},{8,16},{16,8},{24,0},{1,25},{9,17},{17,9},{25,1},{2,26},{10... | collective-permute-start | bytes 638984 | tf_op jit(solution)/shard_map/ppermute | solution.py:532
  41.7 5.3 %collective-permute-start.10 = (f32[2,32,192]{2,1,0:T(8,128)S(1)}, f32[2,32,192]{2,1,0:T(8,128)S(1)}, u32[]{:S(2)}, u32[]{:S(2)}) collective-permute-start(f32[2,32,192]{2,1,0:T(8,128)S(1)} %get-tuple-element.48), channel_id=1, source_target_pairs={{0,24},{8,16},{16,8},{24,0},{1,25},{9,17},{17,9},{25,1},{2,26},{10... | collective-permute-start | bytes 147464 | tf_op jit(solution)/shard_map/ppermute | solution.py:532
  43.3 4.4 %collective-permute-start.8 = (f32[2,32,192]{2,1,0:T(8,128)S(1)}, f32[2,32,192]{2,1,0:T(8,128)S(1)}, u32[]{:S(2)}, u32[]{:S(2)}) collective-permute-start(f32[2,32,192]{2,1,0:T(8,128)S(1)} %get-tuple-element.46), channel_id=1, source_target_pairs={{0,8},{8,0},{16,24},{24,16},{1,9},{9,1},{17,25},{25,17},{2,10},{10... | collective-permute-start | bytes 147464 | tf_op jit(solution)/shard_map/ppermute | solution.py:532
  44.8 4.3 %collective-permute-start.9 = (f32[2,32,192]{2,1,0:T(8,128)S(1)}, f32[2,32,192]{2,1,0:T(8,128)S(1)}, u32[]{:S(2)}, u32[]{:S(2)}) collective-permute-start(f32[2,32,192]{2,1,0:T(8,128)S(1)} %get-tuple-element.47), channel_id=1, source_target_pairs={{0,16},{8,24},{16,0},{24,8},{1,17},{9,25},{17,1},{25,9},{2,18},{10... | collective-permute-start | bytes 147464 | tf_op jit(solution)/shard_map/ppermute | solution.py:532

commit v6 on v5

--- a/solution.py
+++ b/solution.py
@@ -480,7 +480,7 @@
         vectors = jnp.concatenate([ref[part] for ref in done] + [vectors], axis=0)
         flat = jnp.transpose(vectors)
         for peer, out in enumerate(outs):
-            out[part] = flat[peer * dates : (peer + 1) * dates]
+            out[part] = flat[peer * dates : (peer + 1) * dates].astype(out.dtype)
 
 
 def link(sources, before, done, start, pixels, padded, last):
@@ -494,7 +494,8 @@
     specs += [whole] * len(done)
     if last:
         rows = start + pixels
-        outs = [jax.ShapeDtypeStruct((parts, dates, rows), jnp.float32)] * peers
+        away = jax.ShapeDtypeStruct((parts, dates, rows), jnp.bfloat16)
+        outs = [jax.ShapeDtypeStruct((parts, dates, rows), jnp.float32)] + [away] * (peers - 1)
     else:
         outs = [jax.ShapeDtypeStruct((parts, pixels, all_dates), jnp.float32)]
     kept = sent + 3
@@ -538,9 +539,11 @@
     rows = blocks[0].shape[2]
     me = lax.axis_index("date")
     for target in range(peers):
-        value = blocks[target][...]
+        value = blocks[target][...].astype(jnp.float32)
         for other in range(1, peers):
-            value = jnp.where(me == other, blocks[target ^ other][...], value)
+            value = jnp.where(
+                me == other, blocks[target ^ other][...].astype(jnp.float32), value
+            )
         segment = target // out_cols * rows
         out[:, :, target % out_cols, segment : segment + rows] = value
 

time: 50 us -> 49.7 us (level)
  no operation moved by 1% of the time
where the time goes in v6:
time: 49.7 us; the launch traced here: 49.5 us
  Pallas kernels  22.1 us (44%)
  starting transfers between devices  14.6 us (29%)
  waiting for transfers between devices  12.7 us (26%)
    pallas_call x2, Pallas kernels, link(): pl.pallas_call(kernel, grid=(1,), out_shape=outs, in_specs=specs, out_spe...  13.6 us
    ppermute x9, starting transfers between devices, swap(): lax.ppermute(blocks[m], axis, [(i, i ^ m) for i in range(count)])  10.7 us
    ppermute x9, waiting for transfers between devices, swap(): lax.ppermute(blocks[m], axis, [(i, i ^ m) for i in range(count)])  6.96 us
    ppermute x2, waiting for transfers between devices, on_device(): lax.ppermute(edges, 'space', [(i, i + 1) for i in range(strips - 1)])  5.75 us
    ppermute x2, starting transfers between devices, on_device(): lax.ppermute(edges, 'space', [(i, i + 1) for i in range(strips - 1)])  3.95 us
    pallas_call x2, Pallas kernels, pack(): pl.pallas_call(functools.partial(pack_kernel, ends, first, blocks, col_gr...  3.49 us
    pallas_call x1, Pallas kernels, edge(): pl.pallas_call(functools.partial(edge_kernel, cols - LEFT - at * 16, rang...  2.36 us
    pallas_call x2, Pallas kernels, patch(): pl.pallas_call(functools.partial(patch_kernel, low, high, first_block, co...  1.75 us
  transfers between devices with their start and end apart: 11, of which 8 were waited for; matrix products, arithmetic and copies ran while one was open for 0% of the time, Pallas kernels for 24%

profile of v6, /device:TPU:16, one launch (start us, length us, event | category | flops | bytes accessed | tf_op | source)
XLA Modules:
  0.0 49.5 jit_solution(11524174587374665731)
XLA Ops:
  0.0 0.0 copy-start
  0.0 0.0 copy-start.1
  0.0 2.4 %edge.1 = (bf16[3,2,32,384]{3,2,1,0:T(8,128)(2,1)}, bf16[3,2,32,384]{3,2,1,0:T(8,128)(2,1)}) custom-call(bf16[2,32,24,576]{3,2,1,0:T(8,128)(2,1)} %refs_2_.3, s32[32,24,576]{2,1,0:T(8,128)} %refs_5_.3), custom_call_target="tpu_custom_call" | custom-call | tf_op jit(solution)/shard_map/edge/pallas_call | solution.py:77
  2.4 0.0 copy-start.2
  2.4 2.0 %collective-permute-start.4 = (bf16[3,2,32,384]{3,2,1,0:T(8,128)(2,1)}, bf16[3,2,32,384]{3,2,1,0:T(8,128)(2,1)S(1)}, u32[]{:S(2)}, u32[]{:S(2)}) collective-permute-start(bf16[3,2,32,384]{3,2,1,0:T(8,128)(2,1)} %get-tuple-element.36), channel_id=1, source_target_pairs={{0,1},{1,2},{2,3},{3,4},{4,5},{5,6},{6,7},{8,9},{9,10},{10,11},{11... | collective-permute-start | bytes 442376 | tf_op jit(solution)/shard_map/ppermute | solution.py:584
  4.4 0.0 copy-done
  4.4 0.0 copy-done.1
  4.4 1.9 %pack.3 = (bf16[19,2,32,128]{3,2,1,0:T(8,128)(2,1)S(1)}, bf16[19,2,32,128]{3,2,1,0:T(8,128)(2,1)S(1)}, bf16[19,2,32,128]{3,2,1,0:T(8,128)(2,1)S(1)}, bf16[19,2,32,128]{3,2,1,0:T(8,128)(2,1)S(1)}) custom-call(bf16[2,32,24,576]{3,2,1,0:T(8,128)(2,1)S(1)} %copy-done, bf16[2,32,24,576]{3,2,1,0:T(8,128)(2,1)S(1)} %copy-done, ...), custom_call_target="tpu_custom_call" | custom-call | flops 100000000 | bytes 9000000 | tf_op jit(solution)/shard_map/pack/pallas_call | solution.py:224
  6.3 2.9 %collective-permute-done.4.refs_0_ = bf16[3,2,32,384]{3,2,1,0:T(8,128)(2,1)S(1)} collective-permute-done((bf16[3,2,32,384]{3,2,1,0:T(8,128)(2,1)}, bf16[3,2,32,384]{3,2,1,0:T(8,128)(2,1)S(1)}, u32[]{:S(2)}, u32[]{:S(2)}) %collective-permute-start.4) | collective-permute-done | bytes 147488 | tf_op jit(solution)/shard_map/ppermute | solution.py:584
  9.2 0.6 %patch.3 = (bf16[19,2,32,128]{3,2,1,0:T(8,128)(2,1)S(1)}, bf16[19,2,32,128]{3,2,1,0:T(8,128)(2,1)S(1)}, bf16[19,2,32,128]{3,2,1,0:T(8,128)(2,1)S(1)}, bf16[19,2,32,128]{3,2,1,0:T(8,128)(2,1)S(1)}) custom-call(bf16[3,2,32,384]{3,2,1,0:T(8,128)(2,1)S(1)} %collective-permute-done.4.refs_0_, ...), custom_call_target="tpu_custom_call", output_to_operand_aliasing={{0}: (1, {}), {1}: (2, {}), {2}: (3, {}), {3}: (4, {})} | custom-call | tf_op jit(solution)/shard_map/patch/pallas_call | solution.py:293
  9.8 1.6 %collective-permute-start.5 = (bf16[19,2,32,128]{3,2,1,0:T(8,128)(2,1)S(1)}, bf16[19,2,32,128]{3,2,1,0:T(8,128)(2,1)S(1)}, u32[]{:S(2)}, u32[]{:S(2)}) collective-permute-start(bf16[19,2,32,128]{3,2,1,0:T(8,128)(2,1)S(1)} %get-tuple-element.42), channel_id=1, source_target_pairs={{0,8},{8,0},{16,24},{24,16},{1,9},{9,1},{17,25},{25,17},{2,10},{10... | collective-permute-start | bytes 933896 | tf_op jit(solution)/shard_map/ppermute | solution.py:533
  11.3 1.5 %collective-permute-start.6 = (bf16[19,2,32,128]{3,2,1,0:T(8,128)(2,1)S(1)}, bf16[19,2,32,128]{3,2,1,0:T(8,128)(2,1)S(1)}, u32[]{:S(2)}, u32[]{:S(2)}) collective-permute-start(bf16[19,2,32,128]{3,2,1,0:T(8,128)(2,1)S(1)} %get-tuple-element.43), channel_id=1, source_target_pairs={{0,16},{8,24},{16,0},{24,8},{1,17},{9,25},{17,1},{25,9},{2,18},{10... | collective-permute-start | bytes 933896 | tf_op jit(solution)/shard_map/ppermute | solution.py:533
  12.9 0.5 collective-permute-start.7
  13.3 0.0 copy-done.2
  13.3 1.9 %collective-permute-start = (bf16[3,2,32,384]{3,2,1,0:T(8,128)(2,1)S(1)}, bf16[3,2,32,384]{3,2,1,0:T(8,128)(2,1)S(1)}, u32[]{:S(2)}, u32[]{:S(2)}) collective-permute-start(bf16[3,2,32,384]{3,2,1,0:T(8,128)(2,1)S(1)} %copy-done.2), channel_id=1, source_target_pairs={{0,1},{1,2},{2,3},{3,4},{4,5},{5,6},{6,7},{8,9},{9,10},{10,11},{11... | collective-permute-start | bytes 442376 | tf_op jit(solution)/shard_map/ppermute | solution.py:584
  15.3 1.6 %pack.2 = (bf16[13,2,32,128]{3,2,1,0:T(8,128)(2,1)S(1)}, bf16[13,2,32,128]{3,2,1,0:T(8,128)(2,1)S(1)}, bf16[13,2,32,128]{3,2,1,0:T(8,128)(2,1)S(1)}, bf16[13,2,32,128]{3,2,1,0:T(8,128)(2,1)S(1)}) custom-call(bf16[2,32,24,576]{3,2,1,0:T(8,128)(2,1)S(1)} %copy-done, bf16[2,32,24,576]{3,2,1,0:T(8,128)(2,1)S(1)} %copy-done, ...), custom_call_target="tpu_custom_call" | custom-call | flops 100000000 | bytes 9000000 | tf_op jit(solution)/shard_map/pack/pallas_call | solution.py:224
  16.9 2.9 %collective-permute-done.refs_0_ = bf16[3,2,32,384]{3,2,1,0:T(8,128)(2,1)S(1)} collective-permute-done((bf16[3,2,32,384]{3,2,1,0:T(8,128)(2,1)S(1)}, bf16[3,2,32,384]{3,2,1,0:T(8,128)(2,1)S(1)}, u32[]{:S(2)}, u32[]{:S(2)}) %collective-permute-start) | collective-permute-done | bytes 147488 | tf_op jit(solution)/shard_map/ppermute | solution.py:584
  19.8 1.1 %patch.2 = (bf16[13,2,32,128]{3,2,1,0:T(8,128)(2,1)S(1)}, bf16[13,2,32,128]{3,2,1,0:T(8,128)(2,1)S(1)}, bf16[13,2,32,128]{3,2,1,0:T(8,128)(2,1)S(1)}, bf16[13,2,32,128]{3,2,1,0:T(8,128)(2,1)S(1)}) custom-call(bf16[3,2,32,384]{3,2,1,0:T(8,128)(2,1)S(1)} %collective-permute-done.refs_0_, ...), custom_call_target="tpu_custom_call", output_to_operand_aliasing={{0}: (1, {}), {1}: (2, {}), {2}: (3, {}), {3}: (4, {})} | custom-call | tf_op jit(solution)/shard_map/patch/pallas_call | solution.py:293
  20.9 1.6 %collective-permute-start.1 = (bf16[13,2,32,128]{3,2,1,0:T(8,128)(2,1)S(1)}, bf16[13,2,32,128]{3,2,1,0:T(8,128)(2,1)S(1)}, u32[]{:S(2)}, u32[]{:S(2)}) collective-permute-start(bf16[13,2,32,128]{3,2,1,0:T(8,128)(2,1)S(1)} %get-tuple-element.33), channel_id=1, source_target_pairs={{0,8},{8,0},{16,24},{24,16},{1,9},{9,1},{17,25},{25,17},{2,10},{10... | collective-permute-start | bytes 638984 | tf_op jit(solution)/shard_map/ppermute | solution.py:533
  22.5 1.5 %collective-permute-start.2 = (bf16[13,2,32,128]{3,2,1,0:T(8,128)(2,1)S(1)}, bf16[13,2,32,128]{3,2,1,0:T(8,128)(2,1)S(1)}, u32[]{:S(2)}, u32[]{:S(2)}) collective-permute-start(bf16[13,2,32,128]{3,2,1,0:T(8,128)(2,1)S(1)} %get-tuple-element.34), channel_id=1, source_target_pairs={{0,16},{8,24},{16,0},{24,8},{1,17},{9,25},{17,1},{25,9},{2,18},{10... | collective-permute-start | bytes 638984 | tf_op jit(solution)/shard_map/ppermute | solution.py:533
  24.0 0.0 collective-permute-done.5.refs_1_.refs_5_
  24.0 0.5 collective-permute-start.3
  24.5 1.5 %collective-permute-done.6.refs_2_.refs_6_ = bf16[19,2,32,128]{3,2,1,0:T(8,128)(2,1)S(1)} collective-permute-done((bf16[19,2,32,128]{3,2,1,0:T(8,128)(2,1)S(1)}, bf16[19,2,32,128]{3,2,1,0:T(8,128)(2,1)S(1)}, u32[]{:S(2)}, u32[]{:S(2)}) %collective-permute-start.6) | collective-permute-done | bytes 311328 | tf_op jit(solution)/shard_map/ppermute | solution.py:533
  26.0 1.8 %collective-permute-done.7.refs_3_.refs_7_ = bf16[19,2,32,128]{3,2,1,0:T(8,128)(2,1)S(1)} collective-permute-done((bf16[19,2,32,128]{3,2,1,0:T(8,128)(2,1)S(1)}, bf16[19,2,32,128]{3,2,1,0:T(8,128)(2,1)S(1)}, u32[]{:S(2)}, u32[]{:S(2)}) %collective-permute-start.7) | collective-permute-done | bytes 311328 | tf_op jit(solution)/shard_map/ppermute | solution.py:533
  27.8 7.4 %link.2.refs_8_ = f32[2,108,128]{2,1,0:T(8,128)S(1)} custom-call(bf16[19,2,32,128]{3,2,1,0:T(8,128)(2,1)S(1)} %get-tuple-element.41.refs_0_.refs_4_, bf16[19,2,32,128]{3,2,1,0:T(8,128)(2,1)S(1)} %collective-permute-done.5.refs_1_.refs_5_, bf16[19,2,32,128]{3,2,1,0:T(8,128)(2,1)S(1)} %collective-permute-done.6.refs_2_.refs_6_, ...), custom_call_target="tpu_custom_call" | custom-call | flops 3240000000 | bytes 1000000 | tf_op jit(solution)/shard_map/link/pallas_call | solution.py:505
  35.2 0.0 collective-permute-done.1.refs_1_
  35.2 0.2 collective-permute-done.2.refs_2_
  35.4 0.0 collective-permute-done.3.refs_3_
  35.5 6.3 %link.3 = (f32[2,32,192]{2,1,0:T(8,128)S(1)}, bf16[2,32,192]{2,1,0:T(8,128)(2,1)S(1)}, bf16[2,32,192]{2,1,0:T(8,128)(2,1)S(1)}, bf16[2,32,192]{2,1,0:T(8,128)(2,1)S(1)}) custom-call(bf16[13,2,32,128]{3,2,1,0:T(8,128)(2,1)S(1)} %get-tuple-element.32.refs_0_, bf16[13,2,32,128]{3,2,1,0:T(8,128)(2,1)S(1)} %collective-permute-done.1.refs_1_, ...), custom_call_target="tpu_custom_call" | custom-call | flops 2520000000 | bytes 1000000 | tf_op jit(solution)/shard_map/link/pallas_call | solution.py:505
  41.7 1.6 %collective-permute-start.10 = (bf16[2,32,192]{2,1,0:T(8,128)(2,1)S(1)}, bf16[2,32,192]{2,1,0:T(8,128)(2,1)S(1)}, u32[]{:S(2)}, u32[]{:S(2)}) collective-permute-start(bf16[2,32,192]{2,1,0:T(8,128)(2,1)S(1)} %get-tuple-element.48), channel_id=1, source_target_pairs={{0,24},{8,16},{16,8},{24,0},{1,25},{9,17},{17,9},{25,1},{2,26},{10... | collective-permute-start | bytes 73736 | tf_op jit(solution)/shard_map/ppermute | solution.py:533
  43.3 1.5 %collective-permute-start.8 = (bf16[2,32,192]{2,1,0:T(8,128)(2,1)S(1)}, bf16[2,32,192]{2,1,0:T(8,128)(2,1)S(1)}, u32[]{:S(2)}, u32[]{:S(2)}) collective-permute-start(bf16[2,32,192]{2,1,0:T(8,128)(2,1)S(1)} %get-tuple-element.46), channel_id=1, source_target_pairs={{0,8},{8,0},{16,24},{24,16},{1,9},{9,1},{17,25},{25,17},{2,10},{10... | collective-permute-start | bytes 73736 | tf_op jit(solution)/shard_map/ppermute | solution.py:533
  44.8 0.5 %collective-permute-start.9 = (bf16[2,32,192]{2,1,0:T(8,128)(2,1)S(1)}, bf16[2,32,192]{2,1,0:T(8,128)(2,1)S(1)}, u32[]{:S(2)}, u32[]{:S(2)}) collective-permute-start(bf16[2,32,192]{2,1,0:T(8,128)(2,1)S(1)} %get-tuple-element.47), channel_id=1, source_target_pairs={{0,16},{8,24},{16,0},{24,8},{1,17},{9,25},{17,1},{25,9},{2,18},{10... | collective-permute-start | bytes 73736 | tf_op jit(solution)/shard_map/ppermute | solution.py:533
  45.3 1.4 %collective-permute-done.10.refs_3_ = bf16[2,32,192]{2,1,0:T(8,128)(2,1)S(1)} collective-permute-done((bf16[2,32,192]{2,1,0:T(8,128)(2,1)S(1)}, bf16[2,32,192]{2,1,0:T(8,128)(2,1)S(1)}, u32[]{:S(2)}, u32[]{:S(2)}) %collective-permute-start.10) | collective-permute-done | bytes 24608 | tf_op jit(solution)/shard_map/ppermute | solution.py:533
  46.7 0.5 collective-permute-done.8.refs_1_
  47.2 1.5 %collective-permute-done.9.refs_2_ = bf16[2,32,192]{2,1,0:T(8,128)(2,1)S(1)} collective-permute-done((bf16[2,32,192]{2,1,0:T(8,128)(2,1)S(1)}, bf16[2,32,192]{2,1,0:T(8,128)(2,1)S(1)}, u32[]{:S(2)}, u32[]{:S(2)}) %collective-permute-start.9) | collective-permute-done | bytes 24608 | tf_op jit(solution)/shard_map/ppermute | solution.py:533
  48.7 0.8 %place.1 = f32[2,32,4,192]{3,2,1,0:T(4,128)} custom-call(f32[2,32,192]{2,1,0:T(8,128)S(1)} %get-tuple-element.45.refs_0_, bf16[2,32,192]{2,1,0:T(8,128)(2,1)S(1)} %collective-permute-done.8.refs_1_, bf16[2,32,192]{2,1,0:T(8,128)(2,1)S(1)} %collective-permute-done.9.refs_2_, bf16[2,32,192]{2,1,0:T(8,128)(2,1)S(1)} %collective-permute-done.10.refs_3_), custom_call_target="tpu_custom_call" | custom-call | tf_op jit(solution)/shard_map/place/pallas_call | solution.py:554
Async XLA Ops:
  0.0 4.4 %copy-start = (bf16[2,32,24,576]{3,2,1,0:T(8,128)(2,1)S(1)}, bf16[2,32,24,576]{3,2,1,0:T(8,128)(2,1)}, u32[]{:S(2)}) copy-start(bf16[2,32,24,576]{3,2,1,0:T(8,128)(2,1)} %refs_2_.3) | copy-start | bytes 5308420
  0.0 4.4 %copy-start.1 = (s32[32,24,576]{2,1,0:T(8,128)S(1)}, s32[32,24,576]{2,1,0:T(8,128)}, u32[]{:S(2)}) copy-start(s32[32,24,576]{2,1,0:T(8,128)} %refs_5_.3) | copy-start | bytes 5308420
  2.4 11.0 %copy-start.2 = (bf16[3,2,32,384]{3,2,1,0:T(8,128)(2,1)S(1)}, bf16[3,2,32,384]{3,2,1,0:T(8,128)(2,1)}, u32[]{:S(2)}) copy-start(bf16[3,2,32,384]{3,2,1,0:T(8,128)(2,1)} %get-tuple-element.27) | copy-start | bytes 442372
  2.4 6.8 %collective-permute-start.4 = (bf16[3,2,32,384]{3,2,1,0:T(8,128)(2,1)}, bf16[3,2,32,384]{3,2,1,0:T(8,128)(2,1)S(1)}, u32[]{:S(2)}, u32[]{:S(2)}) collective-permute-start(bf16[3,2,32,384]{3,2,1,0:T(8,128)(2,1)} %get-tuple-element.36), channel_id=1, source_target_pairs={{0,1},{1,2},{2,3},{3,4},{4,5},{5,6},{6,7},{8,9},{9,10},{10,11},{11... | collective-permute-start | bytes 442376 | tf_op jit(solution)/shard_map/ppermute | solution.py:584
  9.8 14.2 %collective-permute-start.5 = (bf16[19,2,32,128]{3,2,1,0:T(8,128)(2,1)S(1)}, bf16[19,2,32,128]{3,2,1,0:T(8,128)(2,1)S(1)}, u32[]{:S(2)}, u32[]{:S(2)}) collective-permute-start(bf16[19,2,32,128]{3,2,1,0:T(8,128)(2,1)S(1)} %get-tuple-element.42), channel_id=1, source_target_pairs={{0,8},{8,0},{16,24},{24,16},{1,9},{9,1},{17,25},{25,17},{2,10},{10... | collective-permute-start | bytes 933896 | tf_op jit(solution)/shard_map/ppermute | solution.py:533
  11.3 14.7 %collective-permute-start.6 = (bf16[19,2,32,128]{3,2,1,0:T(8,128)(2,1)S(1)}, bf16[19,2,32,128]{3,2,1,0:T(8,128)(2,1)S(1)}, u32[]{:S(2)}, u32[]{:S(2)}) collective-permute-start(bf16[19,2,32,128]{3,2,1,0:T(8,128)(2,1)S(1)} %get-tuple-element.43), channel_id=1, source_target_pairs={{0,16},{8,24},{16,0},{24,8},{1,17},{9,25},{17,1},{25,9},{2,18},{10... | collective-permute-start | bytes 933896 | tf_op jit(solution)/shard_map/ppermute | solution.py:533
  12.9 15.0 %collective-permute-start.7 = (bf16[19,2,32,128]{3,2,1,0:T(8,128)(2,1)S(1)}, bf16[19,2,32,128]{3,2,1,0:T(8,128)(2,1)S(1)}, u32[]{:S(2)}, u32[]{:S(2)}) collective-permute-start(bf16[19,2,32,128]{3,2,1,0:T(8,128)(2,1)S(1)} %get-tuple-element.44), channel_id=1, source_target_pairs={{0,24},{8,16},{16,8},{24,0},{1,25},{9,17},{17,9},{25,1},{2,26},{10... | collective-permute-start | bytes 933896 | tf_op jit(solution)/shard_map/ppermute | solution.py:533
  13.3 6.5 %collective-permute-start = (bf16[3,2,32,384]{3,2,1,0:T(8,128)(2,1)S(1)}, bf16[3,2,32,384]{3,2,1,0:T(8,128)(2,1)S(1)}, u32[]{:S(2)}, u32[]{:S(2)}) collective-permute-start(bf16[3,2,32,384]{3,2,1,0:T(8,128)(2,1)S(1)} %copy-done.2), channel_id=1, source_target_pairs={{0,1},{1,2},{2,3},{3,4},{4,5},{5,6},{6,7},{8,9},{9,10},{10,11},{11... | collective-permute-start | bytes 442376 | tf_op jit(solution)/shard_map/ppermute | solution.py:584
  20.9 14.3 %collective-permute-start.1 = (bf16[13,2,32,128]{3,2,1,0:T(8,128)(2,1)S(1)}, bf16[13,2,32,128]{3,2,1,0:T(8,128)(2,1)S(1)}, u32[]{:S(2)}, u32[]{:S(2)}) collective-permute-start(bf16[13,2,32,128]{3,2,1,0:T(8,128)(2,1)S(1)} %get-tuple-element.33), channel_id=1, source_target_pairs={{0,8},{8,0},{16,24},{24,16},{1,9},{9,1},{17,25},{25,17},{2,10},{10... | collective-permute-start | bytes 638984 | tf_op jit(solution)/shard_map/ppermute | solution.py:533
  22.5 13.0 %collective-permute-start.2 = (bf16[13,2,32,128]{3,2,1,0:T(8,128)(2,1)S(1)}, bf16[13,2,32,128]{3,2,1,0:T(8,128)(2,1)S(1)}, u32[]{:S(2)}, u32[]{:S(2)}) collective-permute-start(bf16[13,2,32,128]{3,2,1,0:T(8,128)(2,1)S(1)} %get-tuple-element.34), channel_id=1, source_target_pairs={{0,16},{8,24},{16,0},{24,8},{1,17},{9,25},{17,1},{25,9},{2,18},{10... | collective-permute-start | bytes 638984 | tf_op jit(solution)/shard_map/ppermute | solution.py:533
  24.0 11.4 %collective-permute-start.3 = (bf16[13,2,32,128]{3,2,1,0:T(8,128)(2,1)S(1)}, bf16[13,2,32,128]{3,2,1,0:T(8,128)(2,1)S(1)}, u32[]{:S(2)}, u32[]{:S(2)}) collective-permute-start(bf16[13,2,32,128]{3,2,1,0:T(8,128)(2,1)S(1)} %get-tuple-element.35), channel_id=1, source_target_pairs={{0,24},{8,16},{16,8},{24,0},{1,25},{9,17},{17,9},{25,1},{2,26},{10... | collective-permute-start | bytes 638984 | tf_op jit(solution)/shard_map/ppermute | solution.py:533
  41.7 5.0 %collective-permute-start.10 = (bf16[2,32,192]{2,1,0:T(8,128)(2,1)S(1)}, bf16[2,32,192]{2,1,0:T(8,128)(2,1)S(1)}, u32[]{:S(2)}, u32[]{:S(2)}) collective-permute-start(bf16[2,32,192]{2,1,0:T(8,128)(2,1)S(1)} %get-tuple-element.48), channel_id=1, source_target_pairs={{0,24},{8,16},{16,8},{24,0},{1,25},{9,17},{17,9},{25,1},{2,26},{10... | collective-permute-start | bytes 73736 | tf_op jit(solution)/shard_map/ppermute | solution.py:533
  43.3 3.9 %collective-permute-start.8 = (bf16[2,32,192]{2,1,0:T(8,128)(2,1)S(1)}, bf16[2,32,192]{2,1,0:T(8,128)(2,1)S(1)}, u32[]{:S(2)}, u32[]{:S(2)}) collective-permute-start(bf16[2,32,192]{2,1,0:T(8,128)(2,1)S(1)} %get-tuple-element.46), channel_id=1, source_target_pairs={{0,8},{8,0},{16,24},{24,16},{1,9},{9,1},{17,25},{25,17},{2,10},{10... | collective-permute-start | bytes 73736 | tf_op jit(solution)/shard_map/ppermute | solution.py:533
  44.8 3.9 %collective-permute-start.9 = (bf16[2,32,192]{2,1,0:T(8,128)(2,1)S(1)}, bf16[2,32,192]{2,1,0:T(8,128)(2,1)S(1)}, u32[]{:S(2)}, u32[]{:S(2)}) collective-permute-start(bf16[2,32,192]{2,1,0:T(8,128)(2,1)S(1)} %get-tuple-element.47), channel_id=1, source_target_pairs={{0,16},{8,24},{16,0},{24,8},{1,17},{9,25},{17,1},{25,9},{2,18},{10... | collective-permute-start | bytes 73736 | tf_op jit(solution)/shard_map/ppermute | solution.py:533
